TPU v7x, 32 devices: a whole 2x2x4 slice. The times are simulated.
32 devices in a mesh: dp: 2 (over x), expert: 4 (over z), tensor: 4 (over y, core).
Axes of the slice: x: 2, y: 2, z: 4, core: 2. Of those that a mesh axis runs over, the one named last changes fastest.
Arguments:
- tokens: bfloat16 [3840, 1536], P(('dp', 'expert')), may hold values from -6 to 6
- out_cotangent: bfloat16 [3840, 1536], P(('dp', 'expert')), may hold values from -6 to 6
- first_gain: bfloat16 [1536], replicated, may hold values from 0.5 to 1.5
- query_weight: bfloat16 [1536, 1536], P(None, 'tensor'), may hold values from -0.15625 to 0.15625
- key_value_matrix: bfloat16 [1536, 1024], P(None, 'tensor'), may hold values from -0.15625 to 0.15625
- output_weight: bfloat16 [1536, 1536], P('tensor'), may hold values from -1.25 to 1.25
- second_gain: bfloat16 [1536], replicated, may hold values from 0.5 to 1.5
- expert_gate_up: bfloat16 [40, 1536, 1024], P('expert', None, 'tensor'), may hold values from -0.15625 to 0.15625
- expert_down: bfloat16 [40, 512, 1536], P('expert', 'tensor'), may hold values from -1 to 1
- routes: int32 [3840, 8], P(('dp', 'expert')), may hold values from 0 to 39, all different within a row; in each aligned block of 480 rows (0 to 479, 480 to 959, ...) at most 192 rows name the same one
- route_gates: float32 [3840, 8], P(('dp', 'expert')), may hold values from 0 to 1, as said below
- expert_slot: int32 [40], replicated, may hold values from 0 to 39, each once
- parent_segments: int32 [2, 7], P('dp'), may hold values from 0 to 6, as said below
- token_segments: int32 [3840], P('dp'), may hold values from 0 to 6, as said below
Outputs:
- layer_output: bfloat16 [3840, 1536], P(('dp', 'expert'))
- input_gradient: bfloat16 [3840, 1536], P(('dp', 'expert'))
- first_gain_gradient: float32 [1536], replicated
- query_gradient: float32 [1536, 1536], P(None, 'tensor')
- key_value_gradient: float32 [1536, 1024], P(None, 'tensor')
- output_gradient: float32 [1536, 1536], P('tensor')
- second_gain_gradient: float32 [1536], replicated
- expert_gate_up_gradient: float32 [40, 1536, 1024], P('expert', None, 'tensor')
- expert_down_gradient: float32 [40, 512, 1536], P('expert', 'tensor')
Inputs may be any that keep to these rules, and one draw needn't show every extreme that they name: `routes`: each row names 8 different experts. Among the 480 rows of one device no expert is named more than 192 times, and in every draw some device names some expert exactly 192 times. `route_gates`: Positive; each row sums to 1. A permutation of the experts. Expert e's weights are entry expert_slot[e] of the expert arrays. `parent_segments`: each tree has 7 segments: one root, which is its own parent, with two children, each of which has two leaf children. `token_segments`: the root holds 640 tokens, its children 2 * 160 each, the leaves 160 each. A segment's tokens are contiguous and come after those of its parent.
All inputs are finite; a program needn't handle non-finite values.
Results may differ from a plain program's by a relative error of at most 0.025.
Values may be sent and summed in bfloat16 or wider, within the bound.
No kernel may reach another device: no remote copies, remote signals or barrier semaphores. Data moves between devices by JAX's collectives and lax.ppermute only.
A program may use at most 384 MiB of HBM per device.

v0:
```python
from functools import partial

import jax
import jax.numpy as jnp
from jax import lax
from jax.sharding import PartitionSpec as P

HEAD_SIZE = 64
PAIR = 64
CAP = 192


EPS = 1e-05


def normalize(values, gain_vector):
    inverse_rms = lax.rsqrt(jnp.mean(values * values, axis=-1, keepdims=True) + EPS)
    return values * inverse_rms * gain_vector


def rotate(values, position):
    half_width = values.shape[-1] // 2
    frequency = jnp.power(10000.0, -jnp.arange(half_width, dtype=jnp.float32) / half_width)
    angles = position.astype(jnp.float32)[:, None] * frequency[None, :]
    cosine = jnp.cos(angles)[:, None, :]
    sine_part = jnp.sin(angles)[:, None, :]
    first_half = values[..., :half_width]
    second_half = values[..., half_width:]
    return jnp.concatenate(
        [
            first_half * cosine - second_half * sine_part,
            second_half * cosine + first_half * sine_part,
        ],
        axis=-1,
    )


def swiglu(gate_part, up_part):
    return gate_part * jax.nn.sigmoid(gate_part) * up_part


def split_pairs(hidden, pair_width):
    leading = hidden.shape[:-1]
    width = hidden.shape[-1] // 2
    grouped = hidden.reshape(leading + (width // pair_width, 2, pair_width))
    return (
        grouped[..., 0, :].reshape(leading + (width,)),
        grouped[..., 1, :].reshape(leading + (width,)),
    )


def join_pairs(gate_part, up_part, pair_width):
    leading = gate_part.shape[:-1]
    width = gate_part.shape[-1]
    stacked = jnp.stack(
        [
            gate_part.reshape(leading + (width // pair_width, pair_width)),
            up_part.reshape(leading + (width // pair_width, pair_width)),
        ],
        axis=-2,
    )
    return stacked.reshape(leading + (2 * width,))


def tree_layout(parents, segments):
    labels = jnp.arange(parents.shape[0], dtype=jnp.int32)
    up_two = jnp.sum(
        (parents[:, None] == labels[None, :]).astype(jnp.int32) * parents[None, :],
        axis=1,
        dtype=jnp.int32,
    )
    itself = labels[None, :] == labels[:, None]
    ancestry = itself | (labels[None, :] == parents[:, None]) | (labels[None, :] == up_two[:, None])
    member = (segments[:, None] == labels[None, :]).astype(jnp.int32)
    tree_rows = segments.shape[0]
    lengths = jnp.sum(member, axis=0, dtype=jnp.int32)
    row_index = jnp.arange(tree_rows, dtype=jnp.int32)
    first_row = jnp.min(jnp.where(member > 0, row_index[:, None], tree_rows), axis=0)
    ancestor_rows = jnp.sum(
        jnp.where(ancestry & jnp.logical_not(itself), lengths[None, :], 0), axis=1, dtype=jnp.int32
    )
    position = row_index + jnp.sum(
        member * (ancestor_rows - first_row)[None, :], axis=1, dtype=jnp.int32
    )
    reachable = jnp.dot(member, ancestry.astype(jnp.int32))
    return (position, reachable, member)


def expert_forward(row_data, gate_up, down_part):
    hidden = jnp.einsum("slcd,ldf->slcf", row_data, gate_up, preferred_element_type=jnp.float32)
    gate_part, up_part = split_pairs(hidden, PAIR)
    activation = swiglu(gate_part, up_part).astype(jnp.bfloat16)
    expert_part = jnp.einsum(
        "slcf,lfd->slcd", activation, down_part, preferred_element_type=jnp.float32
    ).astype(jnp.bfloat16)
    return (hidden, activation, expert_part)


def expert_backward(row_data, hidden, activation, grad_data, gate_up, down_part):
    gate_part, up_part = split_pairs(hidden, PAIR)
    act_grad = jnp.einsum(
        "slcd,lfd->slcf", grad_data, down_part, preferred_element_type=jnp.float32
    )
    down_grad = jnp.einsum(
        "slcf,slcd->lfd", activation, grad_data, preferred_element_type=jnp.float32
    )
    _, glu_pull = jax.vjp(swiglu, gate_part, up_part)
    gate_grad, up_grad = glu_pull(act_grad)
    hidden_grad = join_pairs(gate_grad, up_grad, PAIR).astype(jnp.bfloat16)
    gate_up_grad = jnp.einsum(
        "slcd,slcf->ldf", row_data, hidden_grad, preferred_element_type=jnp.float32
    )
    row_grad = jnp.einsum(
        "slcf,ldf->slcd", hidden_grad, gate_up, preferred_element_type=jnp.float32
    ).astype(jnp.bfloat16)
    return (gate_up_grad, down_grad, row_grad)


def send_rows(buffer):
    return lax.all_to_all(buffer, "expert", split_axis=0, concat_axis=0, tiled=True)


def return_rows(buffer):
    return lax.all_to_all(buffer, "expert", split_axis=0, concat_axis=0, tiled=True)


def attention_probs(query_vectors, all_keys, allowed, score_scale):
    scores = (
        jnp.einsum("tgrh,kgh->tgrk", query_vectors, all_keys, preferred_element_type=jnp.float32)
        * score_scale
    )
    return jnp.where(allowed[:, None, None, :], scores, -1e30)


def shards(
    tokens,
    out_cotangent,
    first_gain,
    query_weight,
    key_value_matrix,
    output_weight,
    second_gain,
    expert_gate_up,
    expert_down,
    routes,
    route_gates,
    expert_slot,
    parent_segments,
    token_segments,
):
    row_count = tokens.shape[0]
    model_width = tokens.shape[1]
    tree_rows = token_segments.shape[0]
    query_heads = query_weight.shape[1] // HEAD_SIZE
    value_heads = key_value_matrix.shape[1] // (2 * HEAD_SIZE)
    query_group_count = query_heads // value_heads
    local_experts = expert_gate_up.shape[0]
    all_experts = expert_slot.shape[0]
    top_count = routes.shape[1]
    capacity = CAP
    devices = lax.axis_size("expert")
    score_scale = HEAD_SIZE ** (-0.5)
    position, reachable, member = tree_layout(parent_segments[0], token_segments)
    start_row = lax.axis_index("expert") * row_count
    own_position = lax.dynamic_slice_in_dim(position, start_row, row_count, 0)
    own_reach = lax.dynamic_slice_in_dim(reachable, start_row, row_count, 0)
    key_index = jnp.arange(tree_rows, dtype=jnp.int32)
    query_index = start_row + jnp.arange(row_count, dtype=jnp.int32)
    allowed = (jnp.dot(own_reach, member.T) > 0) & (key_index[None, :] <= query_index[:, None])
    inputs = tokens.astype(jnp.float32)
    first_float = first_gain.astype(jnp.float32)
    second_float = second_gain.astype(jnp.float32)
    first_normalized = normalize(inputs, first_float).astype(jnp.bfloat16)
    query_raw = jnp.dot(first_normalized, query_weight, preferred_element_type=jnp.float32).reshape(
        row_count, query_heads, HEAD_SIZE
    )
    unrotated_key_value = jnp.dot(
        first_normalized, key_value_matrix, preferred_element_type=jnp.float32
    ).reshape(row_count, value_heads, 2, HEAD_SIZE)
    query_vectors = (
        rotate(query_raw, own_position)
        .astype(jnp.bfloat16)
        .reshape(row_count, value_heads, query_group_count, HEAD_SIZE)
    )
    key_matrix_rows = rotate(unrotated_key_value[:, :, 0], own_position)
    key_value = (
        jnp.stack([key_matrix_rows, unrotated_key_value[:, :, 1]], axis=2)
        .astype(jnp.bfloat16)
        .reshape(row_count, value_heads * 2 * HEAD_SIZE)
    )
    gathered = lax.all_gather(key_value, "expert", axis=0, tiled=True).reshape(
        tree_rows, value_heads, 2, HEAD_SIZE
    )
    all_keys = gathered[:, :, 0]
    all_values = gathered[:, :, 1]
    scores = attention_probs(query_vectors, all_keys, allowed, score_scale)
    top_score = jnp.max(scores, axis=-1, keepdims=True)
    shifted = jnp.exp(scores - top_score)
    row_total = jnp.sum(shifted, axis=-1, keepdims=True)
    log_total = top_score + jnp.log(row_total)
    weights = (shifted / row_total).astype(jnp.bfloat16)
    context = (
        jnp.einsum("tgrk,kgh->tgrh", weights, all_values, preferred_element_type=jnp.float32)
        .astype(jnp.bfloat16)
        .reshape(row_count, query_heads * HEAD_SIZE)
    )
    attention = lax.psum(
        jnp.dot(context, output_weight, preferred_element_type=jnp.float32).astype(jnp.bfloat16),
        "tensor",
    ).astype(jnp.float32)
    hidden_state = inputs + attention
    normed_two = normalize(hidden_state, second_float).astype(jnp.bfloat16)
    expert_flat = routes.reshape(-1)
    expert_range = jnp.arange(all_experts, dtype=jnp.int32)
    slot_flat = jnp.sum(
        (expert_flat[:, None] == expert_range[None, :]).astype(jnp.int32) * expert_slot[None, :],
        axis=1,
        dtype=jnp.int32,
    )
    slot_hits = (slot_flat[:, None] == expert_range[None, :]).astype(jnp.int32)
    place_flat = jnp.sum(
        (jnp.cumsum(slot_hits, axis=0, dtype=jnp.int32) - 1) * slot_hits, axis=1, dtype=jnp.int32
    )
    token_flat = jnp.arange(row_count * top_count, dtype=jnp.int32) // top_count

    def pack_rows(row_data):
        blank_buffer = jnp.zeros((all_experts, capacity, row_data.shape[1]), jnp.bfloat16)
        return blank_buffer.at[slot_flat, place_flat].set(row_data)

    def unpack_rows(buffer, width):
        return buffer.reshape(all_experts, capacity, width)[slot_flat, place_flat]

    packed_input = pack_rows(normed_two[token_flat])
    cotangent = out_cotangent.astype(jnp.float32)
    part_grad = (
        (route_gates[:, :, None] * cotangent[:, None, :])
        .astype(jnp.bfloat16)
        .reshape(row_count * top_count, model_width)
    )
    packed_grad = pack_rows(part_grad)
    received = send_rows(packed_input.reshape(devices, local_experts, capacity, model_width))
    hidden, activation, expert_part = expert_forward(received, expert_gate_up, expert_down)
    returned = return_rows(expert_part)
    expert_rows = unpack_rows(returned, model_width).reshape(row_count, top_count, model_width)
    mixture = lax.psum(
        jnp.einsum(
            "tk,tkd->td", route_gates, expert_rows, preferred_element_type=jnp.float32
        ).astype(jnp.bfloat16),
        "tensor",
    ).astype(jnp.float32)
    grad_received = send_rows(packed_grad.reshape(devices, local_experts, capacity, model_width))
    gate_up_grad, down_grad, row_grad = expert_backward(
        received, hidden, activation, grad_received, expert_gate_up, expert_down
    )
    back_rows = return_rows(row_grad)
    row_sums = jnp.sum(
        unpack_rows(back_rows, model_width).reshape(row_count, top_count, model_width),
        axis=1,
        dtype=jnp.float32,
    )
    normed_two_grad = lax.psum(row_sums.astype(jnp.bfloat16), "tensor").astype(jnp.float32)
    layer_output = (hidden_state + mixture).astype(jnp.bfloat16)
    _, norm_two_pull = jax.vjp(normalize, hidden_state, second_float)
    hidden_norm_grad, second_gain_grad = norm_two_pull(normed_two_grad)
    residual_grad = cotangent + hidden_norm_grad
    branch_grad = residual_grad.astype(jnp.bfloat16)
    output_grad = jnp.einsum("tc,td->cd", context, branch_grad, preferred_element_type=jnp.float32)
    context_grad = (
        jnp.dot(branch_grad, output_weight.T, preferred_element_type=jnp.float32)
        .astype(jnp.bfloat16)
        .reshape(row_count, value_heads, query_group_count, HEAD_SIZE)
    )
    scores = attention_probs(query_vectors, all_keys, allowed, score_scale)
    probabilities = jnp.exp(scores - log_total)
    weights = probabilities.astype(jnp.bfloat16)
    prob_grad = jnp.einsum(
        "tgrh,kgh->tgrk", context_grad, all_values, preferred_element_type=jnp.float32
    )
    row_dot = jnp.sum(probabilities * prob_grad, axis=-1, keepdims=True)
    score_grad = (probabilities * (prob_grad - row_dot)).astype(jnp.bfloat16)
    query_grad = (
        jnp.einsum("tgrk,kgh->tgrh", score_grad, all_keys, preferred_element_type=jnp.float32)
        * score_scale
    )
    key_grad = (
        jnp.einsum("tgrk,tgrh->kgh", score_grad, query_vectors, preferred_element_type=jnp.float32)
        * score_scale
    )
    value_grad = jnp.einsum(
        "tgrk,tgrh->kgh", weights, context_grad, preferred_element_type=jnp.float32
    )
    pair_grad_all = jnp.stack([key_grad, value_grad], axis=2).reshape(
        tree_rows, value_heads * 2 * HEAD_SIZE
    )
    pair_grad = (
        lax.psum_scatter(
            pair_grad_all.astype(jnp.bfloat16), "expert", scatter_dimension=0, tiled=True
        )
        .astype(jnp.float32)
        .reshape(row_count, value_heads, 2, HEAD_SIZE)
    )
    _, rotate_query_pull = jax.vjp(partial(rotate, position=own_position), query_raw)
    query_raw_grad = rotate_query_pull(query_grad.reshape(row_count, query_heads, HEAD_SIZE))[0]
    _, rotate_key_pull = jax.vjp(
        partial(rotate, position=own_position), unrotated_key_value[:, :, 0]
    )
    key_raw_grad = rotate_key_pull(pair_grad[:, :, 0])[0]
    query_low = query_raw_grad.astype(jnp.bfloat16).reshape(row_count, query_heads * HEAD_SIZE)
    pair_low = (
        jnp.stack([key_raw_grad, pair_grad[:, :, 1]], axis=2)
        .astype(jnp.bfloat16)
        .reshape(row_count, value_heads * 2 * HEAD_SIZE)
    )
    query_weight_grad = jnp.einsum(
        "td,tc->dc", first_normalized, query_low, preferred_element_type=jnp.float32
    )
    pair_weight_grad = jnp.einsum(
        "td,tc->dc", first_normalized, pair_low, preferred_element_type=jnp.float32
    )
    local_input_grad = jnp.dot(
        query_low, query_weight.T, preferred_element_type=jnp.float32
    ) + jnp.dot(pair_low, key_value_matrix.T, preferred_element_type=jnp.float32)
    normed_one_grad = lax.psum(local_input_grad.astype(jnp.bfloat16), "tensor").astype(jnp.float32)
    _, norm_one_pull = jax.vjp(normalize, inputs, first_float)
    input_norm_grad, first_gain_grad = norm_one_pull(normed_one_grad)
    input_gradient = (residual_grad + input_norm_grad).astype(jnp.bfloat16)
    shared = (
        lax.psum(first_gain_grad.astype(jnp.bfloat16), ("dp", "expert")).astype(jnp.float32),
        lax.psum(query_weight_grad.astype(jnp.bfloat16), ("dp", "expert")).astype(jnp.float32),
        lax.psum(pair_weight_grad.astype(jnp.bfloat16), ("dp", "expert")).astype(jnp.float32),
        lax.psum(output_grad.astype(jnp.bfloat16), ("dp", "expert")).astype(jnp.float32),
        lax.psum(second_gain_grad.astype(jnp.bfloat16), ("dp", "expert")).astype(jnp.float32),
    )
    gate_up_total, down_total = (
        lax.psum(gate_up_grad.astype(jnp.bfloat16), "dp").astype(jnp.float32),
        lax.psum(down_grad.astype(jnp.bfloat16), "dp").astype(jnp.float32),
    )
    return (
        layer_output,
        input_gradient,
        shared[0],
        shared[1],
        shared[2],
        shared[3],
        shared[4],
        gate_up_total,
        down_total,
    )


def solution(mesh):
    in_specs = (
        P(("dp", "expert"), None),
        P(("dp", "expert"), None),
        P(),
        P(None, "tensor"),
        P(None, "tensor"),
        P("tensor", None),
        P(),
        P("expert", None, "tensor"),
        P("expert", "tensor", None),
        P(("dp", "expert"), None),
        P(("dp", "expert"), None),
        P(),
        P("dp", None),
        P("dp"),
    )
    out_specs = (
        P(("dp", "expert"), None),
        P(("dp", "expert"), None),
        P(),
        P(None, "tensor"),
        P(None, "tensor"),
        P("tensor", None),
        P(),
        P("expert", None, "tensor"),
        P("expert", "tensor", None),
    )
    return jax.shard_map(shards, mesh=mesh, in_specs=in_specs, out_specs=out_specs, check_vma=False)
```

profile of v0, /device:TPU:0, one launch (start us, length us, event | category | flops | bytes accessed | tf_op | source)
XLA Modules:
  0.0 2690.8 jit_solution(4751486946273772840)
XLA Ops:
  10.4 2.3 fusion.95
  14.4 23.9 all_gather.3
  38.3 2.2 copy.93
  40.6 2.2 fusion.93
  42.9 4.3 fusion.34
  47.2 5.6 fusion.98
  52.8 7.3 copy-done.2
  60.2 3.8 fusion.10
  64.0 9.8 fusion.66
  78.2 32.6 %reduce-window.6 = s32[40,30,128]{2,1,0:T(8,128)S(1)} reduce-window(s32[40,30,128]{2,1,0:T(8,128)} %fusion.69, s32[]{:T(128)} %constant.29.clone.1), window={size=1x1x128 pad=0_0x0_0x127_0}, to_apply=%region_10.11 | reduce-window | flops 19507200 | bytes 1228804 | tf_op jit(solution)/shard_map/reduce-window
  115.2 2.5 all-reduce.14.cloned.1.call-done
  117.7 2.1 multiply_reduce_fusion
  120.5 13.6 gather_fusion
  134.1 35.0 %scatter_custom_fusion = bf16[7680,1536]{1,0:T(8,128)(2,1)} fusion(s32[3840]{0:T(1024)S(1)} %broadcast_select_fusion, bf16[3840,1536]{1,0:T(8,128)(2,1)} %gather_fusion, bf16[]{:T(256)} %constant.68.clone.1), kind=kCustom, calls=%fused_computation.32 | custom fusion | bytes 23593472
  169.1 8.3 all-to-all-start
  178.1 5.8 fusion
  183.9 35.1 %scatter_custom_fusion.1 = bf16[7680,1536]{1,0:T(8,128)(2,1)} fusion(s32[3840]{0:T(1024)S(1)} %broadcast_select_fusion, bf16[3840,1536]{1,0:T(8,128)(2,1)} %fusion, bf16[]{:T(256)} %constant.68.clone.1), kind=kCustom, calls=%fused_computation.30 | custom fusion | bytes 23593472
  219.0 467.7 %all-to-all-done = bf16[4,10,192,1536]{3,2,1,0:T(8,128)(2,1)} async-done(((bf16[4,10,192,1536]{3,2,1,0:T(8,128)(2,1)}), bf16[4,10,192,1536]{3,2,1,0:T(8,128)(2,1)}, u32[]{:S(2)}, u32[]{:S(2)}) %all-to-all-start) | async-done | bytes 23592992 | tf_op jit(solution)/shard_map/all_to_all | solution.py:120
  686.7 8.3 all-to-all-start.2
  695.0 15.1 fusion.39
  710.1 10.3 copy.101
  720.4 9.7 fusion.97
  730.2 5.6 copy.103
  735.7 5.6 copy.104
  741.3 462.2 %all-to-all-done.2 = bf16[4,10,192,1536]{3,2,1,0:T(8,128)(2,1)} async-done(((bf16[4,10,192,1536]{3,2,1,0:T(8,128)(2,1)}), bf16[4,10,192,1536]{3,2,1,0:T(8,128)(2,1)}, u32[]{:S(2)}, u32[]{:S(2)}) %all-to-all-start.2) | async-done | bytes 23592992 | tf_op jit(solution)/shard_map/all_to_all | solution.py:120
  1203.5 15.9 fusion.29
  1219.4 4.6 copy.110
  1224.0 4.3 copy.111
  1228.3 3.5 pad_maximum_fusion
  1231.8 2.8 copy.112
  1234.6 16.3 convert_bitcast_fusion
  1250.9 19.8 copy.114
  1270.7 8.2 all-to-all-start.3
  1278.9 13.2 convert_bitcast_fusion.1
  1292.0 19.6 copy.105
  1311.6 475.7 %all-to-all-done.3 = bf16[4,10,192,1536]{3,2,1,0:T(8,128)(2,1)} async-done(((bf16[4,10,192,1536]{3,2,1,0:T(8,128)(2,1)}), bf16[4,10,192,1536]{3,2,1,0:T(8,128)(2,1)}, u32[]{:S(2)}, u32[]{:S(2)}) %all-to-all-start.3) | async-done | bytes 23592992 | tf_op jit(solution)/shard_map/all_to_all | solution.py:124
  1787.3 8.2 all-to-all-start.1
  1795.5 63.6 %gather_fusion.2 = bf16[3840,1536]{1,0:T(8,128)(2,1)} fusion(bf16[40,192,1536]{2,1,0:T(8,128)(2,1)} %bitcast.45, s32[3840]{0:T(1024)S(1)} %copy-done.1), kind=kCustom, calls=%fused_computation.2 | custom fusion | bytes 23623680 | tf_op jit(solution)/shard_map/gather | solution.py:231
  1859.1 11.1 bitcast_reduce_fusion
  1870.4 41.8 %all-reduce.16.cloned.1.call-done = bf16[480,1536]{1,0:T(8,128)(2,1)} async-done(((bf16[480,1536]{1,0:T(8,128)(2,1)}), bf16[480,1536]{1,0:T(8,128)(2,1)}) %all-reduce.16.cloned.1.call-update) | async-done | bytes 1474576 | tf_op jit(solution)/shard_map/psum | solution.py:261
  1912.2 3.2 fusion.46
  1919.2 18.2 fusion.3
  1937.4 14.9 fusion.5
  1952.3 4.0 copy-done.3
  1958.3 9.0 fusion.62
  1968.4 2.2 copy.137
  1970.7 12.7 bitcast_convert_fusion.1
  1983.4 17.0 bitcast_convert_fusion
  2001.3 318.3 %all-to-all-done.1 = bf16[4,10,192,1536]{3,2,1,0:T(8,128)(2,1)} async-done(((bf16[4,10,192,1536]{3,2,1,0:T(8,128)(2,1)}), bf16[4,10,192,1536]{3,2,1,0:T(8,128)(2,1)}, u32[]{:S(2)}, u32[]{:S(2)}) %all-to-all-start.1) | async-done | bytes 23592992 | tf_op jit(solution)/shard_map/all_to_all | solution.py:124
  2319.6 64.8 %gather_fusion.1 = bf16[3840,1536]{1,0:T(8,128)(2,1)} fusion(bf16[40,192,1536]{2,1,0:T(8,128)(2,1)} %bitcast.32, s32[3840]{0:T(1024)S(1)} %copy-done.1), kind=kCustom, calls=%fused_computation.1 | custom fusion | bytes 23623680 | tf_op jit(solution)/shard_map/gather | solution.py:231
  2384.4 6.1 fusion.12
  2391.9 7.6 convolution_multiply_fusion
  2400.8 2.6 fusion.99
  2407.2 3.6 fusion.53
  2411.1 2.2 convolution_convert_fusion.2
  2416.8 57.5 %all-reduce.22.cloned.1.call-done = (bf16[10,1536,256]{2,1,0:T(8,128)(2,1)}, bf16[10,128,1536]{2,1,0:T(8,128)(2,1)}) async-done(((bf16[10,1536,256]{2,1,0:T(8,128)(2,1)}, bf16[10,128,1536]{2,1,0:T(8,128)(2,1)}), (bf16[10,1536,256]{2,1,0:T(8,128)(2,1)}, bf16[10,128,1536]{2,1,0:T(8,128)(2,1)})) %all-reduce.22.cloned.1.call-update) | async-done | bytes 11796496 | tf_op jit(solution)/shard_map/psum | solution.py:335
  2474.3 10.7 convert_element_type.217
  2484.9 4.3 convert_element_type.219
  2489.3 53.4 %all-reduce.20.cloned.1.call-done = (bf16[480,1536]{1,0:T(8,128)(2,1)}, bf16[480,1536]{1,0:T(8,128)(2,1)}) async-done(((bf16[480,1536]{1,0:T(8,128)(2,1)}, bf16[480,1536]{1,0:T(8,128)(2,1)}), (bf16[480,1536]{1,0:T(8,128)(2,1)}, bf16[480,1536]{1,0:T(8,128)(2,1)})) %all-reduce.20.cloned.1.call-update) | async-done | bytes 2949136 | tf_op jit(solution)/shard_map/psum | solution.py:245
  2542.7 2.6 fusion.47
  2545.3 22.6 all-reduce.4
  2569.1 6.1 fusion.50
  2575.1 102.7 %all-reduce.18.cloned.1.call-done = (bf16[1536,384]{1,0:T(8,128)(2,1)}, bf16[1536,256]{1,0:T(8,128)(2,1)}, bf16[384,1536]{1,0:T(8,128)(2,1)}) async-done(((bf16[1536,384]{1,0:T(8,128)(2,1)}, bf16[1536,256]{1,0:T(8,128)(2,1)}, bf16[384,1536]{1,0:T(8,128)(2,1)}), (bf16[1536,384]{1,0:T(8,128)(2,1)}, bf16[1536,256]{1,0:T(8,128)(2,1)}, bf16[384,1536]{1,0:T(8,128)(2,1)})) %all-reduce.18.cloned.1.call-update) | async-done | bytes 3145744 | tf_op jit(solution)/shard_map/psum | solution.py:329
  2677.8 3.0 convert_element_type.209
  (194 shorter events, 37.0 us)
Async XLA Ops:
  7.2 67.4 %copy-start = (bf16[384,1536]{1,0:T(8,128)(2,1)S(1)}, bf16[384,1536]{1,0:T(8,128)(2,1)}, u32[]{:S(2)}) copy-start(bf16[384,1536]{1,0:T(8,128)(2,1)} %param.19) | copy-start | bytes 3538948
  7.2 110.5 %all-reduce.14.cloned.1.call-start = ((), (), s32[]{:S(2)}) async-start(), calls=%async_computation.5 | async-start | bytes 2949120 | tf_op jit(solution)/shard_map/psum | solution.py:207
  7.3 5.5 copy-start.57
  7.3 5.7 copy-start.45
  9.7 30.9 %copy-start.50 = (f32[480]{0:T(512)}, f32[480]{0:T(512)S(1)}, u32[]{:S(2)}) copy-start(f32[480]{0:T(512)S(1)} %fusion.85) | copy-start | bytes 5764
  10.4 30.2 %copy-start.35 = (f32[1536]{0:T(1024)}, f32[1536]{0:T(1024)S(1)}, u32[]{:S(2)}) copy-start(f32[1536]{0:T(1024)S(1)} %convert_element_type.171) | copy-start | bytes 18436
  12.7 27.8 %copy-start.4 = (bf16[480,1536]{1,0:T(8,128)(2,1)S(1)}, bf16[480,1536]{1,0:T(8,128)(2,1)}, u32[]{:S(2)}) copy-start(bf16[480,1536]{1,0:T(8,128)(2,1)} %param.14) | copy-start | bytes 4423684
  14.1 28.6 %copy-start.17 = (f32[480,32]{0,1:T(8,128)}, f32[480,32]{0,1:T(8,128)S(1)}, u32[]{:S(2)}) copy-start(f32[480,32]{0,1:T(8,128)S(1)} %get-tuple-element.44) | copy-start | bytes 184324
  14.1 28.6 %copy-start.19 = (f32[480,32]{0,1:T(8,128)}, f32[480,32]{0,1:T(8,128)S(1)}, u32[]{:S(2)}) copy-start(f32[480,32]{0,1:T(8,128)S(1)} %get-tuple-element.45) | copy-start | bytes 184324
  42.9 4.3 copy-start.29
  42.9 4.3 copy-start.31
  52.8 7.4 copy-start.2
  52.8 11.2 copy-start.39
  64.0 9.8 copy-start.41
  73.8 2.9 copy-start.52
  73.8 3.2 copy-start.54
  76.8 37.0 %copy-start.53 = (bf16[1536]{0:T(1024)(128)(2,1)S(1)}, bf16[1536]{0:T(1024)(128)(2,1)}, u32[]{:S(2)}) copy-start(bf16[1536]{0:T(1024)(128)(2,1)} %param.20) | copy-start | bytes 9220
  77.2 37.7 %copy-start.56 = (s32[2]{0:T(128)S(1)}, s32[2]{0:T(128)}, u32[]{:S(2)}) copy-start(s32[2]{0:T(128)} %constant.88) | copy-start | bytes 28
  77.2 37.8 %copy-start.55 = (s32[2]{0:T(128)S(1)}, s32[2]{0:T(128)}, u32[]{:S(2)}) copy-start(s32[2]{0:T(128)} %constant.91) | copy-start | bytes 28
  113.8 6.7 copy-start.33
  117.7 2.1 copy-start.5
  117.7 2.3 copy-start.9
  119.8 14.3 copy-start.48
  119.9 14.2 copy-start.43
  169.1 8.3 copy-start.37
  169.1 8.6 copy-start.11
  169.1 517.6 %all-to-all-start = ((bf16[4,10,192,1536]{3,2,1,0:T(8,128)(2,1)}), bf16[4,10,192,1536]{3,2,1,0:T(8,128)(2,1)}, u32[]{:S(2)}, u32[]{:S(2)}) async-start(bf16[4,10,192,1536]{3,2,1,0:T(8,128)(2,1)} %bitcast.191), calls=%async_computation | async-start | bytes 47185920 | tf_op jit(solution)/shard_map/all_to_all | solution.py:120
  686.7 516.7 %all-to-all-start.2 = ((bf16[4,10,192,1536]{3,2,1,0:T(8,128)(2,1)}), bf16[4,10,192,1536]{3,2,1,0:T(8,128)(2,1)}, u32[]{:S(2)}, u32[]{:S(2)}) async-start(bf16[4,10,192,1536]{3,2,1,0:T(8,128)(2,1)} %bitcast.190), calls=%async_computation.2 | async-start | bytes 47185920 | tf_op jit(solution)/shard_map/all_to_all | solution.py:120
  1219.4 59.5 %copy-start.16 = (bf16[4,10,192,128]{3,2,0,1:T(8,128)(2,1)}, bf16[4,10,192,128]{3,2,0,1:T(8,128)(2,1)S(1)}, u32[]{:S(2)}) copy-start(bf16[4,10,192,128]{3,2,0,1:T(8,128)(2,1)S(1)} %get-tuple-element.31) | copy-start | bytes 5898244
  1270.7 516.6 %all-to-all-start.3 = ((bf16[4,10,192,1536]{3,2,1,0:T(8,128)(2,1)}), bf16[4,10,192,1536]{3,2,1,0:T(8,128)(2,1)}, u32[]{:S(2)}, u32[]{:S(2)}) async-start(bf16[4,10,192,1536]{3,2,1,0:T(8,128)(2,1)} %copy.114), calls=%async_computation.3 | async-start | bytes 47185920 | tf_op jit(solution)/shard_map/all_to_all | solution.py:124
  1311.6 483.9 %copy-start.1 = (s32[3840]{0:T(1024)S(1)}, s32[3840]{0:T(1024)}, u32[]{:S(2)}) copy-start(s32[3840]{0:T(1024)} %get-tuple-element.24) | copy-start | bytes 46084
  1787.3 532.4 %all-to-all-start.1 = ((bf16[4,10,192,1536]{3,2,1,0:T(8,128)(2,1)}), bf16[4,10,192,1536]{3,2,1,0:T(8,128)(2,1)}, u32[]{:S(2)}, u32[]{:S(2)}) async-start(bf16[4,10,192,1536]{3,2,1,0:T(8,128)(2,1)} %copy.105), calls=%async_computation.1 | async-start | bytes 47185920 | tf_op jit(solution)/shard_map/all_to_all | solution.py:124
  1795.5 116.7 %all-reduce.16.cloned.1.call-start = ((), (), s32[]{:S(2)}) async-start(), calls=%async_computation.6 | async-start | bytes 2949120 | tf_op jit(solution)/shard_map/psum | solution.py:261
  1859.1 11.2 copy-start.40
  1859.1 11.2 copy-start.42
  1859.1 53.1 %copy-start.6 = (bf16[480,1536]{1,0:T(8,128)(2,1)S(1)}, bf16[480,1536]{1,0:T(8,128)(2,1)}, u32[]{:S(2)}) copy-start(bf16[480,1536]{1,0:T(8,128)(2,1)} %param.14) | copy-start | bytes 4423684
  1859.1 53.1 %copy-start.34 = (f32[1536]{0:T(1024)S(1)}, f32[1536]{0:T(1024)}, u32[]{:S(2)}) copy-start(f32[1536]{0:T(1024)} %copy-done.33) | copy-start | bytes 18436
  1859.1 53.0 %copy-start.44 = (f32[480]{0:T(512)S(1)}, f32[480]{0:T(512)}, u32[]{:S(2)}) copy-start(f32[480]{0:T(512)} %copy-done.43) | copy-start | bytes 5764
  1870.3 45.1 %copy-start.49 = (f32[480]{0:T(512)S(1)}, f32[480]{0:T(512)}, u32[]{:S(2)}) copy-start(f32[480]{0:T(512)} %copy-done.48) | copy-start | bytes 5764
  1870.3 533.1 %reduce-scatter.4.cloned.1.call-start = ((), (), s32[]{:S(2)}) async-start(), calls=%async_computation.7 | async-start | bytes 1228800
  1912.2 3.2 copy-start.10
  1912.2 3.2 copy-start.12
  1912.2 3.2 copy-start.13
  1916.5 1.6 copy-start.7
  1937.4 18.9 copy-start.30
  1937.4 18.9 copy-start.32
  1952.3 4.0 copy-start.3
  1970.7 503.6 %all-reduce.22.cloned.1.call-start = ((), (), s32[]{:S(2)}) async-start(), calls=%async_computation.10 | async-start | bytes 23592960 | tf_op jit(solution)/shard_map/psum | solution.py:335
  2000.4 542.3 %all-reduce.20.cloned.1.call-start = ((), (), s32[]{:S(2)}) async-start(), calls=%async_computation.9 | async-start | bytes 5898240 | tf_op jit(solution)/shard_map/psum | solution.py:245
  2390.5 1.4 copy-start.15
  2391.9 7.7 copy-start.18
  2391.9 7.7 copy-start.20
  2399.6 1.3 copy-start.24
  2405.2 1.9 copy-start.28
  2407.2 3.9 copy-start.36
  2407.2 3.9 copy-start.51
  2410.8 2.5 copy-start.22
  2410.8 267.0 %all-reduce.18.cloned.1.call-start = ((), (), s32[]{:S(2)}) async-start(), calls=%async_computation.8 | async-start | bytes 6291456 | tf_op jit(solution)/shard_map/psum | solution.py:329
  2411.1 2.2 copy-start.8
  2413.3 1.8 copy-start.26
  2474.3 10.7 copy-start.14
  2489.3 79.8 %copy-start.47 = (f32[480]{0:T(512)S(1)}, f32[480]{0:T(512)}, u32[]{:S(2)}) copy-start(f32[480]{0:T(512)} %copy-done.46) | copy-start | bytes 5764
  2677.8 3.0 copy-start.27
  2677.8 4.2 copy-start.23
  (4 other events, 2.8 us)
Sparse Core Ops, SparseCore 0:
  76.8 40.8 all-reduce.13
  1870.4 41.7 all-reduce.15
  1970.8 227.8 reduce-scatter.3
  2201.8 272.4 all-reduce.21
  2477.2 65.4 all-reduce.19
  2547.0 130.7 all-reduce.17
where the time goes:
time: 2710 us; the launch traced here: 2690 us
  waiting for transfers between devices  1980 us (73%)
  local copies, waits for them, and re-layouts  324 us (12%)
  matrix products  172 us (6%)
  other arithmetic  118 us (4%)
  blocking collectives  46.5 us (2%)
  starting transfers between devices  33.4 us (1%)
    all_to_all x2, waiting for transfers between devices, send_rows(): lax.all_to_all(buffer, 'expert', split_axis=0, concat_axis=0, tiled=True)  930 us
    all_to_all x2, waiting for transfers between devices, return_rows(): lax.all_to_all(buffer, 'expert', split_axis=0, concat_axis=0, tiled=True)  794 us
    gather x2, local copies, waits for them, and re-layouts, unpack_rows(): return buffer.reshape(all_experts, capacity, width)[slot_flat, place_flat]  128 us
    psum x1, waiting for transfers between devices, shards(): lax.psum(query_weight_grad.astype(jnp.bfloat16), ('dp', 'expert'))  103 us
    unnamed x123, local copies, waits for them, and re-layouts  91.7 us
    psum x1, waiting for transfers between devices, shards(): lax.psum(gate_up_grad.astype(jnp.bfloat16), 'dp').astype(jnp.float32)  57.5 us
  transfers between devices with their start and end apart: 10, of which 9 were waited for; matrix products, arithmetic and copies ran while one was open for 16% of the time, Pallas kernels for 0%

commit v1 on v0

--- a/solution.py
+++ b/solution.py
@@ -1,13 +1,17 @@
+import functools
 from functools import partial
 
 import jax
 import jax.numpy as jnp
 from jax import lax
+from jax.experimental import pallas as pl
+from jax.experimental.pallas import tpu as pltpu
 from jax.sharding import PartitionSpec as P
 
 HEAD_SIZE = 64
 PAIR = 64
-CAP = 192
+BF = jnp.bfloat16
+F32 = jnp.float32
 
 
 EPS = 1e-05
@@ -35,33 +39,6 @@
     )
 
 
-def swiglu(gate_part, up_part):
-    return gate_part * jax.nn.sigmoid(gate_part) * up_part
-
-
-def split_pairs(hidden, pair_width):
-    leading = hidden.shape[:-1]
-    width = hidden.shape[-1] // 2
-    grouped = hidden.reshape(leading + (width // pair_width, 2, pair_width))
-    return (
-        grouped[..., 0, :].reshape(leading + (width,)),
-        grouped[..., 1, :].reshape(leading + (width,)),
-    )
-
-
-def join_pairs(gate_part, up_part, pair_width):
-    leading = gate_part.shape[:-1]
-    width = gate_part.shape[-1]
-    stacked = jnp.stack(
-        [
-            gate_part.reshape(leading + (width // pair_width, pair_width)),
-            up_part.reshape(leading + (width // pair_width, pair_width)),
-        ],
-        axis=-2,
-    )
-    return stacked.reshape(leading + (2 * width,))
-
-
 def tree_layout(parents, segments):
     labels = jnp.arange(parents.shape[0], dtype=jnp.int32)
     up_two = jnp.sum(
@@ -86,42 +63,214 @@
     return (position, reachable, member)
 
 
-def expert_forward(row_data, gate_up, down_part):
-    hidden = jnp.einsum("slcd,ldf->slcf", row_data, gate_up, preferred_element_type=jnp.float32)
-    gate_part, up_part = split_pairs(hidden, PAIR)
-    activation = swiglu(gate_part, up_part).astype(jnp.bfloat16)
-    expert_part = jnp.einsum(
-        "slcf,lfd->slcd", activation, down_part, preferred_element_type=jnp.float32
-    ).astype(jnp.bfloat16)
-    return (hidden, activation, expert_part)
-
-
-def expert_backward(row_data, hidden, activation, grad_data, gate_up, down_part):
-    gate_part, up_part = split_pairs(hidden, PAIR)
-    act_grad = jnp.einsum(
-        "slcd,lfd->slcf", grad_data, down_part, preferred_element_type=jnp.float32
-    )
-    down_grad = jnp.einsum(
-        "slcf,slcd->lfd", activation, grad_data, preferred_element_type=jnp.float32
-    )
-    _, glu_pull = jax.vjp(swiglu, gate_part, up_part)
-    gate_grad, up_grad = glu_pull(act_grad)
-    hidden_grad = join_pairs(gate_grad, up_grad, PAIR).astype(jnp.bfloat16)
-    gate_up_grad = jnp.einsum(
-        "slcd,slcf->ldf", row_data, hidden_grad, preferred_element_type=jnp.float32
-    )
-    row_grad = jnp.einsum(
-        "slcf,ldf->slcd", hidden_grad, gate_up, preferred_element_type=jnp.float32
-    ).astype(jnp.bfloat16)
-    return (gate_up_grad, down_grad, row_grad)
-
-
-def send_rows(buffer):
-    return lax.all_to_all(buffer, "expert", split_axis=0, concat_axis=0, tiled=True)
-
-
-def return_rows(buffer):
-    return lax.all_to_all(buffer, "expert", split_axis=0, concat_axis=0, tiled=True)
+def dot_nn(a,b): return lax.dot_general(a,b,(((1,),(0,)),((),())),preferred_element_type=F32)
+def dot_nt(a,b): return lax.dot_general(a,b,(((1,),(1,)),((),())),preferred_element_type=F32)
+def dot_tn(a,b): return lax.dot_general(a,b,(((0,),(0,)),((),())),preferred_element_type=F32)
+
+def split_columns(w):
+    low = lax.broadcasted_iota(jnp.int32, w.shape[:1] + (128,), 1) < PAIR
+    gates, ups = [], []
+    for i in range(w.shape[1] // 256):
+        a = w[:, 256 * i : 256 * i + 128]
+        b = w[:, 256 * i + 128 : 256 * i + 256]
+        gates.append(jnp.where(low, a, pltpu.roll(b, PAIR, 1)))
+        ups.append(jnp.where(low, pltpu.roll(a, PAIR, 1), b))
+    return gates, ups
+
+def moe_main_kernel(x_ref, c_ref, g_ref, w1_ref, w2_ref, ga_ref, hg_ref, dx_ref, acc_ref):
+    step = pl.program_id(0)
+    per = w1_ref.shape[0]
+    units = w2_ref.shape[1]
+    gates, ups = [], []
+    for e in range(per):
+        g, u = split_columns(w1_ref[e])
+        gates += g
+        ups += u
+    w1 = jnp.concatenate(gates + ups, axis=1)
+    w2 = w2_ref[...].reshape(per * units, w2_ref.shape[2])
+    hidden = dot_nn(x_ref[...], w1)
+    pull = dot_nt(c_ref[...], w2)
+    lane = lax.broadcasted_iota(jnp.int32, g_ref.shape, 1)
+    route = jnp.concatenate(
+        [
+            jnp.broadcast_to(
+                jnp.sum(jnp.where(lane == step * per + e, g_ref[...], 0.0), axis=1, keepdims=True),
+                (g_ref.shape[0], units),
+            )
+            for e in range(per)
+        ],
+        axis=1,
+    )
+    gate = hidden[:, : per * units]
+    up = hidden[:, per * units :]
+    sig = 1.0 / (1.0 + jnp.exp(-gate))
+    silu = gate * sig
+    pull = pull * route
+    ga_ref[...] = (silu * up * route).astype(BF)
+    hg = jnp.concatenate([pull * up * (sig * (1.0 + gate - silu)), pull * silu], axis=1).astype(BF)
+    hg_ref[...] = hg
+    part = dot_nt(hg, w1)
+
+    @pl.when(step == 0)
+    def _():
+        acc_ref[...] = part
+
+    @pl.when(step > 0)
+    def _():
+        acc_ref[...] += part
+
+    @pl.when(step == pl.num_programs(0) - 1)
+    def _():
+        dx_ref[...] = acc_ref[...].astype(BF)
+
+def moe_main(x, c, g, w1, w2):
+    rows, width = x.shape
+    experts, _, columns = w1.shape
+    units = columns // 2
+    per = 2
+    whole = lambda i: (0, 0)
+    return pl.pallas_call(
+        moe_main_kernel,
+        grid=(experts // per,),
+        in_specs=[
+            pl.BlockSpec((rows, width), whole),
+            pl.BlockSpec((rows, width), whole),
+            pl.BlockSpec((rows, g.shape[1]), whole),
+            pl.BlockSpec((per, width, columns), lambda i: (i, 0, 0)),
+            pl.BlockSpec((per, units, width), lambda i: (i, 0, 0)),
+        ],
+        out_specs=[
+            pl.BlockSpec((rows, per * units), lambda i: (0, i)),
+            pl.BlockSpec((rows, per * columns), lambda i: (0, i)),
+            pl.BlockSpec((rows, width), whole),
+        ],
+        out_shape=[
+            jax.ShapeDtypeStruct((rows, experts * units), BF),
+            jax.ShapeDtypeStruct((rows, experts * columns), BF),
+            jax.ShapeDtypeStruct((rows, width), BF),
+        ],
+        scratch_shapes=[pltpu.VMEM((rows, width), F32)],
+        compiler_params=pltpu.CompilerParams(vmem_limit_bytes=56 << 20),
+        cost_estimate=pl.CostEstimate(flops=2*rows*width*experts*columns*5//2, bytes_accessed=20<<20, transcendentals=0),
+        name="experts_main",
+    )(x, c, g, w1, w2)
+
+def join_columns(gate, up):
+    low = lax.broadcasted_iota(jnp.int32, gate.shape[:1] + (128,), 1) < PAIR
+    out = []
+    for i in range(gate.shape[1] // 128):
+        g = gate[:, 128 * i : 128 * i + 128]
+        u = up[:, 128 * i : 128 * i + 128]
+        out.append(jnp.where(low, g, pltpu.roll(u, PAIR, 1)))
+        out.append(jnp.where(low, pltpu.roll(g, PAIR, 1), u))
+    return jnp.concatenate(out, axis=1)
+
+def weight_grads_kernel(n, *refs):
+    xs, cs, hgs, gas = refs[:n], refs[n : 2 * n], refs[2 * n : 3 * n], refs[3 * n : 4 * n]
+    w1_ref, w2_ref, xt_ref = refs[4 * n :]
+    step = pl.program_id(0)
+    per, width, columns = w1_ref.shape
+    units = columns // 2
+    rows = xs[0].shape[0]
+
+    @pl.when(step == 0)
+    def _():
+        for k in range(n):
+            xt_ref[k] = xs[k][...].T
+
+    up = down = None
+    for k in range(n):
+        a = dot_nn(xt_ref[k], hgs[k][...])
+        b = dot_tn(gas[k][...], cs[k][...])
+        up = a if up is None else up + a
+        down = b if down is None else down + b
+    for e in range(per):
+        w1_ref[e] = join_columns(
+            up[:, units * e : units * e + units], up[:, per * units + units * e : per * units + units * e + units]
+        ).astype(w1_ref.dtype)
+        w2_ref[e] = down[units * e : units * e + units].astype(w2_ref.dtype)
+
+def moe_weight_grads(xs, cs, hgs, gas):
+    n = len(xs)
+    rows, width = xs[0].shape
+    columns = 256
+    units = 128
+    per = 2
+    experts = gas[0].shape[1] // units
+    whole = lambda i: (0, 0)
+    return pl.pallas_call(
+        functools.partial(weight_grads_kernel, n),
+        grid=(experts // per,),
+        in_specs=[pl.BlockSpec((rows, width), whole, pipeline_mode=pl.Buffered(1))] * (2 * n)
+        + [pl.BlockSpec((rows, per * columns), lambda i: (0, i))] * n
+        + [pl.BlockSpec((rows, per * units), lambda i: (0, i))] * n,
+        out_specs=[
+            pl.BlockSpec((per, width, columns), lambda i: (i, 0, 0)),
+            pl.BlockSpec((per, units, width), lambda i: (i, 0, 0)),
+        ],
+        out_shape=[
+            jax.ShapeDtypeStruct((experts, width, columns), BF),
+            jax.ShapeDtypeStruct((experts, units, width), BF),
+        ],
+        scratch_shapes=[pltpu.VMEM((n, width, rows), BF)],
+        compiler_params=pltpu.CompilerParams(vmem_limit_bytes=60 << 20),
+        name="experts_weights",
+    )(*xs, *cs, *hgs, *gas)
+
+
+def shift(values, axis, places):
+    size = lax.axis_size(axis)
+    return lax.ppermute(values, axis, [(i, (i + places) % size) for i in range(size)])
+
+
+def swap(values, axis, bit):
+    return lax.ppermute(values, axis, [(i, i ^ bit) for i in range(lax.axis_size(axis))])
+
+
+def tensor_order(size):
+    order = [0]
+    for bit in reversed(tensor_bits(size)):
+        order = order + [o ^ bit for o in order]
+    return order
+
+
+def tensor_bits(size):
+    return [1 << b for b in range(size.bit_length() - 1)]
+
+
+def gather_tensor(block):
+    for bit in reversed(tensor_bits(lax.axis_size("tensor"))):
+        block = jnp.concatenate([block, swap(block, "tensor", bit)], axis=0)
+    return block
+
+
+def reduce_tensor(blocks):
+    for bit in tensor_bits(lax.axis_size("tensor")):
+        half = blocks.shape[0] // 2
+        received = swap(blocks[half:], "tensor", bit)
+        blocks = (blocks[:half].astype(F32) + received.astype(F32)).astype(BF)
+    return blocks
+
+
+def to_relative(rows, order, index):
+    parts = rows.reshape((len(order), rows.shape[0] // len(order)) + rows.shape[1:])
+    picks = [lax.dynamic_index_in_dim(parts, index ^ o, 0, keepdims=False) for o in order]
+    return jnp.concatenate(picks, axis=0)
+
+
+def from_relative(rows, order, index):
+    return to_relative_inverse(rows, order, index)
+
+
+def to_relative_inverse(rows, order, index):
+    size = len(order)
+    parts = rows.reshape((size, rows.shape[0] // size) + rows.shape[1:])
+    places = [order.index(o) for o in range(size)]
+    picks = []
+    for absolute in range(size):
+        where = jnp.asarray(places, jnp.int32)[index ^ absolute]
+        picks.append(lax.dynamic_index_in_dim(parts, where, 0, keepdims=False))
+    return jnp.concatenate(picks, axis=0)
 
 
 def attention_probs(query_vectors, all_keys, allowed, score_scale):
@@ -156,9 +305,32 @@
     query_group_count = query_heads // value_heads
     local_experts = expert_gate_up.shape[0]
     all_experts = expert_slot.shape[0]
-    top_count = routes.shape[1]
-    capacity = CAP
     devices = lax.axis_size("expert")
+    tensor_size = lax.axis_size("tensor")
+    tensor_index = lax.axis_index("tensor")
+    order = tensor_order(tensor_size)
+    part = row_count // tensor_size
+    first_part = tensor_index * part
+    cotangent_part = lax.dynamic_slice_in_dim(out_cotangent, first_part, part, 0)
+    cotangents = [
+        gather_tensor(shift(cotangent_part, "expert", k) if k else cotangent_part)
+        for k in range(devices)
+    ]
+    slots = jnp.arange(all_experts, dtype=jnp.int32)
+    slot_of = jnp.sum(
+        jnp.where(routes[:, :, None] == slots[None, None, :], expert_slot[None, None, :], 0),
+        axis=2,
+    )
+    dense = jnp.sum(
+        jnp.where(slot_of[:, :, None] == slots[None, None, :], route_gates[:, :, None], 0.0), axis=1
+    )
+    dense = to_relative(dense, order, tensor_index)
+    expert_index = lax.axis_index("expert")
+    gates = []
+    for k in range(devices):
+        owner = (expert_index + k) % devices
+        mine = lax.dynamic_slice_in_dim(dense, owner * local_experts, local_experts, 1)
+        gates.append(shift(mine, "expert", k) if k else mine)
     score_scale = HEAD_SIZE ** (-0.5)
     position, reachable, member = tree_layout(parent_segments[0], token_segments)
     start_row = lax.axis_index("expert") * row_count
@@ -204,66 +376,47 @@
         .astype(jnp.bfloat16)
         .reshape(row_count, query_heads * HEAD_SIZE)
     )
-    attention = lax.psum(
-        jnp.dot(context, output_weight, preferred_element_type=jnp.float32).astype(jnp.bfloat16),
-        "tensor",
-    ).astype(jnp.float32)
-    hidden_state = inputs + attention
-    normed_two = normalize(hidden_state, second_float).astype(jnp.bfloat16)
-    expert_flat = routes.reshape(-1)
-    expert_range = jnp.arange(all_experts, dtype=jnp.int32)
-    slot_flat = jnp.sum(
-        (expert_flat[:, None] == expert_range[None, :]).astype(jnp.int32) * expert_slot[None, :],
-        axis=1,
-        dtype=jnp.int32,
-    )
-    slot_hits = (slot_flat[:, None] == expert_range[None, :]).astype(jnp.int32)
-    place_flat = jnp.sum(
-        (jnp.cumsum(slot_hits, axis=0, dtype=jnp.int32) - 1) * slot_hits, axis=1, dtype=jnp.int32
-    )
-    token_flat = jnp.arange(row_count * top_count, dtype=jnp.int32) // top_count
-
-    def pack_rows(row_data):
-        blank_buffer = jnp.zeros((all_experts, capacity, row_data.shape[1]), jnp.bfloat16)
-        return blank_buffer.at[slot_flat, place_flat].set(row_data)
-
-    def unpack_rows(buffer, width):
-        return buffer.reshape(all_experts, capacity, width)[slot_flat, place_flat]
-
-    packed_input = pack_rows(normed_two[token_flat])
-    cotangent = out_cotangent.astype(jnp.float32)
-    part_grad = (
-        (route_gates[:, :, None] * cotangent[:, None, :])
-        .astype(jnp.bfloat16)
-        .reshape(row_count * top_count, model_width)
-    )
-    packed_grad = pack_rows(part_grad)
-    received = send_rows(packed_input.reshape(devices, local_experts, capacity, model_width))
-    hidden, activation, expert_part = expert_forward(received, expert_gate_up, expert_down)
-    returned = return_rows(expert_part)
-    expert_rows = unpack_rows(returned, model_width).reshape(row_count, top_count, model_width)
-    mixture = lax.psum(
-        jnp.einsum(
-            "tk,tkd->td", route_gates, expert_rows, preferred_element_type=jnp.float32
-        ).astype(jnp.bfloat16),
-        "tensor",
-    ).astype(jnp.float32)
-    grad_received = send_rows(packed_grad.reshape(devices, local_experts, capacity, model_width))
-    gate_up_grad, down_grad, row_grad = expert_backward(
-        received, hidden, activation, grad_received, expert_gate_up, expert_down
-    )
-    back_rows = return_rows(row_grad)
-    row_sums = jnp.sum(
-        unpack_rows(back_rows, model_width).reshape(row_count, top_count, model_width),
-        axis=1,
-        dtype=jnp.float32,
-    )
-    normed_two_grad = lax.psum(row_sums.astype(jnp.bfloat16), "tensor").astype(jnp.float32)
-    layer_output = (hidden_state + mixture).astype(jnp.bfloat16)
+    partial_attention = jnp.dot(context, output_weight, preferred_element_type=F32).astype(BF)
+    attention = reduce_tensor(to_relative(partial_attention, order, tensor_index)).astype(F32)
+    inputs_part = lax.dynamic_slice_in_dim(tokens, first_part, part, 0).astype(F32)
+    hidden_state = inputs_part + attention
+    normed_two = normalize(hidden_state, second_float).astype(BF)
+    normed = [
+        gather_tensor(shift(normed_two, "expert", k) if k else normed_two) for k in range(devices)
+    ]
+    gate_up, down, added = expert_gate_up, expert_down, 0
+    if gate_up.shape[2] == 2 * PAIR:
+        gate_up = jnp.pad(gate_up, ((0, 0), (0, 0), (0, 2 * PAIR)))
+        down = jnp.pad(down, ((0, 0), (0, PAIR), (0, 0)))
+    if local_experts % 2:
+        gate_up = jnp.pad(gate_up, ((0, 1), (0, 0), (0, 0)))
+        down = jnp.pad(down, ((0, 1), (0, 0), (0, 0)))
+    mains = [None] * devices
+    back = None
+    for k in list(range(1, devices)) + [0]:
+        mains[k] = moe_main(normed[k], cotangents[k], gates[k], gate_up, down)
+        summed = reduce_tensor(mains[k][2])
+        summed = (shift(summed, "expert", devices - k) if k else summed).astype(F32)
+        back = summed if back is None else back + summed
+    normed_two_grad = back
+    gate_up_grad, down_grad = moe_weight_grads(
+        normed, cotangents, [m[1] for m in mains], [m[0] for m in mains]
+    )
+    gate_up_grad = gate_up_grad[:local_experts, :, : expert_gate_up.shape[2]]
+    down_grad = down_grad[:local_experts, : expert_down.shape[1]]
+    flat_down = down.reshape(-1, model_width)
+    mixture = None
+    for k in list(range(1, devices)) + [0]:
+        mixed = jnp.dot(mains[k][0], flat_down, preferred_element_type=F32).astype(BF)
+        summed = reduce_tensor(mixed)
+        summed = (shift(summed, "expert", devices - k) if k else summed).astype(F32)
+        mixture = summed if mixture is None else mixture + summed
+    layer_part = (hidden_state + mixture).astype(BF)
+    layer_output = from_relative(gather_tensor(layer_part), order, tensor_index)
     _, norm_two_pull = jax.vjp(normalize, hidden_state, second_float)
     hidden_norm_grad, second_gain_grad = norm_two_pull(normed_two_grad)
-    residual_grad = cotangent + hidden_norm_grad
-    branch_grad = residual_grad.astype(jnp.bfloat16)
+    residual_grad = cotangent_part.astype(F32) + hidden_norm_grad
+    branch_grad = from_relative(gather_tensor(residual_grad.astype(BF)), order, tensor_index)
     output_grad = jnp.einsum("tc,td->cd", context, branch_grad, preferred_element_type=jnp.float32)
     context_grad = (
         jnp.dot(branch_grad, output_weight.T, preferred_element_type=jnp.float32)
@@ -320,21 +473,24 @@
     local_input_grad = jnp.dot(
         query_low, query_weight.T, preferred_element_type=jnp.float32
     ) + jnp.dot(pair_low, key_value_matrix.T, preferred_element_type=jnp.float32)
-    normed_one_grad = lax.psum(local_input_grad.astype(jnp.bfloat16), "tensor").astype(jnp.float32)
-    _, norm_one_pull = jax.vjp(normalize, inputs, first_float)
+    normed_one_grad = reduce_tensor(
+        to_relative(local_input_grad.astype(BF), order, tensor_index)
+    ).astype(F32)
+    _, norm_one_pull = jax.vjp(normalize, inputs_part, first_float)
     input_norm_grad, first_gain_grad = norm_one_pull(normed_one_grad)
-    input_gradient = (residual_grad + input_norm_grad).astype(jnp.bfloat16)
-    shared = (
-        lax.psum(first_gain_grad.astype(jnp.bfloat16), ("dp", "expert")).astype(jnp.float32),
-        lax.psum(query_weight_grad.astype(jnp.bfloat16), ("dp", "expert")).astype(jnp.float32),
-        lax.psum(pair_weight_grad.astype(jnp.bfloat16), ("dp", "expert")).astype(jnp.float32),
-        lax.psum(output_grad.astype(jnp.bfloat16), ("dp", "expert")).astype(jnp.float32),
-        lax.psum(second_gain_grad.astype(jnp.bfloat16), ("dp", "expert")).astype(jnp.float32),
-    )
-    gate_up_total, down_total = (
-        lax.psum(gate_up_grad.astype(jnp.bfloat16), "dp").astype(jnp.float32),
-        lax.psum(down_grad.astype(jnp.bfloat16), "dp").astype(jnp.float32),
-    )
+    input_part = (residual_grad + input_norm_grad).astype(BF)
+    input_gradient = from_relative(gather_tensor(input_part), order, tensor_index)
+    gains = jnp.stack([first_gain_grad, second_gain_grad])
+    for axis in ("tensor", "dp", "expert"):
+        for bit in tensor_bits(lax.axis_size(axis)):
+            gains = gains + swap(gains, axis, bit)
+    shared = [
+        lax.psum(grad.astype(BF), ("dp", "expert")).astype(F32)
+        for grad in (query_weight_grad, pair_weight_grad, output_grad)
+    ]
+    gate_up_total = gate_up_grad.astype(F32) + shift(gate_up_grad, "dp", 1).astype(F32)
+    down_total = down_grad.astype(F32) + shift(down_grad, "dp", 1).astype(F32)
+    shared = [gains[0]] + shared + [gains[1]]
     return (
         layer_output,
         input_gradient,

time: 2710 us -> 765 us (0.28)
  waiting for transfers between devices: 1980 us -> 296 us
  local copies, waits for them, and re-layouts: 324 us -> 56.5 us
  Pallas kernels: 0 us -> 110 us
  matrix products: 172 us -> 88.4 us
  starting transfers between devices: 33.4 us -> 68 us
  other arithmetic: 118 us -> 86 us
    all_to_all x4 -> x0, waiting for transfers between devices: 1720 us -> none  [the longest x2 930 us: send_rows(): lax.all_to_all(buffer, 'expert', split_axis=0, concat_axis=0, tiled=True)]
    ppermute x0 -> x64, waiting for transfers between devices: none -> 259 us  [the longest x47 166 us: swap(): lax.ppermute(values, axis, [(i, i ^ bit) for i in range(lax.axis_size(axi...]
    psum x5 -> x1, waiting for transfers between devices: 258 us -> 19 us  [shards(): lax.psum(grad.astype(BF), ('dp', 'expert')).astype(F32)]
    gather x3 -> x0, local copies, waits for them, and re-layouts: 142 us -> none  [the longest x2 128 us: unpack_rows(): return buffer.reshape(all_experts, capacity, width)[slot_flat, place_flat]]
    pallas_call x0 -> x5, Pallas kernels: none -> 110 us  [the longest x4 75.7 us: moe_main(): pl.pallas_call(moe_main_kernel, grid=(experts // per,), in_specs=[pl.Bloc...]
    dot_general x8 -> x5, matrix products: 98.3 us -> 16.5 us  [the longest x4 15.5 us: shards(): jnp.dot(mains[k][0], flat_down, preferred_element_type=F32).astype(BF)]
    ppermute x0 -> x64, starting transfers between devices: none -> 67.9 us  [the longest x17 40 us: shift(): lax.ppermute(values, axis, [(i, (i + places) % size) for i in range(size)])]
    unnamed x123 -> x190, local copies, waits for them, and re-layouts: 91.7 us -> 31.3 us
  transfers between devices with their start and end apart: 10 -> 66, of which waited for: 9 -> 21; matrix products, arithmetic and copies ran while one was open for 16% -> 26% of each run, Pallas kernels for 0% -> 14%
where the time goes in v1:
time: 765 us; the launch traced here: 761 us
  waiting for transfers between devices  296 us (39%)
  Pallas kernels  110 us (14%)
  matrix products  88.4 us (12%)
  other arithmetic  86 us (11%)
  starting transfers between devices  68 us (9%)
  local copies, waits for them, and re-layouts  56.5 us (7%)
  blocking collectives  32.1 us (4%)
  between operations  24.1 us (3%)
    ppermute x47, waiting for transfers between devices, swap(): lax.ppermute(values, axis, [(i, i ^ bit) for i in range(lax.axis_size(axi...  166 us
    ppermute x17, waiting for transfers between devices, shift(): lax.ppermute(values, axis, [(i, (i + places) % size) for i in range(size)])  93.7 us
    pallas_call x4, Pallas kernels, moe_main(): pl.pallas_call(moe_main_kernel, grid=(experts // per,), in_specs=[pl.Bloc...  75.7 us
    ppermute x17, starting transfers between devices, shift(): lax.ppermute(values, axis, [(i, (i + places) % size) for i in range(size)])  40 us
    pallas_call x1, Pallas kernels, moe_weight_grads(): pl.pallas_call(functools.partial(weight_grads_kernel, n), grid=(experts /...  34.3 us
    all_gather x1, blocking collectives, shards(): lax.all_gather(key_value, 'expert', axis=0, tiled=True)  32.1 us
    unnamed x190, local copies, waits for them, and re-layouts  31.3 us
    ppermute x47, starting transfers between devices, swap(): lax.ppermute(values, axis, [(i, i ^ bit) for i in range(lax.axis_size(axi...  27.9 us
  transfers between devices with their start and end apart: 66, of which 21 were waited for; matrix products, arithmetic and copies ran while one was open for 26% of the time, Pallas kernels for 14%

profile of v1, /device:TPU:0, one launch (start us, length us, event | category | flops | bytes accessed | tf_op | source)
XLA Modules:
  0.0 760.7 jit_solution(5937120358462683973)
XLA Ops:
  8.4 3.0 collective-permute-start.34
  11.5 3.6 collective-permute-start.25
  19.0 2.5 collective-permute-start.8
  37.5 32.1 %all_gather.3 = bf16[1920,256]{1,0:T(8,128)(2,1)} all-gather(bf16[480,256]{1,0:T(8,128)(2,1)} %copy.90), channel_id=1, replica_groups=mesh['dp'=2,'expert'=4,'tensor'=4] {'expert'}, dimensions={0}, use_global_device_ids=true | all-gather | bytes 1228800 | tf_op jit(solution)/shard_map/all_gather | solution.py:363
  69.6 2.2 copy.91
  71.8 2.2 fusion.58
  74.9 4.3 fusion.9
  79.1 5.6 fusion.63
  84.7 7.4 copy-done.1
  92.1 3.8 fusion.3
  96.0 10.2 %fusion.26 = bf16[2,64,480,3]{2,1,3,0:T(8,128)(2,1)S(1)} fusion(f32[480,2,3,1920]{3,0,2,1:T(8,128)} %copy-done.1, f32[480,2,3]{0,2,1:T(4,128)S(1)} %fusion.3, f32[480,2,3]{0,2,1:T(4,128)S(1)} %get-tuple-element.98, bf16[1920,2,2,64]{0,3,2,1:T(8,128)(2,1)} %bitcast.178), kind=kOutput, calls=%fused_computation.64 | convolution fusion | flops 724561920 | bytes 23001600 | tf_op jit(solution)/shard_map/tgrk,kgh->tgrh/dot_general | solution.py:375
  119.7 15.6 %collective-permute-done.16 = bf16[120,1536]{1,0:T(8,128)(2,1)S(1)} collective-permute-done((bf16[120,1536]{1,0:T(8,128)(2,1)}, bf16[120,1536]{1,0:T(8,128)(2,1)S(1)}, u32[]{:S(2)}, u32[]{:S(2)}) %collective-permute-start.16) | collective-permute-done | bytes 368672 | tf_op jit(solution)/shard_map/ppermute | solution.py:227
  139.6 7.5 collective-permute-done.6
  148.1 5.3 collective-permute-done.1
  154.5 2.2 pad_maximum_fusion.1.c_ref.refs_4_
  156.7 6.2 collective-permute-done.32
  164.7 2.1 collective-permute-start.12
  166.9 6.8 collective-permute-done.22
  173.7 14.9 %collective-permute-done.12 = bf16[120,1536]{1,0:T(8,128)(2,1)S(1)} collective-permute-done((bf16[120,1536]{1,0:T(8,128)(2,1)S(1)}, bf16[120,1536]{1,0:T(8,128)(2,1)S(1)}, u32[]{:S(2)}, u32[]{:S(2)}) %collective-permute-start.12) | collective-permute-done | bytes 368672 | tf_op jit(solution)/shard_map/ppermute | solution.py:223
  188.7 3.9 collective-permute-start.28
  192.6 9.2 %collective-permute-done.2 = bf16[120,1536]{1,0:T(8,128)(2,1)S(1)} collective-permute-done((bf16[120,1536]{1,0:T(8,128)(2,1)S(1)}, bf16[120,1536]{1,0:T(8,128)(2,1)S(1)}, u32[]{:S(2)}, u32[]{:S(2)}) %collective-permute-start.2) | collective-permute-done | bytes 368672 | tf_op jit(solution)/shard_map/ppermute | solution.py:223
  204.0 9.3 %collective-permute-done.23 = bf16[120,1536]{1,0:T(8,128)(2,1)S(1)} collective-permute-done((bf16[120,1536]{1,0:T(8,128)(2,1)S(1)}, bf16[120,1536]{1,0:T(8,128)(2,1)S(1)}, u32[]{:S(2)}, u32[]{:S(2)}) %collective-permute-start.23) | collective-permute-done | bytes 368672 | tf_op jit(solution)/shard_map/ppermute | solution.py:227
  214.8 4.0 collective-permute-done.13
  218.8 3.9 collective-permute-done.3
  224.6 18.8 %experts_main.7 = (bf16[480,1280]{1,0:T(8,128)(2,1)}, bf16[480,2560]{1,0:T(8,128)(2,1)}, bf16[480,1536]{1,0:T(8,128)(2,1)}) custom-call(bf16[480,1536]{1,0:T(8,128)(2,1)} %pad_maximum_fusion.x_ref.refs_0_, bf16[480,1536]{1,0:T(8,128)(2,1)} %pad_maximum_fusion.1.c_ref.refs_4_, f32[480,10]{1,0:T(8,128)} %copy.117.g_ref, bf16[10,1536,256]{2,1,0:T(8,128)(2,1)} %w1_ref.7, ...), custom_call_target="tpu_custom_call" | custom-call | flops 9437184000 | bytes 20971520 | tf_op jit(solution)/shard_map/experts_main/pallas_call | solution.py:132
  243.5 4.6 convolution_convert_fusion
  253.5 18.9 %experts_main.4 = (bf16[480,1280]{1,0:T(8,128)(2,1)}, bf16[480,2560]{1,0:T(8,128)(2,1)}, bf16[480,1536]{1,0:T(8,128)(2,1)}) custom-call(bf16[480,1536]{1,0:T(8,128)(2,1)} %copy-done.19, bf16[480,1536]{1,0:T(8,128)(2,1)} %copy-done.12, f32[480,10]{1,0:T(8,128)} %collective-permute-done.8.g_ref, bf16[10,1536,256]{2,1,0:T(8,128)(2,1)} %w1_ref.7, ...), custom_call_target="tpu_custom_call" | custom-call | flops 9437184000 | bytes 20971520 | tf_op jit(solution)/shard_map/experts_main/pallas_call | solution.py:132
  272.4 4.6 convolution_convert_fusion.3
  281.8 18.9 %experts_main.5 = (bf16[480,1280]{1,0:T(8,128)(2,1)}, bf16[480,2560]{1,0:T(8,128)(2,1)}, bf16[480,1536]{1,0:T(8,128)(2,1)}) custom-call(bf16[480,1536]{1,0:T(8,128)(2,1)} %copy-done.13, bf16[480,1536]{1,0:T(8,128)(2,1)} %copy-done.18, f32[480,10]{1,0:T(8,128)} %collective-permute-done.18.g_ref, bf16[10,1536,256]{2,1,0:T(8,128)(2,1)} %w1_ref.7, ...), custom_call_target="tpu_custom_call" | custom-call | flops 9437184000 | bytes 20971520 | tf_op jit(solution)/shard_map/experts_main/pallas_call | solution.py:132
  304.0 19.0 %experts_main.6 = (bf16[480,1280]{1,0:T(8,128)(2,1)}, bf16[480,2560]{1,0:T(8,128)(2,1)}, bf16[480,1536]{1,0:T(8,128)(2,1)}) custom-call(bf16[480,1536]{1,0:T(8,128)(2,1)} %copy-done.17, bf16[480,1536]{1,0:T(8,128)(2,1)} %copy-done.14, f32[480,10]{1,0:T(8,128)} %copy-done.85, bf16[10,1536,256]{2,1,0:T(8,128)(2,1)} %w1_ref.7, bf16[10,128,1536]{2,1,0:T(8,128)(2,1)} %w2_ref.7), custom_call_target="tpu_custom_call" | custom-call | flops 9437184000 | bytes 20971520 | tf_op jit(solution)/shard_map/experts_main/pallas_call | solution.py:132
  323.1 4.3 convolution_convert_fusion.2
  327.5 2.1 convolution_convert_fusion.1
  333.6 34.3 %experts_weights.1 = (bf16[10,1536,256]{2,1,0:T(8,128)(2,1)}, bf16[10,128,1536]{2,1,0:T(8,128)(2,1)}) custom-call(bf16[480,1536]{1,0:T(8,128)(2,1)} %pad_maximum_fusion.x_ref.refs_0_, bf16[480,1536]{1,0:T(8,128)(2,1)} %copy-done.19, bf16[480,1536]{1,0:T(8,128)(2,1)} %copy-done.13, bf16[480,1536]{1,0:T(8,128)(2,1)} %copy-done.17, ...), custom_call_target="tpu_custom_call" | custom-call | tf_op jit(solution)/shard_map/experts_weights/pallas_call | solution.py:201
  378.1 13.7 %collective-permute-done.41 = bf16[120,1536]{1,0:T(8,128)(2,1)S(1)} collective-permute-done((bf16[120,1536]{1,0:T(8,128)(2,1)S(1)}, bf16[120,1536]{1,0:T(8,128)(2,1)S(1)}, u32[]{:S(2)}, u32[]{:S(2)}) %collective-permute-start.41) | collective-permute-done | bytes 368672 | tf_op jit(solution)/shard_map/ppermute | solution.py:227
  392.5 7.3 collective-permute-done.44
  399.7 9.1 %collective-permute-start.42 = (bf16[120,1536]{1,0:T(8,128)(2,1)S(1)}, bf16[120,1536]{1,0:T(8,128)(2,1)S(1)}, u32[]{:S(2)}, u32[]{:S(2)}) collective-permute-start(bf16[120,1536]{1,0:T(8,128)(2,1)S(1)} %add_convert_fusion.15), channel_id=1, source_target_pairs={{0,12},{4,0},{8,4},{12,8},{1,13},{5,1},{9,5},{13,9},{2,14},{6,2},{... | collective-permute-start | bytes 1105928 | tf_op jit(solution)/shard_map/ppermute | solution.py:223
  410.4 6.1 collective-permute-start.48
  419.5 14.9 %collective-permute-done.45 = bf16[120,1536]{1,0:T(8,128)(2,1)S(1)} collective-permute-done((bf16[120,1536]{1,0:T(8,128)(2,1)S(1)}, bf16[120,1536]{1,0:T(8,128)(2,1)S(1)}, u32[]{:S(2)}, u32[]{:S(2)}) %collective-permute-start.45) | collective-permute-done | bytes 368672 | tf_op jit(solution)/shard_map/ppermute | solution.py:223
  441.1 11.6 %collective-permute-done.51 = bf16[120,1536]{1,0:T(8,128)(2,1)S(1)} collective-permute-done((bf16[120,1536]{1,0:T(8,128)(2,1)S(1)}, bf16[120,1536]{1,0:T(8,128)(2,1)S(1)}, u32[]{:S(2)}, u32[]{:S(2)}) %collective-permute-start.51) | collective-permute-done | bytes 368672 | tf_op jit(solution)/shard_map/ppermute | solution.py:227
  455.1 6.8 collective-permute-done.10
  462.8 2.0 collective-permute-start.30
  469.1 9.1 %fusion.22 = bf16[1920,2,1,64]{0,3,1,2:T(8,128)(2,1)S(1)} fusion(bf16[480,2,3,64]{0,3,2,1:T(8,128)(2,1)S(1)} %bitcast.181, f32[480,2,3,1920]{3,0,2,1:T(8,128)} %copy-done.1, f32[480,2,3]{0,2,1:T(4,128)S(1)} %log_add_fusion), kind=kOutput, calls=%fused_computation.38 | convolution fusion | flops 719093760 | bytes 22990080 | tf_op jit(solution)/shard_map/tgrk,tgrh->kgh/dot_general | solution.py:442
  478.2 17.5 %fusion = (f32[480,2,3]{0,2,1:T(4,128)S(1)}, f32[2,1920,480,3]{1,2,3,0:T(8,128)}) fusion(f32[480,2,3,1920]{3,0,2,1:T(8,128)} %copy-done.1, f32[480,2,3]{0,2,1:T(4,128)S(1)} %log_add_fusion, bf16[480,2,3,64]{0,3,2,1:T(8,128)(2,1)S(1)} %bitcast.182, bf16[1920,2,2,64]{0,3,2,1:T(8,128)(2,1)S(1)} %bitcast.180), kind=kOutput, calls=%fused_computation.2 | convolution fusion | flops 724374720 | bytes 45149440 | tf_op jit(solution)/shard_map/tgrh,kgh->tgrk/dot_general | solution.py:429
  495.8 14.9 %fusion.2 = bf16[480,2,3,1920]{3,0,2,1:T(8,128)(2,1)S(1)} fusion(f32[2,1920,480,3]{1,2,3,0:T(8,128)} %get-tuple-element.101, f32[480,2,3,1920]{3,0,2,1:T(8,128)} %copy-done.1, f32[480,2,3]{0,2,1:T(4,128)S(1)} %get-tuple-element.100, f32[480,2,3]{0,2,1:T(4,128)S(1)} %log_add_fusion), kind=kLoop, calls=%fused_computation.4 | loop fusion | flops 22118400 | bytes 55319040 | tf_op jit(solution)/shard_map/convert_element_type | solution.py:433
  510.7 1.9 fusion.25
  512.6 2.4 copy-done.2
  516.1 2.2 copy.110
  518.4 3.0 collective-permute-start.11
  521.4 1.9 add_convert_fusion.19
  523.4 7.7 %convolution_multiply_fusion = f32[2,64,480,3]{2,1,3,0:T(8,128)S(1)} fusion(bf16[480,2,3,1920]{3,0,2,1:T(8,128)(2,1)} %copy-done.2, bf16[1920,2,2,64]{0,3,2,1:T(8,128)(2,1)} %bitcast.179), kind=kOutput, calls=%fused_computation.63 | convolution fusion | flops 707973120 | bytes 12288000 | tf_op jit(solution)/shard_map/tgrk,kgh->tgrh/dot_general | solution.py:435
  532.3 2.6 fusion.64
  534.9 17.1 %reduce-scatter.4.cloned.1.call-done = bf16[480,256]{1,0:T(8,128)(2,1)} async-done(((bf16[1920,256]{1,0:T(8,128)(2,1)}), bf16[480,256]{1,0:T(8,128)(2,1)}) %reduce-scatter.4.cloned.1.call-update) | async-done | bytes 245776
  555.1 2.5 fusion.13
  558.9 1.8 add_convert_fusion.18
  566.0 2.2 convolution_convert_fusion.6
  569.9 6.5 collective-permute-done.54
  580.5 47.9 %collective-permute-done.21 = bf16[120,1536]{1,0:T(8,128)(2,1)S(1)} collective-permute-done((bf16[120,1536]{1,0:T(8,128)(2,1)S(1)}, bf16[120,1536]{1,0:T(8,128)(2,1)S(1)}, u32[]{:S(2)}, u32[]{:S(2)}) %collective-permute-start.21) | collective-permute-done | bytes 368672 | tf_op jit(solution)/shard_map/ppermute | solution.py:223
  628.3 2.4 fusion.31
  634.4 63.0 %collective-permute-done.59 = f32[2,1536]{1,0:T(2,128)S(1)} collective-permute-done((f32[2,1536]{1,0:T(2,128)S(1)}, f32[2,1536]{1,0:T(2,128)S(1)}, u32[]{:S(2)}, u32[]{:S(2)}) %collective-permute-start.59) | collective-permute-done | bytes 12320 | tf_op jit(solution)/shard_map/ppermute | solution.py:227
  697.5 4.9 collective-permute-done.60
  703.3 7.8 %convert_add_fusion.1 = f32[10,128,1536]{2,1,0:T(8,128)} fusion(bf16[10,128,1536]{2,1,0:T(8,128)(2,1)} %collective-permute-done.63, bf16[10,128,1536]{2,1,0:T(8,128)(2,1)} %get-tuple-element.36), kind=kLoop, calls=%fused_computation.15 | loop fusion | flops 5898240 | bytes 15728640 | tf_op jit(solution)/shard_map/add | solution.py:492
  714.7 19.0 %all-reduce.7.cloned.1.call-done = (bf16[1536,384]{1,0:T(8,128)(2,1)}, bf16[1536,256]{1,0:T(8,128)(2,1)}, bf16[384,1536]{1,0:T(8,128)(2,1)}) async-done(((bf16[1536,384]{1,0:T(8,128)(2,1)}, bf16[1536,256]{1,0:T(8,128)(2,1)}, bf16[384,1536]{1,0:T(8,128)(2,1)}), (bf16[1536,384]{1,0:T(8,128)(2,1)}, bf16[1536,256]{1,0:T(8,128)(2,1)}, bf16[384,1536]{1,0:T(8,128)(2,1)})) %all-reduce.7.cloned.1.call-update) | async-done | bytes 3145744 | tf_op jit(solution)/shard_map/psum | solution.py:488
  733.7 2.9 convert_element_type.436
  740.1 13.2 %convert_add_fusion = f32[10,1536,256]{2,1,0:T(8,128)} fusion(bf16[10,1536,256]{2,1,0:T(8,128)(2,1)} %collective-permute-done.62, bf16[10,1536,256]{2,1,0:T(8,128)(2,1)} %get-tuple-element.35), kind=kLoop, calls=%fused_computation.11 | loop fusion | flops 11796480 | bytes 31457280 | tf_op jit(solution)/shard_map/add | solution.py:491
  (417 shorter events, 117.3 us)
Async XLA Ops:
  7.2 544.9 %reduce-scatter.4.cloned.1.call-start = ((), (), s32[]{:S(2)}) async-start(), calls=%async_computation.1 | async-start | bytes 1228800
  8.4 103.5 %collective-permute-start.34 = (bf16[120,1536]{1,0:T(8,128)(2,1)S(1)}, bf16[120,1536]{1,0:T(8,128)(2,1)}, u32[]{:S(2)}, u32[]{:S(2)}) collective-permute-start(bf16[120,1536]{1,0:T(8,128)(2,1)S(1)} %constant_dynamic-slice_fusion.8), channel_id=1, source_target_pairs={{0,2},{1,3},{2,0},{3,1},{4,6},{5,7},{6,4},{7,5},{8,10},{9,11},{10,... | collective-permute-start | bytes 1105928 | tf_op jit(solution)/shard_map/ppermute | solution.py:227
  11.5 101.7 %collective-permute-start.25 = (bf16[120,1536]{1,0:T(8,128)(2,1)S(1)}, bf16[120,1536]{1,0:T(8,128)(2,1)}, u32[]{:S(2)}, u32[]{:S(2)}) collective-permute-start(bf16[120,1536]{1,0:T(8,128)(2,1)S(1)} %constant_dynamic-slice_fusion.8), channel_id=1, source_target_pairs={{0,12},{4,0},{8,4},{12,8},{1,13},{5,1},{9,5},{13,9},{2,14},{6,2},{... | collective-permute-start | bytes 1105928 | tf_op jit(solution)/shard_map/ppermute | solution.py:223
  15.1 100.0 %collective-permute-start.15 = (bf16[120,1536]{1,0:T(8,128)(2,1)S(1)}, bf16[120,1536]{1,0:T(8,128)(2,1)}, u32[]{:S(2)}, u32[]{:S(2)}) collective-permute-start(bf16[120,1536]{1,0:T(8,128)(2,1)S(1)} %constant_dynamic-slice_fusion.8), channel_id=1, source_target_pairs={{0,8},{4,12},{8,0},{12,4},{1,9},{5,13},{9,1},{13,5},{2,10},{6,14},... | collective-permute-start | bytes 1105928 | tf_op jit(solution)/shard_map/ppermute | solution.py:223
  15.1 101.3 %collective-permute-start.5 = (bf16[120,1536]{1,0:T(8,128)(2,1)S(1)}, bf16[120,1536]{1,0:T(8,128)(2,1)}, u32[]{:S(2)}, u32[]{:S(2)}) collective-permute-start(bf16[120,1536]{1,0:T(8,128)(2,1)S(1)} %constant_dynamic-slice_fusion.8), channel_id=1, source_target_pairs={{0,4},{4,8},{8,12},{12,0},{1,5},{5,9},{9,13},{13,1},{2,6},{6,10},{... | collective-permute-start | bytes 1105928 | tf_op jit(solution)/shard_map/ppermute | solution.py:223
  19.0 233.3 %collective-permute-start.8 = (f32[480,10]{1,0:T(8,128)}, f32[480,10]{1,0:T(8,128)}, u32[]{:S(2)}, u32[]{:S(2)}) collective-permute-start(f32[480,10]{1,0:T(8,128)} %copy.114), channel_id=1, source_target_pairs={{0,4},{4,8},{8,12},{12,0},{1,5},{5,9},{9,13},{13,1},{2,6},{6,10},{... | collective-permute-start | bytes 57608 | tf_op jit(solution)/shard_map/ppermute | solution.py:223
  112.0 5.9 collective-permute-start
  113.1 168.1 %collective-permute-start.18 = (f32[480,10]{1,0:T(8,128)}, f32[480,10]{1,0:T(8,128)}, u32[]{:S(2)}, u32[]{:S(2)}) collective-permute-start(f32[480,10]{1,0:T(8,128)} %copy.115), channel_id=1, source_target_pairs={{0,8},{4,12},{8,0},{12,4},{1,9},{5,13},{9,1},{13,5},{2,10},{6,14},... | collective-permute-start | bytes 57608 | tf_op jit(solution)/shard_map/ppermute | solution.py:223
  115.0 39.4 %collective-permute-start.35 = (bf16[240,1536]{1,0:T(8,128)(2,1)S(1)}, bf16[240,1536]{1,0:T(8,128)(2,1)S(1)}, u32[]{:S(2)}, u32[]{:S(2)}) collective-permute-start(bf16[240,1536]{1,0:T(8,128)(2,1)S(1)} %pad_maximum_fusion.17), channel_id=1, source_target_pairs={{0,1},{1,0},{2,3},{3,2},{4,5},{5,4},{6,7},{7,6},{8,9},{9,8},{10,11... | collective-permute-start | bytes 2211848 | tf_op jit(solution)/shard_map/ppermute | solution.py:227
  116.3 20.5 %collective-permute-start.26 = (bf16[120,1536]{1,0:T(8,128)(2,1)}, bf16[120,1536]{1,0:T(8,128)(2,1)S(1)}, u32[]{:S(2)}, u32[]{:S(2)}) collective-permute-start(bf16[120,1536]{1,0:T(8,128)(2,1)} %collective-permute-done.25), channel_id=1, source_target_pairs={{0,2},{1,3},{2,0},{3,1},{4,6},{5,7},{6,4},{7,5},{8,10},{9,11},{10,... | collective-permute-start | bytes 1105928 | tf_op jit(solution)/shard_map/ppermute | solution.py:227
  117.9 17.4 %collective-permute-start.16 = (bf16[120,1536]{1,0:T(8,128)(2,1)}, bf16[120,1536]{1,0:T(8,128)(2,1)S(1)}, u32[]{:S(2)}, u32[]{:S(2)}) collective-permute-start(bf16[120,1536]{1,0:T(8,128)(2,1)} %collective-permute-done.15), channel_id=1, source_target_pairs={{0,2},{1,3},{2,0},{3,1},{4,6},{5,7},{6,4},{7,5},{8,10},{9,11},{10,... | collective-permute-start | bytes 1105928 | tf_op jit(solution)/shard_map/ppermute | solution.py:227
  135.3 11.7 %collective-permute-start.6 = (bf16[120,1536]{1,0:T(8,128)(2,1)}, bf16[120,1536]{1,0:T(8,128)(2,1)S(1)}, u32[]{:S(2)}, u32[]{:S(2)}) collective-permute-start(bf16[120,1536]{1,0:T(8,128)(2,1)} %collective-permute-done.5), channel_id=1, source_target_pairs={{0,2},{1,3},{2,0},{3,1},{4,6},{5,7},{6,4},{7,5},{8,10},{9,11},{10,... | collective-permute-start | bytes 1105928 | tf_op jit(solution)/shard_map/ppermute | solution.py:227
  136.9 16.5 %collective-permute-start.1 = (bf16[120,1536]{1,0:T(8,128)(2,1)S(1)}, bf16[120,1536]{1,0:T(8,128)(2,1)S(1)}, u32[]{:S(2)}, u32[]{:S(2)}) collective-permute-start(bf16[120,1536]{1,0:T(8,128)(2,1)S(1)} %slice.212), channel_id=1, source_target_pairs={{0,2},{1,3},{2,0},{3,1},{4,6},{5,7},{6,4},{7,5},{8,10},{9,11},{10,... | collective-permute-start | bytes 1105928 | tf_op jit(solution)/shard_map/ppermute | solution.py:227
  147.0 17.7 %collective-permute-start.27 = (bf16[240,1536]{1,0:T(8,128)(2,1)S(1)}, bf16[240,1536]{1,0:T(8,128)(2,1)S(1)}, u32[]{:S(2)}, u32[]{:S(2)}) collective-permute-start(bf16[240,1536]{1,0:T(8,128)(2,1)S(1)} %pad_maximum_fusion.15), channel_id=1, source_target_pairs={{0,1},{1,0},{2,3},{3,2},{4,5},{5,4},{6,7},{7,6},{8,9},{9,8},{10,11... | collective-permute-start | bytes 2211848 | tf_op jit(solution)/shard_map/ppermute | solution.py:227
  153.9 9.1 %collective-permute-start.32 = (bf16[120,1536]{1,0:T(8,128)(2,1)S(1)}, bf16[120,1536]{1,0:T(8,128)(2,1)S(1)}, u32[]{:S(2)}, u32[]{:S(2)}) collective-permute-start(bf16[120,1536]{1,0:T(8,128)(2,1)S(1)} %multiply_convert_fusion), channel_id=1, source_target_pairs={{0,2},{1,3},{2,0},{3,1},{4,6},{5,7},{6,4},{7,5},{8,10},{9,11},{10,... | collective-permute-start | bytes 1105928 | tf_op jit(solution)/shard_map/ppermute | solution.py:227
  154.5 34.2 %collective-permute-start.17 = (bf16[240,1536]{1,0:T(8,128)(2,1)S(1)}, bf16[240,1536]{1,0:T(8,128)(2,1)S(1)}, u32[]{:S(2)}, u32[]{:S(2)}) collective-permute-start(bf16[240,1536]{1,0:T(8,128)(2,1)S(1)} %pad_maximum_fusion.13), channel_id=1, source_target_pairs={{0,1},{1,0},{2,3},{3,2},{4,5},{5,4},{6,7},{7,6},{8,9},{9,8},{10,11... | collective-permute-start | bytes 2211848 | tf_op jit(solution)/shard_map/ppermute | solution.py:227
  163.0 10.7 %collective-permute-start.22 = (bf16[120,1536]{1,0:T(8,128)(2,1)S(1)}, bf16[120,1536]{1,0:T(8,128)(2,1)S(1)}, u32[]{:S(2)}, u32[]{:S(2)}) collective-permute-start(bf16[120,1536]{1,0:T(8,128)(2,1)S(1)} %multiply_convert_fusion), channel_id=1, source_target_pairs={{0,12},{4,0},{8,4},{12,8},{1,13},{5,1},{9,5},{13,9},{2,14},{6,2},{... | collective-permute-start | bytes 1105928 | tf_op jit(solution)/shard_map/ppermute | solution.py:223
  164.7 23.9 %collective-permute-start.12 = (bf16[120,1536]{1,0:T(8,128)(2,1)S(1)}, bf16[120,1536]{1,0:T(8,128)(2,1)S(1)}, u32[]{:S(2)}, u32[]{:S(2)}) collective-permute-start(bf16[120,1536]{1,0:T(8,128)(2,1)S(1)} %multiply_convert_fusion), channel_id=1, source_target_pairs={{0,8},{4,12},{8,0},{12,4},{1,9},{5,13},{9,1},{13,5},{2,10},{6,14},... | collective-permute-start | bytes 1105928 | tf_op jit(solution)/shard_map/ppermute | solution.py:223
  173.7 28.6 %collective-permute-start.7 = (bf16[240,1536]{1,0:T(8,128)(2,1)S(1)}, bf16[240,1536]{1,0:T(8,128)(2,1)S(1)}, u32[]{:S(2)}, u32[]{:S(2)}) collective-permute-start(bf16[240,1536]{1,0:T(8,128)(2,1)S(1)} %pad_maximum_fusion.11), channel_id=1, source_target_pairs={{0,1},{1,0},{2,3},{3,2},{4,5},{5,4},{6,7},{7,6},{8,9},{9,8},{10,11... | collective-permute-start | bytes 2211848 | tf_op jit(solution)/shard_map/ppermute | solution.py:227
  188.6 13.2 %collective-permute-start.2 = (bf16[120,1536]{1,0:T(8,128)(2,1)S(1)}, bf16[120,1536]{1,0:T(8,128)(2,1)S(1)}, u32[]{:S(2)}, u32[]{:S(2)}) collective-permute-start(bf16[120,1536]{1,0:T(8,128)(2,1)S(1)} %multiply_convert_fusion), channel_id=1, source_target_pairs={{0,4},{4,8},{8,12},{12,0},{1,5},{5,9},{9,13},{13,1},{2,6},{6,10},{... | collective-permute-start | bytes 1105928 | tf_op jit(solution)/shard_map/ppermute | solution.py:223
  188.7 114.7 %collective-permute-start.28 = (f32[480,10]{1,0:T(8,128)S(1)}, f32[480,10]{1,0:T(8,128)S(1)}, u32[]{:S(2)}, u32[]{:S(2)}) collective-permute-start(f32[480,10]{1,0:T(8,128)S(1)} %copy-done.64), channel_id=1, source_target_pairs={{0,12},{4,0},{8,4},{12,8},{1,13},{5,1},{9,5},{13,9},{2,14},{6,2},{... | collective-permute-start | bytes 57608 | tf_op jit(solution)/shard_map/ppermute | solution.py:223
  201.8 11.5 %collective-permute-start.23 = (bf16[120,1536]{1,0:T(8,128)(2,1)S(1)}, bf16[120,1536]{1,0:T(8,128)(2,1)S(1)}, u32[]{:S(2)}, u32[]{:S(2)}) collective-permute-start(bf16[120,1536]{1,0:T(8,128)(2,1)S(1)} %collective-permute-done.22), channel_id=1, source_target_pairs={{0,2},{1,3},{2,0},{3,1},{4,6},{5,7},{6,4},{7,5},{8,10},{9,11},{10,... | collective-permute-start | bytes 1105928 | tf_op jit(solution)/shard_map/ppermute | solution.py:227
  202.3 16.4 %collective-permute-start.13 = (bf16[120,1536]{1,0:T(8,128)(2,1)S(1)}, bf16[120,1536]{1,0:T(8,128)(2,1)S(1)}, u32[]{:S(2)}, u32[]{:S(2)}) collective-permute-start(bf16[120,1536]{1,0:T(8,128)(2,1)S(1)} %collective-permute-done.12), channel_id=1, source_target_pairs={{0,2},{1,3},{2,0},{3,1},{4,6},{5,7},{6,4},{7,5},{8,10},{9,11},{10,... | collective-permute-start | bytes 1105928 | tf_op jit(solution)/shard_map/ppermute | solution.py:227
  213.3 9.4 %collective-permute-start.3 = (bf16[120,1536]{1,0:T(8,128)(2,1)S(1)}, bf16[120,1536]{1,0:T(8,128)(2,1)S(1)}, u32[]{:S(2)}, u32[]{:S(2)}) collective-permute-start(bf16[120,1536]{1,0:T(8,128)(2,1)S(1)} %collective-permute-done.2), channel_id=1, source_target_pairs={{0,2},{1,3},{2,0},{3,1},{4,6},{5,7},{6,4},{7,5},{8,10},{9,11},{10,... | collective-permute-start | bytes 1105928 | tf_op jit(solution)/shard_map/ppermute | solution.py:227
  222.7 78.0 %collective-permute-start.24 = (bf16[240,1536]{1,0:T(8,128)(2,1)}, bf16[240,1536]{1,0:T(8,128)(2,1)}, u32[]{:S(2)}, u32[]{:S(2)}) collective-permute-start(bf16[240,1536]{1,0:T(8,128)(2,1)} %pad_maximum_fusion.14), channel_id=1, source_target_pairs={{0,1},{1,0},{2,3},{3,2},{4,5},{5,4},{6,7},{7,6},{8,9},{9,8},{10,11... | collective-permute-start | bytes 2211848 | tf_op jit(solution)/shard_map/ppermute | solution.py:227
  222.9 28.3 %collective-permute-start.4 = (bf16[240,1536]{1,0:T(8,128)(2,1)S(1)}, bf16[240,1536]{1,0:T(8,128)(2,1)}, u32[]{:S(2)}, u32[]{:S(2)}) collective-permute-start(bf16[240,1536]{1,0:T(8,128)(2,1)S(1)} %pad_maximum_fusion.10), channel_id=1, source_target_pairs={{0,1},{1,0},{2,3},{3,2},{4,5},{5,4},{6,7},{7,6},{8,9},{9,8},{10,11... | collective-permute-start | bytes 2211848 | tf_op jit(solution)/shard_map/ppermute | solution.py:227
  251.2 25.8 %collective-permute-start.14 = (bf16[240,1536]{1,0:T(8,128)(2,1)S(1)}, bf16[240,1536]{1,0:T(8,128)(2,1)S(1)}, u32[]{:S(2)}, u32[]{:S(2)}) collective-permute-start(bf16[240,1536]{1,0:T(8,128)(2,1)S(1)} %pad_maximum_fusion.12), channel_id=1, source_target_pairs={{0,1},{1,0},{2,3},{3,2},{4,5},{5,4},{6,7},{7,6},{8,9},{9,8},{10,11... | collective-permute-start | bytes 2211848 | tf_op jit(solution)/shard_map/ppermute | solution.py:227
  252.4 115.6 %collective-permute-start.49 = (bf16[240,1536]{1,0:T(8,128)(2,1)}, bf16[240,1536]{1,0:T(8,128)(2,1)}, u32[]{:S(2)}, u32[]{:S(2)}) collective-permute-start(bf16[240,1536]{1,0:T(8,128)(2,1)} %slice.194), channel_id=1, source_target_pairs={{0,1},{1,0},{2,3},{3,2},{4,5},{5,4},{6,7},{7,6},{8,9},{9,8},{10,11... | collective-permute-start | bytes 2211848 | tf_op jit(solution)/shard_map/ppermute | solution.py:227
  277.0 92.8 %collective-permute-start.36 = (bf16[240,1536]{1,0:T(8,128)(2,1)}, bf16[240,1536]{1,0:T(8,128)(2,1)}, u32[]{:S(2)}, u32[]{:S(2)}) collective-permute-start(bf16[240,1536]{1,0:T(8,128)(2,1)} %slice.226), channel_id=1, source_target_pairs={{0,1},{1,0},{2,3},{3,2},{4,5},{5,4},{6,7},{7,6},{8,9},{9,8},{10,11... | collective-permute-start | bytes 2211848 | tf_op jit(solution)/shard_map/ppermute | solution.py:227
  281.3 91.2 %collective-permute-start.40 = (bf16[240,1536]{1,0:T(8,128)(2,1)}, bf16[240,1536]{1,0:T(8,128)(2,1)}, u32[]{:S(2)}, u32[]{:S(2)}) collective-permute-start(bf16[240,1536]{1,0:T(8,128)(2,1)} %slice.182), channel_id=1, source_target_pairs={{0,1},{1,0},{2,3},{3,2},{4,5},{5,4},{6,7},{7,6},{8,9},{9,8},{10,11... | collective-permute-start | bytes 2211848 | tf_op jit(solution)/shard_map/ppermute | solution.py:227
  300.7 109.6 %collective-permute-start.9 = (bf16[240,1536]{1,0:T(8,128)(2,1)}, bf16[240,1536]{1,0:T(8,128)(2,1)}, u32[]{:S(2)}, u32[]{:S(2)}) collective-permute-start(bf16[240,1536]{1,0:T(8,128)(2,1)} %slice.214), channel_id=1, source_target_pairs={{0,1},{1,0},{2,3},{3,2},{4,5},{5,4},{6,7},{7,6},{8,9},{9,8},{10,11... | collective-permute-start | bytes 2211848 | tf_op jit(solution)/shard_map/ppermute | solution.py:227
  303.3 71.0 %collective-permute-start.43 = (bf16[240,1536]{1,0:T(8,128)(2,1)}, bf16[240,1536]{1,0:T(8,128)(2,1)}, u32[]{:S(2)}, u32[]{:S(2)}) collective-permute-start(bf16[240,1536]{1,0:T(8,128)(2,1)} %slice.186), channel_id=1, source_target_pairs={{0,1},{1,0},{2,3},{3,2},{4,5},{5,4},{6,7},{7,6},{8,9},{9,8},{10,11... | collective-permute-start | bytes 2211848 | tf_op jit(solution)/shard_map/ppermute | solution.py:227
  367.9 71.3 %collective-permute-start.19 = (bf16[240,1536]{1,0:T(8,128)(2,1)}, bf16[240,1536]{1,0:T(8,128)(2,1)S(1)}, u32[]{:S(2)}, u32[]{:S(2)}) collective-permute-start(bf16[240,1536]{1,0:T(8,128)(2,1)} %slice.218), channel_id=1, source_target_pairs={{0,1},{1,0},{2,3},{3,2},{4,5},{5,4},{6,7},{7,6},{8,9},{9,8},{10,11... | collective-permute-start | bytes 2211848 | tf_op jit(solution)/shard_map/ppermute | solution.py:227
  369.8 7.5 collective-permute-start.46
  372.5 45.3 %collective-permute-start.50 = (bf16[120,1536]{1,0:T(8,128)(2,1)S(1)}, bf16[120,1536]{1,0:T(8,128)(2,1)S(1)}, u32[]{:S(2)}, u32[]{:S(2)}) collective-permute-start(bf16[120,1536]{1,0:T(8,128)(2,1)S(1)} %slice.236), channel_id=1, source_target_pairs={{0,2},{1,3},{2,0},{3,1},{4,6},{5,7},{6,4},{7,5},{8,10},{9,11},{10,... | collective-permute-start | bytes 1105928 | tf_op jit(solution)/shard_map/ppermute | solution.py:227
  374.4 17.5 %collective-permute-start.41 = (bf16[120,1536]{1,0:T(8,128)(2,1)S(1)}, bf16[120,1536]{1,0:T(8,128)(2,1)S(1)}, u32[]{:S(2)}, u32[]{:S(2)}) collective-permute-start(bf16[120,1536]{1,0:T(8,128)(2,1)S(1)} %slice.230), channel_id=1, source_target_pairs={{0,2},{1,3},{2,0},{3,1},{4,6},{5,7},{6,4},{7,5},{8,10},{9,11},{10,... | collective-permute-start | bytes 1105928 | tf_op jit(solution)/shard_map/ppermute | solution.py:227
  377.3 22.4 %collective-permute-start.44 = (bf16[120,1536]{1,0:T(8,128)(2,1)S(1)}, bf16[120,1536]{1,0:T(8,128)(2,1)S(1)}, u32[]{:S(2)}, u32[]{:S(2)}) collective-permute-start(bf16[120,1536]{1,0:T(8,128)(2,1)S(1)} %slice.232), channel_id=1, source_target_pairs={{0,2},{1,3},{2,0},{3,1},{4,6},{5,7},{6,4},{7,5},{8,10},{9,11},{10,... | collective-permute-start | bytes 1105928 | tf_op jit(solution)/shard_map/ppermute | solution.py:227
  391.8 17.0 %collective-permute-start.47 = (bf16[120,1536]{1,0:T(8,128)(2,1)S(1)}, bf16[120,1536]{1,0:T(8,128)(2,1)S(1)}, u32[]{:S(2)}, u32[]{:S(2)}) collective-permute-start(bf16[120,1536]{1,0:T(8,128)(2,1)S(1)} %slice.234), channel_id=1, source_target_pairs={{0,2},{1,3},{2,0},{3,1},{4,6},{5,7},{6,4},{7,5},{8,10},{9,11},{10,... | collective-permute-start | bytes 1105928 | tf_op jit(solution)/shard_map/ppermute | solution.py:227
  399.7 18.1 %collective-permute-start.42 = (bf16[120,1536]{1,0:T(8,128)(2,1)S(1)}, bf16[120,1536]{1,0:T(8,128)(2,1)S(1)}, u32[]{:S(2)}, u32[]{:S(2)}) collective-permute-start(bf16[120,1536]{1,0:T(8,128)(2,1)S(1)} %add_convert_fusion.15), channel_id=1, source_target_pairs={{0,12},{4,0},{8,4},{12,8},{1,13},{5,1},{9,5},{13,9},{2,14},{6,2},{... | collective-permute-start | bytes 1105928 | tf_op jit(solution)/shard_map/ppermute | solution.py:223
  408.9 25.5 %collective-permute-start.45 = (bf16[120,1536]{1,0:T(8,128)(2,1)S(1)}, bf16[120,1536]{1,0:T(8,128)(2,1)S(1)}, u32[]{:S(2)}, u32[]{:S(2)}) collective-permute-start(bf16[120,1536]{1,0:T(8,128)(2,1)S(1)} %add_convert_fusion.14), channel_id=1, source_target_pairs={{0,8},{4,12},{8,0},{12,4},{1,9},{5,13},{9,1},{13,5},{2,10},{6,14},... | collective-permute-start | bytes 1105928 | tf_op jit(solution)/shard_map/ppermute | solution.py:223
  410.4 25.6 %collective-permute-start.48 = (bf16[120,1536]{1,0:T(8,128)(2,1)S(1)}, bf16[120,1536]{1,0:T(8,128)(2,1)S(1)}, u32[]{:S(2)}, u32[]{:S(2)}) collective-permute-start(bf16[120,1536]{1,0:T(8,128)(2,1)S(1)} %add_convert_fusion.13), channel_id=1, source_target_pairs={{0,4},{4,8},{8,12},{12,0},{1,5},{5,9},{9,13},{13,1},{2,6},{6,10},{... | collective-permute-start | bytes 1105928 | tf_op jit(solution)/shard_map/ppermute | solution.py:223
  417.8 35.4 %collective-permute-start.29 = (bf16[240,1536]{1,0:T(8,128)(2,1)S(1)}, bf16[240,1536]{1,0:T(8,128)(2,1)S(1)}, u32[]{:S(2)}, u32[]{:S(2)}) collective-permute-start(bf16[240,1536]{1,0:T(8,128)(2,1)S(1)} %copy-done.51), channel_id=1, source_target_pairs={{0,1},{1,0},{2,3},{3,2},{4,5},{5,4},{6,7},{7,6},{8,9},{9,8},{10,11... | collective-permute-start | bytes 2211848 | tf_op jit(solution)/shard_map/ppermute | solution.py:227
  417.9 285.4 %collective-permute-start.63 = (bf16[10,128,1536]{2,1,0:T(8,128)(2,1)}, bf16[10,128,1536]{2,1,0:T(8,128)(2,1)}, u32[]{:S(2)}, u32[]{:S(2)}) collective-permute-start(bf16[10,128,1536]{2,1,0:T(8,128)(2,1)} %get-tuple-element.36), channel_id=1, source_target_pairs={{0,16},{16,0},{1,17},{17,1},{2,18},{18,2},{3,19},{19,3},{4,20},{20... | collective-permute-start | bytes 11796488 | tf_op jit(solution)/shard_map/ppermute | solution.py:223
  434.4 305.7 %collective-permute-start.62 = (bf16[10,1536,256]{2,1,0:T(8,128)(2,1)}, bf16[10,1536,256]{2,1,0:T(8,128)(2,1)}, u32[]{:S(2)}, u32[]{:S(2)}) collective-permute-start(bf16[10,1536,256]{2,1,0:T(8,128)(2,1)} %get-tuple-element.35), channel_id=1, source_target_pairs={{0,16},{16,0},{1,17},{17,1},{2,18},{18,2},{3,19},{19,3},{4,20},{20... | collective-permute-start | bytes 23592968 | tf_op jit(solution)/shard_map/ppermute | solution.py:223
  435.9 142.1 %collective-permute-start.37 = (bf16[120,1536]{1,0:T(8,128)(2,1)}, bf16[120,1536]{1,0:T(8,128)(2,1)}, u32[]{:S(2)}, u32[]{:S(2)}) collective-permute-start(bf16[120,1536]{1,0:T(8,128)(2,1)} %slice.228), channel_id=1, source_target_pairs={{0,2},{1,3},{2,0},{3,1},{4,6},{5,7},{6,4},{7,5},{8,10},{9,11},{10,... | collective-permute-start | bytes 1105928 | tf_op jit(solution)/shard_map/ppermute | solution.py:227
  439.2 13.5 %collective-permute-start.51 = (bf16[120,1536]{1,0:T(8,128)(2,1)S(1)}, bf16[120,1536]{1,0:T(8,128)(2,1)S(1)}, u32[]{:S(2)}, u32[]{:S(2)}) collective-permute-start(bf16[120,1536]{1,0:T(8,128)(2,1)S(1)} %fusion.55), channel_id=1, source_target_pairs={{0,2},{1,3},{2,0},{3,1},{4,6},{5,7},{6,4},{7,5},{8,10},{9,11},{10,... | collective-permute-start | bytes 1105928 | tf_op jit(solution)/shard_map/ppermute | solution.py:227
  452.7 9.3 %collective-permute-start.10 = (bf16[120,1536]{1,0:T(8,128)(2,1)S(1)}, bf16[120,1536]{1,0:T(8,128)(2,1)S(1)}, u32[]{:S(2)}, u32[]{:S(2)}) collective-permute-start(bf16[120,1536]{1,0:T(8,128)(2,1)S(1)} %slice.216), channel_id=1, source_target_pairs={{0,2},{1,3},{2,0},{3,1},{4,6},{5,7},{6,4},{7,5},{8,10},{9,11},{10,... | collective-permute-start | bytes 1105928 | tf_op jit(solution)/shard_map/ppermute | solution.py:227
  453.2 9.6 %collective-permute-start.52 = (bf16[240,1536]{1,0:T(8,128)(2,1)S(1)}, bf16[240,1536]{1,0:T(8,128)(2,1)S(1)}, u32[]{:S(2)}, u32[]{:S(2)}) collective-permute-start(bf16[240,1536]{1,0:T(8,128)(2,1)S(1)} %pad_maximum_fusion.19), channel_id=1, source_target_pairs={{0,1},{1,0},{2,3},{3,2},{4,5},{5,4},{6,7},{7,6},{8,9},{9,8},{10,11... | collective-permute-start | bytes 2211848 | tf_op jit(solution)/shard_map/ppermute | solution.py:227
  462.0 56.4 %collective-permute-start.20 = (bf16[120,1536]{1,0:T(8,128)(2,1)}, bf16[120,1536]{1,0:T(8,128)(2,1)}, u32[]{:S(2)}, u32[]{:S(2)}) collective-permute-start(bf16[120,1536]{1,0:T(8,128)(2,1)} %slice.220), channel_id=1, source_target_pairs={{0,2},{1,3},{2,0},{3,1},{4,6},{5,7},{6,4},{7,5},{8,10},{9,11},{10,... | collective-permute-start | bytes 1105928 | tf_op jit(solution)/shard_map/ppermute | solution.py:227
  462.8 95.1 %collective-permute-start.30 = (bf16[120,1536]{1,0:T(8,128)(2,1)}, bf16[120,1536]{1,0:T(8,128)(2,1)}, u32[]{:S(2)}, u32[]{:S(2)}) collective-permute-start(bf16[120,1536]{1,0:T(8,128)(2,1)} %slice.224), channel_id=1, source_target_pairs={{0,2},{1,3},{2,0},{3,1},{4,6},{5,7},{6,4},{7,5},{8,10},{9,11},{10,... | collective-permute-start | bytes 1105928 | tf_op jit(solution)/shard_map/ppermute | solution.py:227
  518.3 215.4 %all-reduce.7.cloned.1.call-start = ((), (), s32[]{:S(2)}) async-start(), calls=%async_computation.2 | async-start | bytes 6291456 | tf_op jit(solution)/shard_map/psum | solution.py:488
  518.4 61.4 %collective-permute-start.11 = (bf16[120,1536]{1,0:T(8,128)(2,1)}, bf16[120,1536]{1,0:T(8,128)(2,1)}, u32[]{:S(2)}, u32[]{:S(2)}) collective-permute-start(bf16[120,1536]{1,0:T(8,128)(2,1)} %add_convert_fusion.20), channel_id=1, source_target_pairs={{0,12},{4,0},{8,4},{12,8},{1,13},{5,1},{9,5},{13,9},{2,14},{6,2},{... | collective-permute-start | bytes 1105928 | tf_op jit(solution)/shard_map/ppermute | solution.py:223
  557.9 5.7 collective-permute-start.53
  565.5 10.9 %collective-permute-start.54 = (bf16[120,1536]{1,0:T(8,128)(2,1)}, bf16[120,1536]{1,0:T(8,128)(2,1)}, u32[]{:S(2)}, u32[]{:S(2)}) collective-permute-start(bf16[120,1536]{1,0:T(8,128)(2,1)} %slice.240), channel_id=1, source_target_pairs={{0,2},{1,3},{2,0},{3,1},{4,6},{5,7},{6,4},{7,5},{8,10},{9,11},{10,... | collective-permute-start | bytes 1105928 | tf_op jit(solution)/shard_map/ppermute | solution.py:227
  578.1 50.3 %collective-permute-start.21 = (bf16[120,1536]{1,0:T(8,128)(2,1)S(1)}, bf16[120,1536]{1,0:T(8,128)(2,1)S(1)}, u32[]{:S(2)}, u32[]{:S(2)}) collective-permute-start(bf16[120,1536]{1,0:T(8,128)(2,1)S(1)} %copy-done.63), channel_id=1, source_target_pairs={{0,8},{4,12},{8,0},{12,4},{1,9},{5,13},{9,1},{13,5},{2,10},{6,14},... | collective-permute-start | bytes 1105928 | tf_op jit(solution)/shard_map/ppermute | solution.py:223
  579.4 49.0 %collective-permute-start.31 = (bf16[120,1536]{1,0:T(8,128)(2,1)}, bf16[120,1536]{1,0:T(8,128)(2,1)S(1)}, u32[]{:S(2)}, u32[]{:S(2)}) collective-permute-start(bf16[120,1536]{1,0:T(8,128)(2,1)} %add_convert_fusion.18), channel_id=1, source_target_pairs={{0,4},{4,8},{8,12},{12,0},{1,5},{5,9},{9,13},{13,1},{2,6},{6,10},{... | collective-permute-start | bytes 1105928 | tf_op jit(solution)/shard_map/ppermute | solution.py:223
  579.8 53.1 %collective-permute-start.58 = (f32[2,1536]{1,0:T(2,128)S(1)}, f32[2,1536]{1,0:T(2,128)S(1)}, u32[]{:S(2)}, u32[]{:S(2)}) collective-permute-start(f32[2,1536]{1,0:T(2,128)S(1)} %fusion.54), channel_id=1, source_target_pairs={{0,2},{1,3},{2,0},{3,1},{4,6},{5,7},{6,4},{7,5},{8,10},{9,11},{10,... | collective-permute-start | bytes 36872 | tf_op jit(solution)/shard_map/ppermute | solution.py:227
  630.8 71.8 %collective-permute-start.55 = (bf16[120,1536]{1,0:T(8,128)(2,1)S(1)}, bf16[120,1536]{1,0:T(8,128)(2,1)S(1)}, u32[]{:S(2)}, u32[]{:S(2)}) collective-permute-start(bf16[120,1536]{1,0:T(8,128)(2,1)S(1)} %get-tuple-element.52), channel_id=1, source_target_pairs={{0,2},{1,3},{2,0},{3,1},{4,6},{5,7},{6,4},{7,5},{8,10},{9,11},{10,... | collective-permute-start | bytes 1105928 | tf_op jit(solution)/shard_map/ppermute | solution.py:227
  631.6 71.1 %collective-permute-start.38 = (bf16[120,1536]{1,0:T(8,128)(2,1)S(1)}, bf16[120,1536]{1,0:T(8,128)(2,1)S(1)}, u32[]{:S(2)}, u32[]{:S(2)}) collective-permute-start(bf16[120,1536]{1,0:T(8,128)(2,1)S(1)} %get-tuple-element.53), channel_id=1, source_target_pairs={{0,2},{1,3},{2,0},{3,1},{4,6},{5,7},{6,4},{7,5},{8,10},{9,11},{10,... | collective-permute-start | bytes 1105928 | tf_op jit(solution)/shard_map/ppermute | solution.py:227
  632.9 64.6 %collective-permute-start.59 = (f32[2,1536]{1,0:T(2,128)S(1)}, f32[2,1536]{1,0:T(2,128)S(1)}, u32[]{:S(2)}, u32[]{:S(2)}) collective-permute-start(f32[2,1536]{1,0:T(2,128)S(1)} %fusion.89), channel_id=1, source_target_pairs={{0,16},{16,0},{1,17},{17,1},{2,18},{18,2},{3,19},{19,3},{4,20},{20... | collective-permute-start | bytes 36872 | tf_op jit(solution)/shard_map/ppermute | solution.py:227
  697.5 5.0 collective-permute-start.60
  702.5 8.7 %collective-permute-start.61 = (f32[2,1536]{1,0:T(2,128)S(1)}, f32[2,1536]{1,0:T(2,128)S(1)}, u32[]{:S(2)}, u32[]{:S(2)}) collective-permute-start(f32[2,1536]{1,0:T(2,128)S(1)} %add.374), channel_id=1, source_target_pairs={{0,8},{4,12},{8,0},{12,4},{1,9},{5,13},{9,1},{13,5},{2,10},{6,14},... | collective-permute-start | bytes 36872 | tf_op jit(solution)/shard_map/ppermute | solution.py:227
  702.6 9.2 %collective-permute-start.56 = (bf16[240,1536]{1,0:T(8,128)(2,1)S(1)}, bf16[240,1536]{1,0:T(8,128)(2,1)S(1)}, u32[]{:S(2)}, u32[]{:S(2)}) collective-permute-start(bf16[240,1536]{1,0:T(8,128)(2,1)S(1)} %pad_maximum_fusion.21), channel_id=1, source_target_pairs={{0,1},{1,0},{2,3},{3,2},{4,5},{5,4},{6,7},{7,6},{8,9},{9,8},{10,11... | collective-permute-start | bytes 2211848 | tf_op jit(solution)/shard_map/ppermute | solution.py:227
  702.7 9.1 %collective-permute-start.39 = (bf16[240,1536]{1,0:T(8,128)(2,1)S(1)}, bf16[240,1536]{1,0:T(8,128)(2,1)S(1)}, u32[]{:S(2)}, u32[]{:S(2)}) collective-permute-start(bf16[240,1536]{1,0:T(8,128)(2,1)S(1)} %pad_maximum_fusion.18), channel_id=1, source_target_pairs={{0,1},{1,0},{2,3},{3,2},{4,5},{5,4},{6,7},{7,6},{8,9},{9,8},{10,11... | collective-permute-start | bytes 2211848 | tf_op jit(solution)/shard_map/ppermute | solution.py:227
  (88 other events, 1234.6 us)
Sparse Core Ops, SparseCore 0:
  518.5 33.5 reduce-scatter.3
  570.0 163.6 all-reduce.6

commit v2 on v0

v2 whole, which is shorter than its diff:
```python
import functools
import math

import jax
import jax.numpy as jnp
import numpy as np
from jax import lax
from jax.experimental import pallas as pl
from jax.experimental.pallas import tpu as pltpu
from jax.sharding import PartitionSpec as P

HEAD_SIZE = 64
PAIR = 64
BF = jnp.bfloat16
F32 = jnp.float32
EPS = 1e-05


def normalize(values, gain_vector):
    inverse_rms = lax.rsqrt(jnp.mean(values * values, axis=-1, keepdims=True) + EPS)
    return values * inverse_rms * gain_vector


SMEM = pl.BlockSpec(memory_space=pltpu.SMEM)
VMEM = pl.BlockSpec(memory_space=pltpu.VMEM)
CHEAP = pl.CostEstimate(flops=1000, bytes_accessed=1000, transcendentals=0)


def roomy(mebibytes):
    return pltpu.CompilerParams(vmem_limit_bytes=mebibytes << 20)


def dot_nn(a, b):
    return lax.dot_general(a, b, (((1,), (0,)), ((), ())), preferred_element_type=F32)


def dot_nt(a, b):
    return lax.dot_general(a, b, (((1,), (1,)), ((), ())), preferred_element_type=F32)


def dot_tn(a, b):
    return lax.dot_general(a, b, (((0,), (0,)), ((), ())), preferred_element_type=F32)


def split_columns(w):
    low = lax.broadcasted_iota(jnp.int32, w.shape[:1] + (128,), 1) < PAIR
    gates, ups = [], []
    for i in range(w.shape[1] // 256):
        a = w[:, 256 * i : 256 * i + 128]
        b = w[:, 256 * i + 128 : 256 * i + 256]
        gates.append(jnp.where(low, a, pltpu.roll(b, PAIR, 1)))
        ups.append(jnp.where(low, pltpu.roll(a, PAIR, 1), b))
    return gates, ups


def join_columns(gate, up):
    low = lax.broadcasted_iota(jnp.int32, gate.shape[:1] + (128,), 1) < PAIR
    out = []
    for i in range(gate.shape[1] // 128):
        g = gate[:, 128 * i : 128 * i + 128]
        u = up[:, 128 * i : 128 * i + 128]
        out.append(jnp.where(low, g, pltpu.roll(u, PAIR, 1)))
        out.append(jnp.where(low, pltpu.roll(g, PAIR, 1), u))
    return jnp.concatenate(out, axis=1)


def expert_step(
    first, all_experts, x_ref, c_ref, g_ref, w1_ref, w2_ref, ga_ref, hg_ref, acc_ref
):
    per, width, columns = w1_ref.shape
    units = columns // 2
    gates, ups = [], []
    for e in range(per):
        g, u = split_columns(w1_ref[e])
        gates += g
        ups += u
    w1 = jnp.concatenate(gates + ups, axis=1)
    w2 = w2_ref[...].reshape(per * units, width)
    half = x_ref.shape[0] // 2
    parts = [slice(0, half), slice(half, 2 * half)]
    fronts = [(dot_nn(x_ref[s], w1), dot_nt(c_ref[s], w2)) for s in parts]
    for s, (hidden, pull) in zip(parts, fronts):
        weights = g_ref[s].astype(F32)
        lane = lax.broadcasted_iota(jnp.int32, weights.shape, 1)
        route = []
        for e in range(per):
            mine = (lane == first + e) | (lane == first + e + all_experts)
            weight = jnp.sum(jnp.where(mine, weights, 0.0), axis=1, keepdims=True)
            route.append(jnp.broadcast_to(weight, (half, units)))
        route = jnp.concatenate(route, axis=1)
        gate = hidden[:, : per * units]
        up = hidden[:, per * units :]
        sig = 1.0 / (1.0 + jnp.exp(-gate))
        silu = gate * sig
        pull = pull * route
        activation = (silu * up * route).astype(BF)
        ga_ref[s] = activation
        gate_grad = (pull * up * (sig * (1.0 + gate - silu))).astype(BF)
        up_grad = (pull * silu).astype(BF)
        hg_ref[s] = join_columns(gate_grad, up_grad)
        if acc_ref is not None:
            acc_ref[s] += dot_nt(jnp.concatenate([gate_grad, up_grad], axis=1), w1)


def main_kernel(
    all_experts, place_ref, x_ref, c_ref, g_ref, w1_ref, w2_ref, ga_ref, hg_ref, kept_ref,
    sent_ref, acc_ref,
):
    step = pl.program_id(0)

    @pl.when(step == 0)
    def _():
        acc_ref[...] = jnp.zeros_like(acc_ref)

    first = place_ref[1] + step * w1_ref.shape[0]
    expert_step(first, all_experts, x_ref, c_ref, g_ref, w1_ref, w2_ref, ga_ref, hg_ref, acc_ref)

    @pl.when(step == pl.num_programs(0) - 1)
    def _():
        write_halves(acc_ref, place_ref[2], kept_ref, sent_ref)


def other_kernel(all_experts, place_ref, x_ref, c_ref, g_ref, w1_ref, w2_ref, ga_ref, hg_ref):
    first = place_ref[1] + place_ref[3] * w1_ref.shape[0]
    expert_step(first, all_experts, x_ref, c_ref, g_ref, w1_ref, w2_ref, ga_ref, hg_ref, None)


class Rows:
    def __init__(self, array, index=None):
        self.array, self.index = array, index

    def spec(self, rows, width, column=0):
        index = self.index
        return pl.BlockSpec(
            (rows, width),
            lambda i, place: (place[0] if index is None else index, column),
            pipeline_mode=pl.Buffered(1),
        )


def experts_main(place, x, c, g, g_column, w1, w2, rows, all_experts, part):
    experts, width, columns = w1.shape
    units = columns // 2
    per = 2
    half = (rows // (2 * part), part, width)
    return pl.pallas_call(
        functools.partial(main_kernel, all_experts),
        grid_spec=pltpu.PrefetchScalarGridSpec(
            num_scalar_prefetch=1,
            grid=(experts // per,),
            in_specs=[
                x.spec(rows, width),
                c.spec(rows, width),
                g.spec(rows, 128, g_column),
                pl.BlockSpec((per, width, columns), lambda i, p: (i, 0, 0)),
                pl.BlockSpec((per, units, width), lambda i, p: (i, 0, 0)),
            ],
            out_specs=[
                pl.BlockSpec((rows, per * units), lambda i, p: (0, i)),
                pl.BlockSpec((rows, per * columns), lambda i, p: (0, i)),
                pl.BlockSpec(half, lambda i, p: (0, 0, 0)),
                pl.BlockSpec(half, lambda i, p: (0, 0, 0)),
            ],
            scratch_shapes=[pltpu.VMEM((rows, width), F32)],
        ),
        out_shape=[
            jax.ShapeDtypeStruct((rows, experts * units), BF),
            jax.ShapeDtypeStruct((rows, experts * columns), BF),
            jax.ShapeDtypeStruct(half, BF),
            jax.ShapeDtypeStruct(half, BF),
        ],
        compiler_params=roomy(48),
        cost_estimate=CHEAP,
        name="experts_main",
    )(place, x.array, c.array, g.array, w1, w2)


def experts_other(place, x, c, w1, w2, rows, all_experts):
    experts, width, columns = w1.shape
    units = columns // 2
    per = experts // 2
    groups = x.shape[0] // rows
    once = pl.Buffered(1)
    other = lambda i, p: (1 - p[3]) * groups + i
    return pl.pallas_call(
        functools.partial(other_kernel, all_experts),
        grid_spec=pltpu.PrefetchScalarGridSpec(
            num_scalar_prefetch=1,
            grid=(groups,),
            in_specs=[
                pl.BlockSpec((rows, width), lambda i, p: (i, 0)),
                pl.BlockSpec((rows, width), lambda i, p: (other(i, p), 0)),
                pl.BlockSpec((rows, 128), lambda i, p: (other(i, p), width // 128)),
                pl.BlockSpec((per, width, columns), lambda i, p: (p[3], 0, 0), pipeline_mode=once),
                pl.BlockSpec((per, units, width), lambda i, p: (p[3], 0, 0), pipeline_mode=once),
            ],
            out_specs=[
                pl.BlockSpec((rows, per * units), lambda i, p: (i, 0)),
                pl.BlockSpec((rows, per * columns), lambda i, p: (i, 0)),
            ],
        ),
        out_shape=[
            jax.ShapeDtypeStruct((groups * rows, per * units), BF),
            jax.ShapeDtypeStruct((groups * rows, per * columns), BF),
        ],
        compiler_params=roomy(60),
        cost_estimate=CHEAP,
        name="experts_other",
    )(place, x, c, c, w1, w2)


def weights_kernel(groups, count, half, first, place_ref, *refs):
    m = len(groups)
    xs, c_hbm, hgs, gas = refs[:m], refs[m], refs[m + 1 : 2 * m + 1], refs[2 * m + 1 : 3 * m + 1]
    out_ref, x_ref, c_ref, hg_ref, ga_ref, up_ref, down_ref, sems = refs[3 * m + 1 :]
    _, rows, width = x_ref.shape
    columns = out_ref.shape[2]
    units = columns // 2
    tree, zone = place_ref[3], place_ref[4]
    for k, (x_index, h_index, shift_by, total) in enumerate(groups):
        if shift_by is None:
            group = (1 - tree) * total + h_index
            expert = first
        else:
            group = tree * total + lax.rem(zone + total - shift_by, total)
            expert = tree * half + first
        c_rows = pl.ds(pl.multiple_of(group * rows, 32), rows)
        h_rows = pl.ds(h_index * rows, rows)
        for i, copy in enumerate(
            (
                (xs[k].at[pl.ds(x_index * rows, rows)], x_ref),
                (hgs[k].at[h_rows, pl.ds(pl.multiple_of(expert * columns, 128), count * columns)], hg_ref),
                (c_hbm.at[c_rows, pl.ds(0, width)], c_ref),
                (gas[k].at[h_rows, pl.ds(pl.multiple_of(expert * units, 128), count * units)], ga_ref),
            )
        ):
            pltpu.make_async_copy(copy[0], copy[1].at[k], sems.at[i, k]).start()
    up_ref[...] = jnp.zeros_like(up_ref)
    down_ref[...] = jnp.zeros_like(down_ref)

    def body(k, carry):
        for i, ref in enumerate((x_ref, hg_ref)):
            pltpu.make_async_copy(ref.at[k], ref.at[k], sems.at[i, k]).wait()
        up_ref[...] += dot_tn(x_ref[k], hg_ref[k])
        for i, ref in enumerate((c_ref, ga_ref)):
            pltpu.make_async_copy(ref.at[k], ref.at[k], sems.at[2 + i, k]).wait()
        down_ref[...] += dot_tn(ga_ref[k], c_ref[k])
        return carry

    lax.fori_loop(0, m, body, 0)
    for e in range(count):
        out_ref[e, :width] = up_ref[:, columns * e : columns * (e + 1)].astype(BF)
        for t in range(width // columns):
            out_ref[e, width + units * t : width + units * (t + 1)] = down_ref[
                units * e : units * (e + 1), columns * t : columns * t + columns
            ].astype(BF)


def experts_weights(place, groups, c, first, count, half, rows):
    width = groups[0][0].shape[1]
    units = 2 * PAIR
    columns = 2 * units
    m = len(groups)
    hbm = pl.BlockSpec(memory_space=pl.ANY)
    return pl.pallas_call(
        functools.partial(weights_kernel, [g[3:] for g in groups], count, half, first),
        in_specs=[SMEM] + [hbm] * (3 * m + 1),
        out_specs=VMEM,
        out_shape=jax.ShapeDtypeStruct((count, width + width // 2, columns), BF),
        scratch_shapes=[
            pltpu.VMEM((m, rows, width), BF),
            pltpu.VMEM((m, rows, width), BF),
            pltpu.VMEM((m, rows, count * columns), BF),
            pltpu.VMEM((m, rows, count * units), BF),
            pltpu.VMEM((width, count * columns), F32),
            pltpu.VMEM((count * units, width), F32),
            pltpu.SemaphoreType.DMA((4, m)),
        ],
        compiler_params=roomy(60),
        cost_estimate=CHEAP,
        name="experts_weights",
    )(place, *[g[0] for g in groups], c, *[g[1] for g in groups], *[g[2] for g in groups])


def finish_kernel(source, *refs):
    o1_ref, o2_ref = refs[-2:]
    width, columns = o1_ref.shape[1:]
    units = o2_ref.shape[1]
    stored = source.shape[2]
    total = source[0].astype(F32)
    o1_ref[0] = total[:width, :columns]
    for t in range(width // stored):
        rows = total[width + stored // 2 * t : width + stored // 2 * (t + 1)]
        o2_ref[0, :, stored * t : stored * (t + 1)] = rows[:units]


def finish_weights(grads, before, first, half, up_shape, down_shape):
    extra = [] if before is None else list(before)
    count = grads.shape[0] // 2
    if 2 * half > up_shape[0] and first + count == half:
        steps = 2 * count - 1
    else:
        steps = 2 * count
    place = lambda i: (i // count) * half + first + i % count
    return pl.pallas_call(
        finish_kernel,
        grid=(steps,),
        in_specs=[pl.BlockSpec((1,) + grads.shape[1:], lambda i: (i, 0, 0))]
        + [pl.BlockSpec(memory_space=pl.ANY)] * len(extra),
        out_specs=[
            pl.BlockSpec((1,) + up_shape[1:], lambda i: (place(i), 0, 0)),
            pl.BlockSpec((1,) + down_shape[1:], lambda i: (place(i), 0, 0)),
        ],
        out_shape=[jax.ShapeDtypeStruct(up_shape, F32), jax.ShapeDtypeStruct(down_shape, F32)],
        input_output_aliases={1: 0, 2: 1} if extra else {},
        compiler_params=roomy(60),
        cost_estimate=CHEAP,
        name="finish_weights",
    )(grads, *extra)


def write_halves(total_ref, core, kept_ref, sent_ref):
    part = kept_ref.shape[1]
    for n in range(kept_ref.shape[0]):
        pair = 2 * n * part
        own = core * part
        if part % 8:
            low = total_ref[pair : pair + part]
            high = total_ref[pair + part : pair + 2 * part]
            kept_ref[n] = jnp.where(own == 0, low, high).astype(BF)
            sent_ref[n] = jnp.where(own == 0, high, low).astype(BF)
        else:
            other = pl.multiple_of(pair + part - own, 8)
            own = pl.multiple_of(pair + own, 8)
            kept_ref[n] = total_ref[pl.ds(own, part)].astype(BF)
            sent_ref[n] = total_ref[pl.ds(other, part)].astype(BF)


def block_info_kernel_part(zone, seg_ref, par_ref, info_ref, block):
    blocks = info_ref.shape[0]
    slots = info_ref.shape[1] - 1
    total = seg_ref.shape[0] // block
    counts = []
    for a in range(blocks):
        mine = zone * blocks + a
        own = seg_ref[mine * block]
        above = par_ref[0, own]
        top = par_ref[0, above]
        count = jnp.int32(0)
        for c in range(total - 1):
            other = seg_ref[c * block]
            seen = (c < mine) & ((other == own) | (other == above) | (other == top))
            info_ref[a, jnp.minimum(count, slots - 1)] = (zone - c // blocks) * blocks + c % blocks
            count = count + seen.astype(jnp.int32)
        info_ref[a, slots] = count
        counts.append(count)
    return counts


def rope_angles(count, cos_ref, sin_ref, far_cos_ref, far_sin_ref):
    far_cos = far_cos_ref[pl.ds(count, 1)]
    far_sin = far_sin_ref[pl.ds(count, 1)]
    return (
        cos_ref[...] * far_cos - sin_ref[...] * far_sin,
        sin_ref[...] * far_cos + cos_ref[...] * far_sin,
    )


def turn(values, cosine, sine):
    lane = lax.broadcasted_iota(jnp.int32, values.shape, 1)
    crossed = jnp.where(
        lane % HEAD_SIZE < HEAD_SIZE // 2, -pltpu.roll(values, 96, 1), pltpu.roll(values, 32, 1)
    )
    return values * cosine + crossed * sine


def rope_tables(block, slots):
    frequency = 10000.0 ** (-np.arange(HEAD_SIZE // 2) / (HEAD_SIZE // 2))
    frequency = np.tile(frequency, 4)[None]
    near = np.arange(block)[:, None] * frequency
    far = np.arange(slots)[:, None] * block * frequency
    return [jnp.asarray(f(a), F32) for a in (near, far) for f in (np.cos, np.sin)]


def key_value_kernel(
    zone_ref, seg_ref, par_ref, x_ref, gain_ref, w_ref, c_ref, s_ref, fc_ref, fs_ref,
    normed_ref, kv_ref, info_ref,
):
    block = c_ref.shape[0]
    counts = block_info_kernel_part(zone_ref[0], seg_ref, par_ref, info_ref, block)
    x = x_ref[...].astype(F32)
    inverse = lax.rsqrt(jnp.mean(x * x, axis=-1, keepdims=True) + EPS)
    normed = (x * inverse * gain_ref[...].astype(F32)).astype(BF)
    normed_ref[...] = normed
    raw = dot_nn(normed, w_ref[...])
    low = lax.broadcasted_iota(jnp.int32, (block, 128), 1) < HEAD_SIZE
    for a, count in enumerate(counts):
        cosine, sine = rope_angles(count, c_ref, s_ref, fc_ref, fs_ref)
        rows = slice(a * block, (a + 1) * block)
        for t in range(raw.shape[1] // 128):
            tile = raw[rows, 128 * t : 128 * t + 128]
            kv_ref[rows, 128 * t : 128 * t + 128] = jnp.where(
                low, turn(tile, cosine, sine), tile
            ).astype(BF)


def query_kernel(info_ref, normed_ref, w_ref, c_ref, s_ref, fc_ref, fs_ref, q_ref):
    block = c_ref.shape[0]
    blocks = info_ref.shape[0]
    slots = info_ref.shape[1] - 1
    raw = dot_nn(normed_ref[...], w_ref[...])
    for a in range(blocks):
        cosine, sine = rope_angles(info_ref[a, slots], c_ref, s_ref, fc_ref, fs_ref)
        rows = slice(a * block, (a + 1) * block)
        for t in range(raw.shape[1] // 128):
            tile = raw[rows, 128 * t : 128 * t + 128]
            q_ref[rows, 128 * t : 128 * t + 128] = (
                turn(tile, cosine, sine).astype(BF).astype(F32) * HEAD_SIZE**-0.5
            ).astype(BF)


def head_low(tiles, head):
    tile = tiles[:, 128 * (head // 2) : 128 * (head // 2) + 128]
    low = lax.broadcasted_iota(jnp.int32, tile.shape, 1) < HEAD_SIZE
    if head % 2:
        tile = pltpu.roll(tile, HEAD_SIZE, 1)
    return jnp.where(low, tile, jnp.zeros_like(tile))


def head_high(tiles, head):
    tile = tiles[:, 128 * (head // 2) : 128 * (head // 2) + 128]
    low = lax.broadcasted_iota(jnp.int32, tile.shape, 1) < HEAD_SIZE
    if head % 2 == 0:
        tile = pltpu.roll(tile, HEAD_SIZE, 1)
    return jnp.where(low, jnp.zeros_like(tile), tile)


def collect(info_ref, kv_ref, seen_ref, step, block, group):
    slots = info_ref.shape[1] - 1
    count = info_ref[step, slots]
    columns = slice(128 * group, 128 * group + 128)
    for m in range(slots - 1):
        source = jnp.where(m < count, info_ref[step, m], 0)
        seen_ref[m * block : (m + 1) * block] = kv_ref[
            pl.ds(pl.multiple_of(source * block, 32), block), columns
        ]
    seen_ref[(slots - 1) * block : slots * block] = kv_ref[
        pl.ds(pl.multiple_of(step * block, 32), block), columns
    ]
    if seen_ref.shape[0] > slots * block:
        seen_ref[slots * block :] = jnp.zeros_like(seen_ref[slots * block :])
    return seen_ref[...]


def seen_mask(info_ref, step, block, width):
    slots = info_ref.shape[1] - 1
    column = lax.broadcasted_iota(jnp.int32, (block, width), 1)
    row = lax.broadcasted_iota(jnp.int32, (block, width), 0)
    before = (slots - 1) * block
    return (column < info_ref[step, slots] * block) | (
        (column >= before) & (column - before <= row)
    )


def attention_kernel(
    groups, heads, info_ref, place_ref, q_ref, kv_ref, wo_ref, ctx_ref, lse_ref, kept_ref, sent_ref,
    seen_ref, out_ref,
):
    step = pl.program_id(0)
    block = q_ref.shape[0]
    per = heads // groups
    mask = seen_mask(info_ref, step, block, seen_ref.shape[0])
    mask = jnp.concatenate([mask] * per, axis=0)
    queries = q_ref[...]
    lane = lax.broadcasted_iota(jnp.int32, lse_ref.shape, 1)
    totals = jnp.zeros(lse_ref.shape, F32)
    found = []
    for g in range(groups):
        seen = collect(info_ref, kv_ref, seen_ref, step, block, g)
        packed = jnp.concatenate([head_low(queries, g * per + r) for r in range(per)], axis=0)
        scores = jnp.where(mask, dot_nt(packed, seen), -1e30)
        top = jnp.max(scores, axis=1, keepdims=True)
        shifted = jnp.exp(scores - top)
        total = jnp.sum(shifted, axis=1, keepdims=True)
        result = dot_nn(shifted.astype(BF), seen) / total
        log_total = top + jnp.log(total)
        for r in range(per):
            rows = slice(r * block, (r + 1) * block)
            found.append(result[rows])
            totals = jnp.where(lane == g * per + r, log_total[rows], totals)
    lse_ref[...] = totals
    low = lax.broadcasted_iota(jnp.int32, (block, 128), 1) < HEAD_SIZE
    tiles = []
    for t in range(ctx_ref.shape[1] // 128):
        left = pltpu.roll(found[2 * t], HEAD_SIZE, 1)
        right = found[2 * t + 1] if 2 * t + 1 < heads else jnp.zeros_like(left)
        tiles.append(jnp.where(low, left, right).astype(BF))
    context = jnp.concatenate(tiles, axis=1)
    ctx_ref[...] = context
    out_ref[pl.ds(pl.multiple_of(step * block, 32), block)] = dot_nn(context, wo_ref[...])

    @pl.when(step == pl.num_programs(0) - 1)
    def _():
        write_halves(out_ref, place_ref[2], kept_ref, sent_ref)


def attention_back_kernel(
    groups, heads, info_ref, place_ref, q_ref, kv_ref, lse_ref, g_ref, ctx_ref, n_ref, wo_ref,
    c_ref, s_ref, fc_ref, fs_ref, dq_ref, dkv_ref, kept_ref, sent_ref, seen_ref, acc_ref,
    out_grad_ref, q_grad_ref,
):
    step = pl.program_id(0)
    block = q_ref.shape[0]
    slots = info_ref.shape[1] - 1
    per = heads // groups

    @pl.when(step == 0)
    def _():
        acc_ref[...] = jnp.zeros_like(acc_ref)
        out_grad_ref[...] = jnp.zeros_like(out_grad_ref)
        q_grad_ref[...] = jnp.zeros_like(q_grad_ref)

    mask = seen_mask(info_ref, step, block, seen_ref.shape[0])
    mask = jnp.concatenate([mask] * per, axis=0)
    queries = q_ref[...]
    out_grad_ref[...] += dot_tn(ctx_ref[...], g_ref[...])
    pulled = dot_nt(g_ref[...], wo_ref[...]).astype(BF)
    lane = lax.broadcasted_iota(jnp.int32, lse_ref.shape, 1)
    count = info_ref[step, slots]
    found = []
    for g in range(groups):
        seen = collect(info_ref, kv_ref, seen_ref, step, block, g)
        packed = jnp.concatenate([head_low(queries, g * per + r) for r in range(per)], axis=0)
        grads = jnp.concatenate([head_high(pulled, g * per + r) for r in range(per)], axis=0)
        log_total = jnp.concatenate(
            [
                jnp.sum(jnp.where(lane == g * per + r, lse_ref[...], 0.0), axis=1, keepdims=True)
                for r in range(per)
            ],
            axis=0,
        )
        scores = jnp.where(mask, dot_nt(packed, seen), -1e30)
        probabilities = jnp.exp(scores - log_total)
        prob_grad = dot_nt(grads, seen)
        row_dot = jnp.sum(probabilities * prob_grad, axis=1, keepdims=True)
        score_grad = (probabilities * (prob_grad - row_dot)).astype(BF)
        query_grad = dot_nn(score_grad, seen)
        pair_grad = (dot_tn(packed, score_grad) + dot_tn(grads, probabilities.astype(BF))).T
        for r in range(per):
            found.append(query_grad[r * block : (r + 1) * block])
        columns = slice(128 * g, 128 * g + 128)
        for m in range(slots - 1):

            @pl.when(m < count)
            def _():
                rows = pl.ds(pl.multiple_of(info_ref[step, m] * block, 32), block)
                acc_ref[rows, columns] += pair_grad[m * block : (m + 1) * block]

        rows = pl.ds(pl.multiple_of(step * block, 32), block)
        acc_ref[rows, columns] += pair_grad[(slots - 1) * block : slots * block]
    cosine, sine = rope_angles(count, c_ref, s_ref, fc_ref, fs_ref)
    low = lax.broadcasted_iota(jnp.int32, (block, 128), 1) < HEAD_SIZE
    for t in range(dq_ref.shape[1] // 128):
        left = found[2 * t]
        right = (
            pltpu.roll(found[2 * t + 1], HEAD_SIZE, 1)
            if 2 * t + 1 < heads
            else jnp.zeros_like(left)
        )
        tile = jnp.where(low, left, right) * HEAD_SIZE**-0.5
        dq_ref[:, 128 * t : 128 * t + 128] = turn(tile, cosine, -sine).astype(BF)

    q_grad_ref[...] += dot_tn(dq_ref[...], n_ref[...])

    @pl.when(step == pl.num_programs(0) - 1)
    def _():
        dkv_ref[...] = acc_ref[...].astype(BF)
        rows = kept_ref.shape[0]

        @pl.when(place_ref[3] == 0)
        def _():
            kept_ref[...] = out_grad_ref[:rows].astype(BF)
            sent_ref[...] = q_grad_ref[:rows].astype(BF)

        @pl.when(place_ref[3] != 0)
        def _():
            kept_ref[...] = q_grad_ref[:rows].astype(BF)
            sent_ref[...] = out_grad_ref[:rows].astype(BF)


def project_back_kernel(info_ref, place_ref, *refs):
    *pieces, n_ref, dq_ref, wq_ref, wkv_ref, c_ref, s_ref, fc_ref, fs_ref = refs[:-7]
    kept_ref, sent_ref, kept_kv_ref, sent_kv_ref, low_ref, back_ref, grad_ref = refs[-7:]
    block = c_ref.shape[0]
    blocks = info_ref.shape[0]
    slots = info_ref.shape[1] - 1
    total = pieces[0][...].astype(F32)
    for piece in pieces[1:]:
        total = total + piece[...].astype(F32)
    low = lax.broadcasted_iota(jnp.int32, (block, 128), 1) < HEAD_SIZE
    for a in range(blocks):
        cosine, sine = rope_angles(info_ref[a, slots], c_ref, s_ref, fc_ref, fs_ref)
        rows = slice(a * block, (a + 1) * block)
        for t in range(total.shape[1] // 128):
            tile = total[rows, 128 * t : 128 * t + 128]
            low_ref[rows, 128 * t : 128 * t + 128] = jnp.where(
                low, turn(tile, cosine, -sine), tile
            ).astype(BF)
    back_ref[...] = dot_nt(dq_ref[...], wq_ref[...]) + dot_nt(low_ref[...], wkv_ref[...])
    write_halves(back_ref, place_ref[2], kept_ref, sent_ref)
    grad_ref[...] = dot_tn(low_ref[...], n_ref[...])
    share = kept_kv_ref.shape[0]
    own = pl.multiple_of(place_ref[3] * share, 8)
    other = pl.multiple_of(share - own, 8)
    kept_kv_ref[...] = grad_ref[pl.ds(own, share)].astype(BF)
    sent_kv_ref[...] = grad_ref[pl.ds(other, share)].astype(BF)


def project_key_value(zone, segments, parents, tokens, gain, weight, tables, blocks, slots):
    rows, width = tokens.shape
    whole = lambda i: (0, 0)
    operands = (tokens, gain[None], weight, *tables)
    return pl.pallas_call(
        key_value_kernel,
        grid=(1,),
        in_specs=[SMEM] * 3 + [pl.BlockSpec(o.shape, whole) for o in operands],
        out_specs=[
            pl.BlockSpec((rows, width), whole),
            pl.BlockSpec((rows, weight.shape[1]), whole),
            SMEM,
        ],
        out_shape=[
            jax.ShapeDtypeStruct((rows, width), BF),
            jax.ShapeDtypeStruct((rows, weight.shape[1]), BF),
            jax.ShapeDtypeStruct((blocks, slots + 1), jnp.int32),
        ],
        compiler_params=roomy(32),
        cost_estimate=CHEAP,
        name="project_key_value",
    )(zone, segments, parents, *operands)


def project_query(info, normed, weight, tables):
    return pl.pallas_call(
        query_kernel,
        in_specs=[SMEM] + [VMEM] * 6,
        out_specs=VMEM,
        out_shape=jax.ShapeDtypeStruct((normed.shape[0], weight.shape[1]), BF),
        compiler_params=roomy(32),
        cost_estimate=CHEAP,
        name="project_query",
    )(info, normed, weight, *tables)


def lanes_up(size):
    return -(-size // 128) * 128


def attention_forward(info, place, queries, key_value, output_weight, heads, part):
    rows, columns = queries.shape
    blocks, slots = info.shape[0], info.shape[1] - 1
    block = rows // blocks
    groups = key_value.shape[1] // 128
    width = output_weight.shape[1]
    by_block = lambda i, *_: (i, 0)
    whole = lambda i, *_: (0, 0)
    half = (rows // (2 * part), part, width)
    return pl.pallas_call(
        functools.partial(attention_kernel, groups, heads),
        grid_spec=pltpu.PrefetchScalarGridSpec(
            num_scalar_prefetch=2,
            grid=(blocks,),
            in_specs=[
                pl.BlockSpec((block, columns), by_block),
                pl.BlockSpec(key_value.shape, whole),
                pl.BlockSpec(output_weight.shape, whole),
            ],
            out_specs=[
                pl.BlockSpec((block, columns), by_block),
                pl.BlockSpec((block, 128), by_block),
                pl.BlockSpec(half, lambda i, *_: (0, 0, 0)),
                pl.BlockSpec(half, lambda i, *_: (0, 0, 0)),
            ],
            scratch_shapes=[
                pltpu.VMEM((lanes_up(slots * block), 128), BF),
                pltpu.VMEM((rows, width), F32),
            ],
        ),
        out_shape=[
            jax.ShapeDtypeStruct((rows, columns), BF),
            jax.ShapeDtypeStruct((rows, 128), F32),
            jax.ShapeDtypeStruct(half, BF),
            jax.ShapeDtypeStruct(half, BF),
        ],
        compiler_params=roomy(48),
        cost_estimate=CHEAP,
        name="attention_forward",
    )(info, place, queries, key_value, output_weight)


def attention_backward(
    info, place, queries, key_value, log_totals, branch_grad, context, normed, output_weight,
    tables, heads,
):
    rows, columns = queries.shape
    blocks, slots = info.shape[0], info.shape[1] - 1
    block = rows // blocks
    groups = key_value.shape[1] // 128
    width = output_weight.shape[1]
    by_block = lambda i, *_: (i, 0)
    whole = lambda i, *_: (0, 0)
    share = (heads * HEAD_SIZE, width)
    return pl.pallas_call(
        functools.partial(attention_back_kernel, groups, heads),
        grid_spec=pltpu.PrefetchScalarGridSpec(
            num_scalar_prefetch=2,
            grid=(blocks,),
            in_specs=[
                pl.BlockSpec((block, columns), by_block),
                pl.BlockSpec(key_value.shape, whole),
                pl.BlockSpec((block, 128), by_block),
                pl.BlockSpec((block, width), by_block),
                pl.BlockSpec((block, columns), by_block),
                pl.BlockSpec((block, width), by_block),
                pl.BlockSpec(output_weight.shape, whole),
            ]
            + [pl.BlockSpec(t.shape, whole) for t in tables],
            out_specs=[
                pl.BlockSpec((block, columns), by_block),
                pl.BlockSpec(key_value.shape, whole),
                pl.BlockSpec(share, whole),
                pl.BlockSpec(share, whole),
            ],
            scratch_shapes=[
                pltpu.VMEM((lanes_up(slots * block), 128), BF),
                pltpu.VMEM(key_value.shape, F32),
                pltpu.VMEM((columns, width), F32),
                pltpu.VMEM((columns, width), F32),
            ],
        ),
        out_shape=[
            jax.ShapeDtypeStruct((rows, columns), BF),
            jax.ShapeDtypeStruct(key_value.shape, BF),
            jax.ShapeDtypeStruct(share, BF),
            jax.ShapeDtypeStruct(share, BF),
        ],
        compiler_params=roomy(56),
        cost_estimate=CHEAP,
        name="attention_backward",
    )(info, place, queries, key_value, log_totals, branch_grad, context, normed, output_weight, *tables)


def project_backward(info, place, pieces, normed, query_low, query_weight, pair_weight, tables, part):
    rows, width = normed.shape
    columns = pair_weight.shape[1]
    half = (rows // (2 * part), part, width)
    share = (columns // 2, width)
    return pl.pallas_call(
        project_back_kernel,
        in_specs=[SMEM] * 2 + [VMEM] * (len(pieces) + 8),
        out_specs=[VMEM] * 4,
        out_shape=[jax.ShapeDtypeStruct(shape, BF) for shape in (half, half, share, share)],
        scratch_shapes=[
            pltpu.VMEM((rows, columns), BF),
            pltpu.VMEM((rows, width), F32),
            pltpu.VMEM((columns, width), F32),
        ],
        compiler_params=roomy(48),
        cost_estimate=CHEAP,
        name="project_backward",
    )(info, place, *pieces, normed, query_low, query_weight, pair_weight, *tables)


def shift(values, axis, places):
    size = lax.axis_size(axis)
    return lax.ppermute(values, axis, [(i, (i + places) % size) for i in range(size)])


def slide(values, axis, places):
    size = lax.axis_size(axis)
    return lax.ppermute(
        values, axis, [(i, i + places) for i in range(size) if 0 <= i + places < size]
    )


def swap(values, axis, bit):
    return lax.ppermute(values, axis, [(i, i ^ bit) for i in range(lax.axis_size(axis))])


def bits_of(size):
    return [1 << b for b in range(size.bit_length() - 1)]


def hold(values, *others):
    return lax.optimization_barrier((values,) + others)[0]


def halves(held, bit):
    pairs = held.reshape(held.shape[:1] + (held.shape[1] // 2, 2) + held.shape[2:])
    mine = jnp.where((lax.axis_index("tensor") & bit) != 0, 1, 0)
    return (
        lax.dynamic_index_in_dim(pairs, mine, 2, keepdims=False),
        lax.dynamic_index_in_dim(pairs, 1 - mine, 2, keepdims=False),
    )


class Line:
    def __init__(self):
        self.last = None

    def mark(self, value):
        self.last = value
        return value

    def take(self, values):
        if isinstance(values, list):
            return list(lax.optimization_barrier((*values, self.last))[:-1])
        return hold(values, self.last)

    def after(self, values, others):
        return hold(values, others)


class Gathering:
    def __init__(self, line, pieces):
        self.held = line.mark(jnp.stack(pieces)[:, None])
        self.bits = bits_of(lax.axis_size("tensor"))[::-1]
        self.send(line)

    def send(self, line):
        if self.bits:
            self.coming = swap(self.held, "tensor", self.bits[0])

    def step(self, line):
        other = line.take(self.coming)
        mine = (lax.axis_index("tensor") & self.bits[0]) != 0
        held = jnp.where(
            mine, jnp.stack([other, self.held], axis=2), jnp.stack([self.held, other], axis=2)
        )
        self.held = line.mark(held.reshape((held.shape[0], -1) + held.shape[3:]))
        self.bits = self.bits[1:]
        self.send(line)

    def rows(self):
        return self.held.reshape(-1, self.held.shape[-1])


class Summing:
    def __init__(self, line, rows=None, split=None):
        size = lax.axis_size("tensor")
        self.bits = bits_of(size)
        if split is None:
            self.held = rows.reshape((rows.shape[0], size, -1) + rows.shape[2:])
            self.send(line)
        else:
            self.kept, sent = split
            self.coming = swap(line.take(sent), "tensor", self.bits[0])

    def send(self, line):
        if self.bits:
            self.kept, sent = halves(self.held, self.bits[0])
            self.coming = swap(line.mark(sent), "tensor", self.bits[0])

    def step(self, line):
        coming = line.take(self.coming)
        self.held = line.mark((self.kept.astype(F32) + coming.astype(F32)).astype(BF))
        self.bits = self.bits[1:]
        self.send(line)


class Mixing:
    def __init__(self, line, groups, part):
        self.bits = bits_of(lax.axis_size("tensor"))
        both = [halves(g.reshape(1, -1, part, g.shape[1]), self.bits[0]) for g in groups]
        self.kept = jnp.concatenate([b[0] for b in both], axis=0)
        sent = line.mark(jnp.concatenate([b[1] for b in both], axis=0))
        self.coming = swap(sent, "tensor", self.bits[0])

    def step(self, line):
        coming = line.take(self.coming)
        self.held = line.mark((self.kept.astype(F32) + coming.astype(F32)).astype(BF))
        self.bits = self.bits[1:]
        if self.bits:
            self.kept, sent = halves(self.held, self.bits[0])
            self.coming = swap(line.mark(sent), "tensor", self.bits[0])

    def homes(self, line):
        groups = line.take(self.held[:, 0])
        size = groups.shape[0]
        return [groups[0]] + [shift(groups[k], "expert", size - k) for k in range(1, size)]


class Exchange:
    def __init__(self, line, half, up_shape, down_shape):
        self.line, self.half, self.shapes = line, half, (up_shape, down_shape)
        self.waiting, self.flying, self.landed, self.totals = [], None, [], None
        self.done = 0

    def add(self, grads):
        self.waiting.append(self.line.mark(grads))
        if self.flying is None:
            self.begin()

    def begin(self):
        grads = self.line.take(self.waiting.pop(0))
        self.flying = lax.all_gather(grads, "dp", axis=0, tiled=True)

    def land(self):
        if self.flying is not None:
            self.landed.append(self.line.mark(self.line.take(self.flying)))
            self.flying = None
            if self.waiting:
                self.begin()

    def settle(self):
        while self.landed:
            grads = self.line.take(self.landed.pop(0))
            self.totals = finish_weights(grads, self.totals, self.done, self.half, *self.shapes)
            self.line.mark(self.totals[1])
            self.done += grads.shape[0] // 2


class AllSum:
    def __init__(self, line, kept, sent):
        self.kept = kept
        self.size = lax.axis_size("expert")
        self.coming = swap(line.take(sent), "dp", 1)
        self.stage = 0

    def spread(self, blocks):
        return lax.all_to_all(blocks, "expert", split_axis=0, concat_axis=0)

    def step(self, line):
        coming = line.take(self.coming)
        if self.stage == 0:
            both = line.mark((self.kept.astype(F32) + coming.astype(F32)).astype(BF))
            self.coming = self.spread(both.reshape((self.size, -1) + both.shape[1:]))
        elif self.stage == 1:
            total = coming[0].astype(F32)
            for k in range(1, self.size):
                total = total + coming[k].astype(F32)
            own = line.mark(jnp.broadcast_to(total.astype(BF)[None], coming.shape))
            self.coming = self.spread(own)
        elif self.stage == 2:
            self.own = line.mark(coming.reshape(self.kept.shape))
            self.coming = swap(self.own, "dp", 1)
        else:
            first = lax.axis_index("dp") == 0
            self.shares = (
                jnp.where(first, self.own, coming).astype(F32),
                jnp.where(first, coming, self.own).astype(F32),
            )
            line.mark(self.shares[0])
        self.stage += 1


class SmallSum:
    def __init__(self, line, values):
        self.values = values
        self.coming = swap(line.take(values), "dp", 1)
        self.stage = 0

    def step(self, line):
        coming = line.take(self.coming)
        if self.stage == 0:
            both = self.values + coming
            size = lax.axis_size("expert")
            own = line.mark(jnp.broadcast_to(both[None], (size,) + both.shape))
            self.coming = lax.all_to_all(own, "expert", split_axis=0, concat_axis=0)
        else:
            self.values = line.mark(jnp.sum(coming, axis=0))
        self.stage += 1


def shards(
    tokens,
    out_cotangent,
    first_gain,
    query_weight,
    key_value_matrix,
    output_weight,
    second_gain,
    expert_gate_up,
    expert_down,
    routes,
    route_gates,
    expert_slot,
    parent_segments,
    token_segments,
):
    row_count, width = tokens.shape
    tree_rows = token_segments.shape[0]
    query_columns = query_weight.shape[1]
    heads = query_columns // HEAD_SIZE
    local_experts = expert_gate_up.shape[0]
    all_experts = expert_slot.shape[0]
    devices = lax.axis_size("expert")
    zone = lax.axis_index("expert")
    tensor_bits = bits_of(lax.axis_size("tensor"))
    core = lax.axis_index("tensor") % 2
    part = row_count // lax.axis_size("tensor")
    first_part = lax.axis_index("tensor") * part
    leaf = tree_rows // 12
    block = math.gcd(leaf, row_count)
    blocks = row_count // block
    slots = 7 * leaf // block
    tables = rope_tables(block, slots)
    if query_columns % 128:
        query_weight = jnp.pad(query_weight, ((0, 0), (0, HEAD_SIZE)))
        output_weight = jnp.pad(output_weight, ((0, HEAD_SIZE), (0, 0)))

    normed_one, key_value, info = project_key_value(
        zone[None].astype(jnp.int32), token_segments, parent_segments, tokens, first_gain,
        key_value_matrix, tables, blocks, slots,
    )
    key_values = [key_value] + [slide(key_value, "expert", k) for k in range(1, devices)]
    queries = project_query(info, normed_one, query_weight, tables)
    experts_range = jnp.arange(all_experts, dtype=jnp.int32)[None, None, :]
    routed = jnp.sum(
        jnp.where(routes[:, :, None] == experts_range, expert_slot[None, None, :], 0), axis=2
    )
    dense = jnp.sum(
        jnp.where(routed[:, :, None] == experts_range, route_gates[:, :, None], 0.0), axis=1
    )
    dense_high = lax.reduce_precision(dense, 8, 7)
    own_gates = jnp.concatenate(
        [
            dense_high.astype(BF),
            (dense - dense_high).astype(BF),
            jnp.zeros((row_count, 128 - 2 * all_experts), BF),
        ],
        axis=1,
    )
    cotangent_part = lax.dynamic_slice_in_dim(out_cotangent, first_part, part, 0)
    gates_part = lax.dynamic_slice_in_dim(own_gates, first_part, part, 0)
    all_cotangents = lax.all_gather(
        jnp.concatenate([cotangent_part, gates_part], axis=1),
        ("dp", "expert", "tensor"),
        axis=0,
        tiled=True,
    )
    line = Line()
    line.mark(queries)
    key_values = line.mark(jnp.concatenate(line.take(key_values), axis=0))
    tree = lax.axis_index("dp")
    places = [
        jnp.stack(
            [tree * devices + (zone - k) % devices, zone * local_experts, core, tree, zone]
        ).astype(jnp.int32)
        for k in range(devices)
    ]
    context, log_totals, *split = attention_forward(
        info, places[0], queries, key_values, output_weight, heads, part
    )
    line.mark(context)
    summing = Summing(line, split=[h[None] for h in split])
    while summing.bits:
        summing.step(line)
    attention = summing.held[0, 0].astype(F32)
    inputs_part = lax.dynamic_slice_in_dim(tokens, first_part, part, 0).astype(F32)
    hidden_state = inputs_part + attention
    second_float = second_gain.astype(F32)
    normed_two = line.mark(normalize(hidden_state, second_float).astype(BF))

    gate_up, down = expert_gate_up, expert_down
    if gate_up.shape[2] == 2 * PAIR:
        gate_up = jnp.pad(gate_up, ((0, 0), (0, 0), (0, 2 * PAIR)))
        down = jnp.pad(down, ((0, 0), (0, PAIR), (0, 0)))
    if local_experts % 2:
        gate_up = jnp.pad(gate_up, ((0, 1), (0, 0), (0, 0)))
        down = jnp.pad(down, ((0, 1), (0, 0), (0, 0)))
    experts = gate_up.shape[0]
    half = experts // 2
    cots = [Rows(out_cotangent, 0)] + [Rows(all_cotangents) for _ in range(1, devices)]
    gates = [(Rows(own_gates, 0), 0)] + [(Rows(all_cotangents), width // 128)] * (devices - 1)
    xs = [None] * devices
    mains = [None] * devices
    running, homes = [], []
    total = None

    def advance(total):
        while homes:
            home = line.mark(line.take(homes.pop(0))).astype(F32)
            total = home if total is None else total + home
        for k, summing in list(running):
            summing.step(line)
            if not summing.bits:
                running.remove((k, summing))
                own = line.take(summing.held[0, 0])
                homes.append(shift(own, "expert", devices - k) if k else own)
        return total

    def run_main(k, total):
        mains[k] = experts_main(
            places[k], Rows(line.take(xs[k].array), xs[k].index), cots[k], *gates[k], gate_up,
            down, row_count, all_experts, part,
        )
        line.mark(mains[k][2])
        total = advance(total)
        running.append((k, Summing(line, split=[h[None] for h in mains[k][2:]])))
        return total

    nearest = shift(normed_two, "expert", 1)
    own_rows = Gathering(line, [normed_two])
    other_part = swap(normed_two, "dp", 1)
    nearest = line.mark(line.take(nearest))
    near_rows = Gathering(line, [nearest])
    own_rows.step(line)
    others = [shift(line.take(normed_two), "expert", k) for k in range(2, devices)]
    while own_rows.bits:
        own_rows.step(line)
    xs[0] = Rows(own_rows.rows(), 0)
    total = run_main(0, total)
    other_part = line.mark(line.take(other_part))
    x_other = lax.all_gather(other_part, ("expert", "tensor"), axis=0, tiled=True)
    near_rows.step(line)
    far = []
    for k in range(2, devices, 2):
        far.append(Gathering(line, line.take(others[k - 2 : k])))
    while near_rows.bits:
        near_rows.step(line)
    xs[1] = Rows(near_rows.rows(), 0)
    total = run_main(1, total)
    for n, gathering in enumerate(far):
        while gathering.bits:
            gathering.step(line)
            total = advance(total)
        rows = gathering.rows()
        for j in range(2):
            xs[2 + 2 * n + j] = Rows(rows, j)
            total = run_main(2 + 2 * n + j, total)
    hidden_grads, activations = [k[1] for k in mains], [k[0] for k in mains]
    flat_down = down.reshape(-1, width)
    mixed = []
    while running or homes:
        if len(mixed) < devices:
            array = line.take(activations[len(mixed)])
            mixed.append(
                line.mark(jnp.dot(array, flat_down, preferred_element_type=F32).astype(BF))
            )
        total = advance(total)
    while len(mixed) < devices:
        array = line.take(activations[len(mixed)])
        mixed.append(line.mark(jnp.dot(array, flat_down, preferred_element_type=F32).astype(BF)))
    normed_two_grad = total
    _, norm_two_pull = jax.vjp(normalize, hidden_state, second_float)
    hidden_norm_grad, second_gain_grad = norm_two_pull(normed_two_grad)
    residual_grad = line.mark(cotangent_part.astype(F32) + hidden_norm_grad)

    gathering = Gathering(line, [residual_grad.astype(BF)])
    mixing = Mixing(line, line.take(mixed), part)
    ga_other, hg_other = experts_other(
        places[0], line.take(x_other), all_cotangents, gate_up, down, row_count, all_experts
    )
    line.mark(ga_other)

    def weight_grads(first, count):
        x_late = line.take(x_other)
        groups = [
            (xs[k].array, hidden_grads[k], activations[k], xs[k].index, 0, k, devices)
            for k in range(devices)
        ] + [(x_late, hg_other, ga_other, k, k, None, devices) for k in range(devices)]
        parts = [
            experts_weights(
                places[0], groups[g : g + 8], all_cotangents, first, count, half, row_count
            )
            for g in range(0, len(groups), 8)
        ]
        if len(parts) == 1:
            return parts[0]
        return sum(p.astype(F32) for p in parts).astype(BF)

    exchange = Exchange(line, half, expert_gate_up.shape, expert_down.shape)
    split_count = (half + 1) // 2
    gathering.step(line)
    mixing.step(line)
    while gathering.bits:
        gathering.step(line)
    branch_grad = line.mark(gathering.rows())
    query_low, pair_all, *split = attention_backward(
        info, places[0], queries, key_values, log_totals, line.take(branch_grad), context,
        normed_one, output_weight, tables, heads,
    )
    line.mark(query_low)
    pieces = line.take(pair_all).reshape(devices, row_count, pair_all.shape[1])
    pieces = [pieces[0]] + [slide(pieces[k], "expert", -k) for k in range(1, devices)]
    outer_sum = AllSum(line, *split)
    first_grads = line.mark(weight_grads(0, split_count))
    pieces = line.take(pieces)
    line.mark(pieces[1])
    exchange.add(first_grads)
    *split, pair_kept, pair_sent = project_backward(
        info, places[0], pieces, normed_one, query_low, query_weight, key_value_matrix, tables,
        part,
    )
    line.mark(pair_kept)
    summing = Summing(line, split=[h[None] for h in split])
    outer_sum.step(line)
    pair_sum = AllSum(line, pair_kept, pair_sent)
    summing.step(line)
    last_grads = line.mark(weight_grads(split_count, half - split_count))
    while summing.bits:
        summing.step(line)
    outer_sum.step(line)
    pair_sum.step(line)
    while mixing.bits:
        mixing.step(line)
    normed_one_grad = summing.held[0, 0].astype(F32)
    _, norm_one_pull = jax.vjp(normalize, inputs_part, first_gain.astype(F32))
    input_norm_grad, first_gain_grad = norm_one_pull(normed_one_grad)
    input_part = line.mark((residual_grad + input_norm_grad).astype(BF))
    extra = jnp.zeros((8, width), F32).at[0].set(first_gain_grad).at[1].set(second_gain_grad)
    gathering = Gathering(line, [jnp.concatenate([input_part, extra.astype(BF)], axis=0)])
    homes = mixing.homes(line)
    exchange.add(last_grads)
    gathering.step(line)
    outer_sum.step(line)
    pair_sum.step(line)
    while gathering.bits:
        gathering.step(line)
    exchange.land()
    rows = gathering.held.reshape(-1, part + 8, width)
    input_gradient = rows[:, :part].reshape(row_count, width)
    gains = SmallSum(line, jnp.sum(rows[:, part:].astype(F32), axis=0))
    mixture = homes[0].astype(F32)
    for home in homes[1:]:
        mixture = mixture + line.take(home).astype(F32)
    gathering = Gathering(line, [line.mark((hidden_state + mixture).astype(BF))])
    pair_sum.step(line)
    gains.step(line)
    outer_sum.step(line)
    gathering.step(line)
    while gathering.bits:
        gathering.step(line)
    layer_output = gathering.rows()
    pair_sum.step(line)
    exchange.settle()
    gains.step(line)
    gains = gains.values
    while exchange.flying is not None:
        exchange.land()
        exchange.settle()
    totals = exchange.totals
    return (
        layer_output,
        input_gradient,
        gains[0],
        outer_sum.shares[1].T,
        jnp.concatenate(pair_sum.shares, axis=0).T,
        outer_sum.shares[0],
        gains[1],
        *totals,
    )


def solution(mesh):
    in_specs = (
        P(("dp", "expert"), None),
        P(("dp", "expert"), None),
        P(),
        P(None, "tensor"),
        P(None, "tensor"),
        P("tensor", None),
        P(),
        P("expert", None, "tensor"),
        P("expert", "tensor", None),
        P(("dp", "expert"), None),
        P(("dp", "expert"), None),
        P(),
        P("dp", None),
        P("dp"),
    )
    out_specs = (
        P(("dp", "expert"), None),
        P(("dp", "expert"), None),
        P(),
        P(None, "tensor"),
        P(None, "tensor"),
        P("tensor", None),
        P(),
        P("expert", None, "tensor"),
        P("expert", "tensor", None),
    )
    return jax.shard_map(shards, mesh=mesh, in_specs=in_specs, out_specs=out_specs, check_vma=False)
```

time: 2710 us -> 609 us (0.22)
  waiting for transfers between devices: 1980 us -> 182 us
  local copies, waits for them, and re-layouts: 324 us -> 32.1 us
  Pallas kernels: 0 us -> 186 us
  matrix products: 172 us -> 8.26 us
  starting transfers between devices: 33.4 us -> 115 us
  other arithmetic: 118 us -> 60.4 us
  blocking collectives: 46.5 us -> 0 us
    all_to_all x4 -> x5, waiting for transfers between devices: 1720 us -> 6.57 us  [the longest x4 6.57 us: spread(): return lax.all_to_all(blocks, 'expert', split_axis=0, concat_axis=0)]
    psum x5 -> x0, waiting for transfers between devices: 258 us -> none  [the longest x1 103 us: shards(): lax.psum(query_weight_grad.astype(jnp.bfloat16), ('dp', 'expert'))]
    pallas_call x0 -> x14, Pallas kernels: none -> 186 us  [the longest x4 63.1 us: experts_main(): pl.pallas_call(functools.partial(main_kernel, all_experts), grid_spec=plt...]
    ppermute x0 -> x47, waiting for transfers between devices: none -> 173 us  [the longest x32 76.9 us: swap(): lax.ppermute(values, axis, [(i, i ^ bit) for i in range(lax.axis_size(axi...]
    dot_general x24 -> x4, matrix products: 172 us -> 8.26 us  [shards(): jnp.dot(array, flat_down, preferred_element_type=F32).astype(BF)]
    gather x3 -> x0, local copies, waits for them, and re-layouts: 142 us -> none  [the longest x2 128 us: unpack_rows(): return buffer.reshape(all_experts, capacity, width)[slot_flat, place_flat]]
    ppermute x0 -> x47, starting transfers between devices: none -> 79.6 us  [the longest x9 34.2 us: shift(): lax.ppermute(values, axis, [(i, (i + places) % size) for i in range(size)])]
    unnamed x123, local copies, waits for them, and re-layouts: 91.7 us -> 16.3 us
  transfers between devices with their start and end apart: 10 -> 56, of which waited for: 9 -> 23; matrix products, arithmetic and copies ran while one was open for 16% -> 14% of each run, Pallas kernels for 0% -> 21%
where the time goes in v2:
time: 609 us; the launch traced here: 600 us
  Pallas kernels  186 us (31%)
  waiting for transfers between devices  182 us (30%)
  starting transfers between devices  115 us (19%)
  other arithmetic  60.4 us (10%)
  local copies, waits for them, and re-layouts  32.1 us (5%)
  between operations  17.2 us (3%)
  matrix products  8.26 us (1%)
    ppermute x32, waiting for transfers between devices, swap(): lax.ppermute(values, axis, [(i, i ^ bit) for i in range(lax.axis_size(axi...  76.9 us
    pallas_call x4, Pallas kernels, experts_main(): pl.pallas_call(functools.partial(main_kernel, all_experts), grid_spec=plt...  63.1 us
    ppermute x9, waiting for transfers between devices, shift(): lax.ppermute(values, axis, [(i, (i + places) % size) for i in range(size)])  62.8 us
    pallas_call x2, Pallas kernels, experts_weights(): pl.pallas_call(functools.partial(weights_kernel, [g[3:] for g in groups],...  46.2 us
    ppermute x9, starting transfers between devices, shift(): lax.ppermute(values, axis, [(i, (i + places) % size) for i in range(size)])  34.2 us
    ppermute x6, waiting for transfers between devices, slide(): lax.ppermute(values, axis, [(i, i + places) for i in range(size) if 0 <=...  33.8 us
    all_to_all x4, starting transfers between devices, spread(): return lax.all_to_all(blocks, 'expert', split_axis=0, concat_axis=0)  30.8 us
    ppermute x32, starting transfers between devices, swap(): lax.ppermute(values, axis, [(i, i ^ bit) for i in range(lax.axis_size(axi...  29.4 us
  transfers between devices with their start and end apart: 56, of which 23 were waited for; matrix products, arithmetic and copies ran while one was open for 14% of the time, Pallas kernels for 21%

profile of v2, /device:TPU:0, one launch (start us, length us, event | category | flops | bytes accessed | tf_op | source)
XLA Modules:
  0.0 600.3 jit_solution(3011764054804075414)
XLA Ops:
  13.8 2.4 project_key_value.1
  16.3 5.6 collective-permute-start
  21.9 4.5 collective-permute-start.1
  31.7 9.6 %collective-permute-done.1 = bf16[480,256]{1,0:T(8,128)(2,1)} collective-permute-done((bf16[480,256]{1,0:T(8,128)(2,1)}, bf16[480,256]{1,0:T(8,128)(2,1)}, u32[]{:S(2)}, u32[]{:S(2)}) %collective-permute-start.1) | collective-permute-done | bytes 245792 | tf_op jit(solution)/shard_map/ppermute | solution.py:781
  41.3 4.5 collective-permute-done.2
  49.7 9.8 %attention_forward.1 = (bf16[480,384]{1,0:T(8,128)(2,1)S(1)}, f32[480,128]{1,0:T(8,128)S(1)}, bf16[2,120,1536]{2,1,0:T(8,128)(2,1)S(1)}, bf16[2,120,1536]{2,1,0:T(8,128)(2,1)}) custom-call(s32[3,8]{1,0:T(4,128)S(1)} %get-tuple-element.156.info_ref, s32[5]{0:T(128)S(1)} %stack.215.place_ref, bf16[480,384]{1,0:T(8,128)(2,1)S(1)} %project_query.1.q_ref, ...), custom_call_target="tpu_custom_call" | custom-call | flops 1000 | bytes 1000 | tf_op jit(solution)/shard_map/attention_forward/pallas_call | solution.py:668
  61.8 2.6 collective-permute-done.3
  67.5 9.1 %collective-permute-done.4 = bf16[1,1,120,1536]{3,2,1,0:T(8,128)(2,1)S(1)} collective-permute-done((bf16[1,1,120,1536]{3,2,1,0:T(8,128)(2,1)S(1)}, bf16[1,1,120,1536]{3,2,1,0:T(8,128)(2,1)S(1)}, u32[]{:S(2)}, u32[]{:S(2)}) %collective-permute-start.4) | collective-permute-done | bytes 368672 | tf_op jit(solution)/shard_map/ppermute | solution.py:787
  77.1 6.9 %collective-permute-start.6 = (bf16[120,1536]{1,0:T(8,128)(2,1)S(1)}, bf16[120,1536]{1,0:T(8,128)(2,1)S(1)}, u32[]{:S(2)}, u32[]{:S(2)}) collective-permute-start(bf16[120,1536]{1,0:T(8,128)(2,1)S(1)} %multiply_convert_fusion), channel_id=1, source_target_pairs={{0,4},{4,8},{8,12},{12,0},{1,5},{5,9},{9,13},{13,1},{2,6},{6,10},{... | collective-permute-start | bytes 1105928 | tf_op jit(solution)/shard_map/ppermute | solution.py:776
  85.6 17.9 %collective-permute-done.6 = bf16[120,1536]{1,0:T(8,128)(2,1)S(1)} collective-permute-done((bf16[120,1536]{1,0:T(8,128)(2,1)S(1)}, bf16[120,1536]{1,0:T(8,128)(2,1)S(1)}, u32[]{:S(2)}, u32[]{:S(2)}) %collective-permute-start.6) | collective-permute-done | bytes 368672 | tf_op jit(solution)/shard_map/ppermute | solution.py:776
  106.8 9.0 %collective-permute-start.8 = (bf16[120,1536]{1,0:T(8,128)(2,1)S(1)}, bf16[120,1536]{1,0:T(8,128)(2,1)}, u32[]{:S(2)}, u32[]{:S(2)}) collective-permute-start(bf16[120,1536]{1,0:T(8,128)(2,1)S(1)} %multiply_convert_fusion), channel_id=1, source_target_pairs={{0,8},{4,12},{8,0},{12,4},{1,9},{5,13},{9,1},{13,5},{2,10},{6,14},... | collective-permute-start | bytes 1105928 | tf_op jit(solution)/shard_map/ppermute | solution.py:776
  115.8 3.0 collective-permute-start.9
  120.8 15.4 %experts_main.4 = (bf16[480,1280]{1,0:T(8,128)(2,1)S(1)}, bf16[480,2560]{1,0:T(8,128)(2,1)}, bf16[2,120,1536]{2,1,0:T(8,128)(2,1)S(1)}, bf16[2,120,1536]{2,1,0:T(8,128)(2,1)}) custom-call(s32[5]{0:T(128)S(1)} %stack.215.place_ref, bf16[480,1536]{1,0:T(8,128)(2,1)S(1)} %bitcast.168, bf16[480,1536]{1,0:T(8,128)(2,1)S(1)} %copy-done.17, ...), custom_call_target="tpu_custom_call" | custom-call | flops 1000 | bytes 1000 | tf_op jit(solution)/shard_map/experts_main/pallas_call | solution.py:146
  137.4 7.4 %collective-permute-done.8 = bf16[120,1536]{1,0:T(8,128)(2,1)} collective-permute-done((bf16[120,1536]{1,0:T(8,128)(2,1)S(1)}, bf16[120,1536]{1,0:T(8,128)(2,1)}, u32[]{:S(2)}, u32[]{:S(2)}) %collective-permute-start.8) | collective-permute-done | bytes 368672 | tf_op jit(solution)/shard_map/ppermute | solution.py:776
  144.8 2.3 fusion.20
  150.3 15.7 %experts_main.5 = (bf16[480,1280]{1,0:T(8,128)(2,1)S(1)}, bf16[480,2560]{1,0:T(8,128)(2,1)}, bf16[2,120,1536]{2,1,0:T(8,128)(2,1)S(1)}, bf16[2,120,1536]{2,1,0:T(8,128)(2,1)S(1)}) custom-call(s32[5]{0:T(128)S(1)} %stack.233.place_ref, bf16[480,1536]{1,0:T(8,128)(2,1)S(1)} %bitcast.171, bf16[3840,1664]{1,0:T(8,128)(2,1)} %all-gather.5.cloned.1.call-done.c_ref.g_ref.refs_8_, ...), custom_call_target="tpu_custom_call" | custom-call | flops 1000 | bytes 1000 | tf_op jit(solution)/shard_map/experts_main/pallas_call | solution.py:146
  168.6 3.2 maximum_select_fusion.4
  172.3 6.3 %collective-permute-done.17 = bf16[1,1,120,1536]{3,2,1,0:T(8,128)(2,1)S(1)} collective-permute-done((bf16[1,1,120,1536]{3,2,1,0:T(8,128)(2,1)S(1)}, bf16[1,1,120,1536]{3,2,1,0:T(8,128)(2,1)S(1)}, u32[]{:S(2)}, u32[]{:S(2)}) %collective-permute-start.17) | collective-permute-done | bytes 368672 | tf_op jit(solution)/shard_map/ppermute | solution.py:787
  181.5 7.4 %collective-permute-done.18 = bf16[1,1,120,1536]{3,2,1,0:T(8,128)(2,1)} collective-permute-done((bf16[1,1,120,1536]{3,2,1,0:T(8,128)(2,1)S(1)}, bf16[1,1,120,1536]{3,2,1,0:T(8,128)(2,1)}, u32[]{:S(2)}, u32[]{:S(2)}) %collective-permute-start.18) | collective-permute-done | bytes 368672 | tf_op jit(solution)/shard_map/ppermute | solution.py:787
  190.0 10.2 %collective-permute-start.19 = (bf16[120,1536]{1,0:T(8,128)(2,1)S(1)}, bf16[120,1536]{1,0:T(8,128)(2,1)S(1)}, u32[]{:S(2)}, u32[]{:S(2)}) collective-permute-start(bf16[120,1536]{1,0:T(8,128)(2,1)S(1)} %bitcast.213), channel_id=1, source_target_pairs={{0,12},{4,0},{8,4},{12,8},{1,13},{5,1},{9,5},{13,9},{2,14},{6,2},{... | collective-permute-start | bytes 1105928 | tf_op jit(solution)/shard_map/ppermute | solution.py:776
  200.2 2.3 maximum_select_fusion
  204.4 15.5 %experts_main.6 = (bf16[480,1280]{1,0:T(8,128)(2,1)S(1)}, bf16[480,2560]{1,0:T(8,128)(2,1)S(1)}, bf16[2,120,1536]{2,1,0:T(8,128)(2,1)S(1)}, bf16[2,120,1536]{2,1,0:T(8,128)(2,1)S(1)}) custom-call(s32[5]{0:T(128)S(1)} %stack.226.place_ref, bf16[960,1536]{1,0:T(8,128)(2,1)} %bitcast.177, bf16[3840,1664]{1,0:T(8,128)(2,1)} %all-gather.5.cloned.1.call-done.c_ref.g_ref.refs_8_, ...), custom_call_target="tpu_custom_call" | custom-call | flops 1000 | bytes 1000 | tf_op jit(solution)/shard_map/experts_main/pallas_call | solution.py:146
  222.5 16.5 %experts_main.7 = (bf16[480,1280]{1,0:T(8,128)(2,1)S(1)}, bf16[480,2560]{1,0:T(8,128)(2,1)S(1)}, bf16[2,120,1536]{2,1,0:T(8,128)(2,1)S(1)}, bf16[2,120,1536]{2,1,0:T(8,128)(2,1)S(1)}) custom-call(s32[5]{0:T(128)S(1)} %stack.251.place_ref, bf16[960,1536]{1,0:T(8,128)(2,1)} %bitcast.178, bf16[3840,1664]{1,0:T(8,128)(2,1)} %all-gather.5.cloned.1.call-done.c_ref.g_ref.refs_8_, ...), custom_call_target="tpu_custom_call" | custom-call | flops 1000 | bytes 1000 | tf_op jit(solution)/shard_map/experts_main/pallas_call | solution.py:146
  242.8 2.1 convolution_convert_fusion.3
  244.9 7.1 %collective-permute-done.22 = bf16[1,1,120,1536]{3,2,1,0:T(8,128)(2,1)S(1)} collective-permute-done((bf16[1,1,120,1536]{3,2,1,0:T(8,128)(2,1)S(1)}, bf16[1,1,120,1536]{3,2,1,0:T(8,128)(2,1)S(1)}, u32[]{:S(2)}, u32[]{:S(2)}) %collective-permute-start.22) | collective-permute-done | bytes 368672 | tf_op jit(solution)/shard_map/ppermute | solution.py:787
  256.1 14.5 %collective-permute-done.24 = bf16[120,1536]{1,0:T(8,128)(2,1)S(1)} collective-permute-done((bf16[120,1536]{1,0:T(8,128)(2,1)S(1)}, bf16[120,1536]{1,0:T(8,128)(2,1)S(1)}, u32[]{:S(2)}, u32[]{:S(2)}) %collective-permute-start.24) | collective-permute-done | bytes 368672 | tf_op jit(solution)/shard_map/ppermute | solution.py:776
  270.8 2.1 convolution_convert_fusion.1
  272.9 9.9 %collective-permute-done.25 = bf16[120,1536]{1,0:T(8,128)(2,1)S(1)} collective-permute-done((bf16[120,1536]{1,0:T(8,128)(2,1)S(1)}, bf16[120,1536]{1,0:T(8,128)(2,1)S(1)}, u32[]{:S(2)}, u32[]{:S(2)}) %collective-permute-start.25) | collective-permute-done | bytes 368672 | tf_op jit(solution)/shard_map/ppermute | solution.py:776
  283.3 2.2 convert_bitcast_fusion.1
  285.5 2.1 convolution_convert_fusion
  290.0 2.2 pad_maximum_fusion
  292.6 20.9 %experts_other.1 = (bf16[1920,640]{1,0:T(8,128)(2,1)}, bf16[1920,1280]{1,0:T(8,128)(2,1)}) custom-call(s32[5]{0:T(128)} %copy-done.37, bf16[1920,1536]{1,0:T(8,128)(2,1)} %all-gather.7.cloned.1.call-done.x_ref.refs_4_.refs_5_.refs_6_.refs_7_, bf16[3840,1664]{1,0:T(8,128)(2,1)} %all-gather.5.cloned.1.call-done.c_ref.g_ref.refs_8_, ...), custom_call_target="tpu_custom_call" | custom-call | flops 1000 | bytes 1000 | tf_op jit(solution)/shard_map/experts_other/pallas_call | solution.py:185
  316.4 2.2 add_convert_fusion
  321.5 22.1 %attention_backward.1 = (bf16[480,384]{1,0:T(8,128)(2,1)}, bf16[1920,256]{1,0:T(8,128)(2,1)}, bf16[384,1536]{1,0:T(8,128)(2,1)}, bf16[384,1536]{1,0:T(8,128)(2,1)}) custom-call(s32[3,8]{1,0:T(4,128)} %copy-done.35, s32[5]{0:T(128)} %copy-done.37, bf16[480,384]{1,0:T(8,128)(2,1)} %copy-done.18, bf16[1920,256]{1,0:T(8,128)(2,1)} %copy-done.7, ...), custom_call_target="tpu_custom_call" | custom-call | flops 1000 | bytes 1000 | tf_op jit(solution)/shard_map/attention_backward/pallas_call | solution.py:713
  343.6 29.0 %experts_weights.2 = bf16[3,2304,256]{2,1,0:T(8,128)(2,1)} custom-call(s32[5]{0:T(128)} %copy-done.37, bf16[480,1536]{1,0:T(8,128)(2,1)} %bitcast.169, bf16[480,1536]{1,0:T(8,128)(2,1)} %bitcast.172, bf16[960,1536]{1,0:T(8,128)(2,1)} %bitcast.179, bf16[960,1536]{1,0:T(8,128)(2,1)} %bitcast.180, ...), custom_call_target="tpu_custom_call" | custom-call | flops 1000 | bytes 1000 | tf_op jit(solution)/shard_map/experts_weights/pallas_call | solution.py:265
  378.4 6.6 %collective-permute-done.30.refs_1_ = bf16[480,256]{1,0:T(8,128)(2,1)S(1)} collective-permute-done((bf16[480,256]{1,0:T(8,128)(2,1)S(1)}, bf16[480,256]{1,0:T(8,128)(2,1)S(1)}, u32[]{:S(2)}, u32[]{:S(2)}) %collective-permute-start.30) | collective-permute-done | bytes 245792 | tf_op jit(solution)/shard_map/ppermute | solution.py:781
  385.1 13.0 %collective-permute-done.31.refs_2_ = bf16[480,256]{1,0:T(8,128)(2,1)S(1)} collective-permute-done((bf16[480,256]{1,0:T(8,128)(2,1)S(1)}, bf16[480,256]{1,0:T(8,128)(2,1)S(1)}, u32[]{:S(2)}, u32[]{:S(2)}) %collective-permute-start.31) | collective-permute-done | bytes 245792 | tf_op jit(solution)/shard_map/ppermute | solution.py:781
  398.1 4.1 project_backward.1
  402.2 16.7 %collective-permute-done.33 = bf16[384,1536]{1,0:T(8,128)(2,1)S(1)} collective-permute-done((bf16[384,1536]{1,0:T(8,128)(2,1)}, bf16[384,1536]{1,0:T(8,128)(2,1)S(1)}, u32[]{:S(2)}, u32[]{:S(2)}) %collective-permute-start.33) | collective-permute-done | bytes 1179680 | tf_op jit(solution)/shard_map/ppermute | solution.py:787
  420.2 4.3 all-to-all-start
  428.9 17.2 %experts_weights.3 = bf16[2,2304,256]{2,1,0:T(8,128)(2,1)} custom-call(s32[5]{0:T(128)} %copy-done.37, bf16[480,1536]{1,0:T(8,128)(2,1)} %bitcast.170, bf16[480,1536]{1,0:T(8,128)(2,1)} %bitcast.173, bf16[960,1536]{1,0:T(8,128)(2,1)} %bitcast.181, bf16[960,1536]{1,0:T(8,128)(2,1)} %bitcast.182, ...), custom_call_target="tpu_custom_call" | custom-call | flops 1000 | bytes 1000 | tf_op jit(solution)/shard_map/experts_weights/pallas_call | solution.py:265
  447.5 4.0 all-to-all-done
  454.0 4.4 all-to-all-start.1
  460.6 2.2 collective-permute-start.41
  462.9 2.5 collective-permute-start.34
  465.3 10.4 %collective-permute-done.41 = bf16[1,1,128,1536]{3,2,1,0:T(8,128)(2,1)} collective-permute-done((bf16[1,1,128,1536]{3,2,1,0:T(8,128)(2,1)S(1)}, bf16[1,1,128,1536]{3,2,1,0:T(8,128)(2,1)}, u32[]{:S(2)}, u32[]{:S(2)}) %collective-permute-start.41) | collective-permute-done | bytes 393248 | tf_op jit(solution)/shard_map/ppermute | solution.py:787
  475.8 2.1 maximum_select_fusion.8
  477.9 2.1 maximum_select_fusion.9
  480.1 3.0 collective-permute-done.34
  486.5 3.5 all-to-all-start.2
  490.0 2.3 fusion
  493.3 3.8 collective-permute-start.37
  498.2 2.4 collective-permute-start.42
  503.3 18.6 %all-to-all-start.3 = ((bf16[4,32,1536]{2,1,0:T(8,128)(2,1)}), bf16[4,32,1536]{2,1,0:T(8,128)(2,1)}, u32[]{:S(2)}, u32[]{:S(2)}) async-start(bf16[4,32,1536]{2,1,0:T(8,128)(2,1)} %broadcast_in_dim.119), calls=%async_computation.3 | async-start | bytes 786432 | tf_op jit(solution)/shard_map/all_to_all | solution.py:931
  521.9 2.1 maximum_select_fusion.1
  525.3 13.1 %collective-permute-done.38 = bf16[120,1536]{1,0:T(8,128)(2,1)} collective-permute-done((bf16[120,1536]{1,0:T(8,128)(2,1)}, bf16[120,1536]{1,0:T(8,128)(2,1)}, u32[]{:S(2)}, u32[]{:S(2)}) %collective-permute-start.38) | collective-permute-done | bytes 368672 | tf_op jit(solution)/shard_map/ppermute | solution.py:776
  541.8 2.5 collective-permute-start.40
  544.4 10.6 %collective-permute-done.44 = f32[8,1536]{1,0:T(8,128)S(1)} collective-permute-done((f32[8,1536]{1,0:T(8,128)S(1)}, f32[8,1536]{1,0:T(8,128)S(1)}, u32[]{:S(2)}, u32[]{:S(2)}) %collective-permute-start.44) | collective-permute-done | bytes 49184 | tf_op jit(solution)/shard_map/ppermute | solution.py:787
  555.7 4.2 all-to-all-start.4
  559.9 3.3 convert_bitcast_fusion
  567.2 3.7 collective-permute-done.46
  572.1 8.9 %finish_weights.2 = (f32[10,1536,256]{2,1,0:T(8,128)}, f32[10,128,1536]{2,1,0:T(8,128)}) custom-call(bf16[6,2304,256]{2,1,0:T(8,128)(2,1)} %all-gather.9.cloned.1.call-done.source), custom_call_target="tpu_custom_call" | custom-call | flops 1000 | bytes 1000 | tf_op jit(solution)/shard_map/finish_weights/pallas_call | solution.py:305
  583.4 2.7 maximum_select_fusion.7
  586.1 6.4 %finish_weights.3 = (f32[10,1536,256]{2,1,0:T(8,128)}, f32[10,128,1536]{2,1,0:T(8,128)}) custom-call(bf16[4,2304,256]{2,1,0:T(8,128)(2,1)} %all-gather.11.cloned.1.call-done.source, f32[10,1536,256]{2,1,0:T(8,128)} %get-tuple-element.276.refs_0_, f32[10,128,1536]{2,1,0:T(8,128)} %get-tuple-element.272.refs_1_), custom_call_target="tpu_custom_call", output_to_operand_aliasing={{0}: (1, {}), {1}: (2, {})} | custom-call | flops 1000 | bytes 1000 | tf_op jit(solution)/shard_map/finish_weights/pallas_call | solution.py:305
  (292 shorter events, 98.9 us)
Async XLA Ops:
  8.0 142.3 %all-gather.5.cloned.1.call-start = ((), (), s32[]{:S(2)}) async-start(), calls=%async_computation.5 | async-start | bytes 13178880 | tf_op jit(solution)/shard_map/all_gather | solution.py:1036
  12.5 280.1 %all-gather.7.cloned.1.call-start = ((), (), s32[]{:S(2)}) async-start(), calls=%async_computation.6 | async-start | bytes 6266880 | tf_op jit(solution)/shard_map/all_gather | solution.py:1115
  16.3 33.4 %copy-start.35 = (s32[3,8]{1,0:T(4,128)}, s32[3,8]{1,0:T(4,128)S(1)}, u32[]{:S(2)}) copy-start(s32[3,8]{1,0:T(4,128)S(1)} %get-tuple-element.156.info_ref) | copy-start | bytes 292
  16.3 15.4 %collective-permute-start = (bf16[480,256]{1,0:T(8,128)(2,1)}, bf16[480,256]{1,0:T(8,128)(2,1)}, u32[]{:S(2)}, u32[]{:S(2)}) collective-permute-start(bf16[480,256]{1,0:T(8,128)(2,1)} %get-tuple-element.159), channel_id=1, source_target_pairs={{0,4},{4,8},{8,12},{1,5},{5,9},{9,13},{2,6},{6,10},{10,14},{3,7},{... | collective-permute-start | bytes 737288 | tf_op jit(solution)/shard_map/ppermute | solution.py:781
  21.9 19.4 %collective-permute-start.1 = (bf16[480,256]{1,0:T(8,128)(2,1)}, bf16[480,256]{1,0:T(8,128)(2,1)}, u32[]{:S(2)}, u32[]{:S(2)}) collective-permute-start(bf16[480,256]{1,0:T(8,128)(2,1)} %get-tuple-element.159), channel_id=1, source_target_pairs={{0,8},{4,12},{1,9},{5,13},{2,10},{6,14},{3,11},{7,15},{16,24},{20,... | collective-permute-start | bytes 737288 | tf_op jit(solution)/shard_map/ppermute | solution.py:781
  26.4 19.4 %collective-permute-start.2 = (bf16[480,256]{1,0:T(8,128)(2,1)}, bf16[480,256]{1,0:T(8,128)(2,1)}, u32[]{:S(2)}, u32[]{:S(2)}) collective-permute-start(bf16[480,256]{1,0:T(8,128)(2,1)} %get-tuple-element.159), channel_id=1, source_target_pairs={{0,12},{1,13},{2,14},{3,15},{16,28},{17,29},{18,30},{19,31}} | collective-permute-start | bytes 737288 | tf_op jit(solution)/shard_map/ppermute | solution.py:781
  31.5 28.0 %copy-start.18 = (bf16[480,384]{1,0:T(8,128)(2,1)}, bf16[480,384]{1,0:T(8,128)(2,1)S(1)}, u32[]{:S(2)}) copy-start(bf16[480,384]{1,0:T(8,128)(2,1)S(1)} %project_query.1.q_ref) | copy-start | bytes 1105924
  31.6 87.6 %copy-start.37 = (s32[5]{0:T(128)}, s32[5]{0:T(128)S(1)}, u32[]{:S(2)}) copy-start(s32[5]{0:T(128)S(1)} %stack.215.place_ref) | copy-start | bytes 64
  61.8 2.6 collective-permute-start.3
  66.0 10.7 %collective-permute-start.4 = (bf16[1,1,120,1536]{3,2,1,0:T(8,128)(2,1)S(1)}, bf16[1,1,120,1536]{3,2,1,0:T(8,128)(2,1)S(1)}, u32[]{:S(2)}, u32[]{:S(2)}) collective-permute-start(bf16[1,1,120,1536]{3,2,1,0:T(8,128)(2,1)S(1)} %constant_dynamic-slice_fusion.8), channel_id=1, source_target_pairs={{0,2},{1,3},{2,0},{3,1},{4,6},{5,7},{6,4},{7,5},{8,10},{9,11},{10,... | collective-permute-start | bytes 1105928 | tf_op jit(solution)/shard_map/ppermute | solution.py:787
  77.0 42.0 %copy-start.43 = (bf16[120,1536]{1,0:T(8,128)(2,1)}, bf16[120,1536]{1,0:T(8,128)(2,1)S(1)}, u32[]{:S(2)}) copy-start(bf16[120,1536]{1,0:T(8,128)(2,1)S(1)} %get-tuple-element.335) | copy-start | bytes 1105924
  77.1 26.3 %collective-permute-start.6 = (bf16[120,1536]{1,0:T(8,128)(2,1)S(1)}, bf16[120,1536]{1,0:T(8,128)(2,1)S(1)}, u32[]{:S(2)}, u32[]{:S(2)}) collective-permute-start(bf16[120,1536]{1,0:T(8,128)(2,1)S(1)} %multiply_convert_fusion), channel_id=1, source_target_pairs={{0,4},{4,8},{8,12},{12,0},{1,5},{5,9},{9,13},{13,1},{2,6},{6,10},{... | collective-permute-start | bytes 1105928 | tf_op jit(solution)/shard_map/ppermute | solution.py:776
  84.0 19.4 %collective-permute-start.5 = (bf16[1,1,120,1536]{3,2,1,0:T(8,128)(2,1)S(1)}, bf16[1,1,120,1536]{3,2,1,0:T(8,128)(2,1)S(1)}, u32[]{:S(2)}, u32[]{:S(2)}) collective-permute-start(bf16[1,1,120,1536]{3,2,1,0:T(8,128)(2,1)S(1)} %bitcast.193), channel_id=1, source_target_pairs={{0,2},{1,3},{2,0},{3,1},{4,6},{5,7},{6,4},{7,5},{8,10},{9,11},{10,... | collective-permute-start | bytes 1105928 | tf_op jit(solution)/shard_map/ppermute | solution.py:787
  103.6 15.4 %collective-permute-start.7 = (bf16[1,2,120,1536]{3,2,1,0:T(8,128)(2,1)S(1)}, bf16[1,2,120,1536]{3,2,1,0:T(8,128)(2,1)S(1)}, u32[]{:S(2)}, u32[]{:S(2)}) collective-permute-start(bf16[1,2,120,1536]{3,2,1,0:T(8,128)(2,1)S(1)} %maximum_select_fusion.10), channel_id=1, source_target_pairs={{0,1},{1,0},{2,3},{3,2},{4,5},{5,4},{6,7},{7,6},{8,9},{9,8},{10,11... | collective-permute-start | bytes 2211848 | tf_op jit(solution)/shard_map/ppermute | solution.py:787
  103.6 32.5 %collective-permute-start.11 = (bf16[120,1536]{1,0:T(8,128)(2,1)S(1)}, bf16[120,1536]{1,0:T(8,128)(2,1)}, u32[]{:S(2)}, u32[]{:S(2)}) collective-permute-start(bf16[120,1536]{1,0:T(8,128)(2,1)S(1)} %multiply_convert_fusion), channel_id=1, source_target_pairs={{0,16},{16,0},{1,17},{17,1},{2,18},{18,2},{3,19},{19,3},{4,20},{20... | collective-permute-start | bytes 1105928 | tf_op jit(solution)/shard_map/ppermute | solution.py:787
  105.3 30.9 %collective-permute-start.10 = (bf16[1,1,120,1536]{3,2,1,0:T(8,128)(2,1)S(1)}, bf16[1,1,120,1536]{3,2,1,0:T(8,128)(2,1)S(1)}, u32[]{:S(2)}, u32[]{:S(2)}) collective-permute-start(bf16[1,1,120,1536]{3,2,1,0:T(8,128)(2,1)S(1)} %bitcast.205), channel_id=1, source_target_pairs={{0,2},{1,3},{2,0},{3,1},{4,6},{5,7},{6,4},{7,5},{8,10},{9,11},{10,... | collective-permute-start | bytes 1105928 | tf_op jit(solution)/shard_map/ppermute | solution.py:787
  106.8 38.0 %collective-permute-start.8 = (bf16[120,1536]{1,0:T(8,128)(2,1)S(1)}, bf16[120,1536]{1,0:T(8,128)(2,1)}, u32[]{:S(2)}, u32[]{:S(2)}) collective-permute-start(bf16[120,1536]{1,0:T(8,128)(2,1)S(1)} %multiply_convert_fusion), channel_id=1, source_target_pairs={{0,8},{4,12},{8,0},{12,4},{1,9},{5,13},{9,1},{13,5},{2,10},{6,14},... | collective-permute-start | bytes 1105928 | tf_op jit(solution)/shard_map/ppermute | solution.py:776
  115.8 28.9 %collective-permute-start.9 = (bf16[120,1536]{1,0:T(8,128)(2,1)S(1)}, bf16[120,1536]{1,0:T(8,128)(2,1)}, u32[]{:S(2)}, u32[]{:S(2)}) collective-permute-start(bf16[120,1536]{1,0:T(8,128)(2,1)S(1)} %multiply_convert_fusion), channel_id=1, source_target_pairs={{0,12},{4,0},{8,4},{12,8},{1,13},{5,1},{9,5},{13,9},{2,14},{6,2},{... | collective-permute-start | bytes 1105928 | tf_op jit(solution)/shard_map/ppermute | solution.py:776
  136.2 106.6 %copy-start.8 = (bf16[480,1280]{1,0:T(8,128)(2,1)}, bf16[480,1280]{1,0:T(8,128)(2,1)S(1)}, u32[]{:S(2)}) copy-start(bf16[480,1280]{1,0:T(8,128)(2,1)S(1)} %get-tuple-element.201.refs_17_) | copy-start | bytes 3686404
  137.3 11.2 %collective-permute-start.14 = (bf16[1,2,120,1536]{3,2,1,0:T(8,128)(2,1)}, bf16[1,2,120,1536]{3,2,1,0:T(8,128)(2,1)}, u32[]{:S(2)}, u32[]{:S(2)}) collective-permute-start(bf16[1,2,120,1536]{3,2,1,0:T(8,128)(2,1)} %maximum_select_fusion.11), channel_id=1, source_target_pairs={{0,1},{1,0},{2,3},{3,2},{4,5},{5,4},{6,7},{7,6},{8,9},{9,8},{10,11... | collective-permute-start | bytes 2211848 | tf_op jit(solution)/shard_map/ppermute | solution.py:787
  144.8 21.2 %collective-permute-start.13 = (bf16[1,2,120,1536]{3,2,1,0:T(8,128)(2,1)}, bf16[1,2,120,1536]{3,2,1,0:T(8,128)(2,1)}, u32[]{:S(2)}, u32[]{:S(2)}) collective-permute-start(bf16[1,2,120,1536]{3,2,1,0:T(8,128)(2,1)} %bitcast.20), channel_id=1, source_target_pairs={{0,1},{1,0},{2,3},{3,2},{4,5},{5,4},{6,7},{7,6},{8,9},{9,8},{10,11... | collective-permute-start | bytes 2211848 | tf_op jit(solution)/shard_map/ppermute | solution.py:787
  147.1 21.5 %collective-permute-start.12 = (bf16[2,1,120,1536]{3,2,0,1:T(8,128)(2,1)}, bf16[2,1,120,1536]{3,2,0,1:T(8,128)(2,1)}, u32[]{:S(2)}, u32[]{:S(2)}) collective-permute-start(bf16[2,1,120,1536]{3,2,0,1:T(8,128)(2,1)} %get-tuple-element.355), channel_id=1, source_target_pairs={{0,2},{1,3},{2,0},{3,1},{4,6},{5,7},{6,4},{7,5},{8,10},{9,11},{10,... | collective-permute-start | bytes 2211848 | tf_op jit(solution)/shard_map/ppermute | solution.py:787
  167.8 10.7 %collective-permute-start.17 = (bf16[1,1,120,1536]{3,2,1,0:T(8,128)(2,1)S(1)}, bf16[1,1,120,1536]{3,2,1,0:T(8,128)(2,1)S(1)}, u32[]{:S(2)}, u32[]{:S(2)}) collective-permute-start(bf16[1,1,120,1536]{3,2,1,0:T(8,128)(2,1)S(1)} %constant_dynamic-slice_fusion.5), channel_id=1, source_target_pairs={{0,2},{1,3},{2,0},{3,1},{4,6},{5,7},{6,4},{7,5},{8,10},{9,11},{10,... | collective-permute-start | bytes 1105928 | tf_op jit(solution)/shard_map/ppermute | solution.py:787
  168.6 10.1 %collective-permute-start.16 = (bf16[1,2,120,1536]{3,2,1,0:T(8,128)(2,1)S(1)}, bf16[1,2,120,1536]{3,2,1,0:T(8,128)(2,1)S(1)}, u32[]{:S(2)}, u32[]{:S(2)}) collective-permute-start(bf16[1,2,120,1536]{3,2,1,0:T(8,128)(2,1)S(1)} %bitcast.175), channel_id=1, source_target_pairs={{0,1},{1,0},{2,3},{3,2},{4,5},{5,4},{6,7},{7,6},{8,9},{9,8},{10,11... | collective-permute-start | bytes 2211848 | tf_op jit(solution)/shard_map/ppermute | solution.py:787
  171.8 28.4 %collective-permute-start.15 = (bf16[2,2,120,1536]{3,2,0,1:T(8,128)(2,1)}, bf16[2,2,120,1536]{3,2,0,1:T(8,128)(2,1)}, u32[]{:S(2)}, u32[]{:S(2)}) collective-permute-start(bf16[2,2,120,1536]{3,2,0,1:T(8,128)(2,1)} %maximum_select_fusion.4), channel_id=1, source_target_pairs={{0,1},{1,0},{2,3},{3,2},{4,5},{5,4},{6,7},{7,6},{8,9},{9,8},{10,11... | collective-permute-start | bytes 4423688 | tf_op jit(solution)/shard_map/ppermute | solution.py:787
  178.9 10.0 %collective-permute-start.18 = (bf16[1,1,120,1536]{3,2,1,0:T(8,128)(2,1)S(1)}, bf16[1,1,120,1536]{3,2,1,0:T(8,128)(2,1)}, u32[]{:S(2)}, u32[]{:S(2)}) collective-permute-start(bf16[1,1,120,1536]{3,2,1,0:T(8,128)(2,1)S(1)} %constant_dynamic-slice_fusion.4), channel_id=1, source_target_pairs={{0,2},{1,3},{2,0},{3,1},{4,6},{5,7},{6,4},{7,5},{8,10},{9,11},{10,... | collective-permute-start | bytes 1105928 | tf_op jit(solution)/shard_map/ppermute | solution.py:787
  179.9 305.8 %all-gather.9.cloned.1.call-start = ((), (), s32[]{:S(2)}) async-start(), calls=%async_computation.7 | async-start | bytes 10616832 | tf_op jit(solution)/shard_map/all_gather | solution.py:906
  190.0 32.4 %collective-permute-start.19 = (bf16[120,1536]{1,0:T(8,128)(2,1)S(1)}, bf16[120,1536]{1,0:T(8,128)(2,1)S(1)}, u32[]{:S(2)}, u32[]{:S(2)}) collective-permute-start(bf16[120,1536]{1,0:T(8,128)(2,1)S(1)} %bitcast.213), channel_id=1, source_target_pairs={{0,12},{4,0},{8,4},{12,8},{1,13},{5,1},{9,5},{13,9},{2,14},{6,2},{... | collective-permute-start | bytes 1105928 | tf_op jit(solution)/shard_map/ppermute | solution.py:776
  222.4 16.6 %collective-permute-start.20 = (bf16[1,2,120,1536]{3,2,1,0:T(8,128)(2,1)S(1)}, bf16[1,2,120,1536]{3,2,1,0:T(8,128)(2,1)}, u32[]{:S(2)}, u32[]{:S(2)}) collective-permute-start(bf16[1,2,120,1536]{3,2,1,0:T(8,128)(2,1)S(1)} %bitcast.174), channel_id=1, source_target_pairs={{0,1},{1,0},{2,3},{3,2},{4,5},{5,4},{6,7},{7,6},{8,9},{9,8},{10,11... | collective-permute-start | bytes 2211848 | tf_op jit(solution)/shard_map/ppermute | solution.py:787
  239.0 46.5 %copy-start.13 = (bf16[480,1280]{1,0:T(8,128)(2,1)}, bf16[480,1280]{1,0:T(8,128)(2,1)S(1)}, u32[]{:S(2)}) copy-start(bf16[480,1280]{1,0:T(8,128)(2,1)S(1)} %get-tuple-element.216.refs_20_) | copy-start | bytes 3686404
  240.9 11.1 %collective-permute-start.22 = (bf16[1,1,120,1536]{3,2,1,0:T(8,128)(2,1)S(1)}, bf16[1,1,120,1536]{3,2,1,0:T(8,128)(2,1)S(1)}, u32[]{:S(2)}, u32[]{:S(2)}) collective-permute-start(bf16[1,1,120,1536]{3,2,1,0:T(8,128)(2,1)S(1)} %constant_dynamic-slice_fusion.3), channel_id=1, source_target_pairs={{0,2},{1,3},{2,0},{3,1},{4,6},{5,7},{6,4},{7,5},{8,10},{9,11},{10,... | collective-permute-start | bytes 1105928 | tf_op jit(solution)/shard_map/ppermute | solution.py:787
  242.6 9.6 %collective-permute-start.21 = (bf16[1,2,120,1536]{3,2,1,0:T(8,128)(2,1)S(1)}, bf16[1,2,120,1536]{3,2,1,0:T(8,128)(2,1)S(1)}, u32[]{:S(2)}, u32[]{:S(2)}) collective-permute-start(bf16[1,2,120,1536]{3,2,1,0:T(8,128)(2,1)S(1)} %bitcast.176), channel_id=1, source_target_pairs={{0,1},{1,0},{2,3},{3,2},{4,5},{5,4},{6,7},{7,6},{8,9},{9,8},{10,11... | collective-permute-start | bytes 2211848 | tf_op jit(solution)/shard_map/ppermute | solution.py:787
  252.1 18.5 %collective-permute-start.24 = (bf16[120,1536]{1,0:T(8,128)(2,1)S(1)}, bf16[120,1536]{1,0:T(8,128)(2,1)S(1)}, u32[]{:S(2)}, u32[]{:S(2)}) collective-permute-start(bf16[120,1536]{1,0:T(8,128)(2,1)S(1)} %bitcast.214), channel_id=1, source_target_pairs={{0,8},{4,12},{8,0},{12,4},{1,9},{5,13},{9,1},{13,5},{2,10},{6,14},... | collective-permute-start | bytes 1105928 | tf_op jit(solution)/shard_map/ppermute | solution.py:776
  252.4 18.2 %collective-permute-start.23 = (bf16[1,1,120,1536]{3,2,1,0:T(8,128)(2,1)S(1)}, bf16[1,1,120,1536]{3,2,1,0:T(8,128)(2,1)S(1)}, u32[]{:S(2)}, u32[]{:S(2)}) collective-permute-start(bf16[1,1,120,1536]{3,2,1,0:T(8,128)(2,1)S(1)} %constant_dynamic-slice_fusion.2), channel_id=1, source_target_pairs={{0,2},{1,3},{2,0},{3,1},{4,6},{5,7},{6,4},{7,5},{8,10},{9,11},{10,... | collective-permute-start | bytes 1105928 | tf_op jit(solution)/shard_map/ppermute | solution.py:787
  270.7 12.1 %collective-permute-start.25 = (bf16[120,1536]{1,0:T(8,128)(2,1)S(1)}, bf16[120,1536]{1,0:T(8,128)(2,1)S(1)}, u32[]{:S(2)}, u32[]{:S(2)}) collective-permute-start(bf16[120,1536]{1,0:T(8,128)(2,1)S(1)} %bitcast.215), channel_id=1, source_target_pairs={{0,4},{4,8},{8,12},{12,0},{1,5},{5,9},{9,13},{13,1},{2,6},{6,10},{... | collective-permute-start | bytes 1105928 | tf_op jit(solution)/shard_map/ppermute | solution.py:776
  292.2 24.1 %collective-permute-start.26 = (bf16[4,2,120,1536]{3,2,0,1:T(8,128)(2,1)}, bf16[4,2,120,1536]{3,2,0,1:T(8,128)(2,1)}, u32[]{:S(2)}, u32[]{:S(2)}) collective-permute-start(bf16[4,2,120,1536]{3,2,0,1:T(8,128)(2,1)} %pad_maximum_fusion), channel_id=1, source_target_pairs={{0,1},{1,0},{2,3},{3,2},{4,5},{5,4},{6,7},{7,6},{8,9},{9,8},{10,11... | collective-permute-start | bytes 8847368 | tf_op jit(solution)/shard_map/ppermute | solution.py:787
  292.2 21.2 %collective-permute-start.27 = (bf16[1,1,120,1536]{3,2,1,0:T(8,128)(2,1)S(1)}, bf16[1,1,120,1536]{3,2,1,0:T(8,128)(2,1)}, u32[]{:S(2)}, u32[]{:S(2)}) collective-permute-start(bf16[1,1,120,1536]{3,2,1,0:T(8,128)(2,1)S(1)} %convert_bitcast_fusion.2), channel_id=1, source_target_pairs={{0,2},{1,3},{2,0},{3,1},{4,6},{5,7},{6,4},{7,5},{8,10},{9,11},{10,... | collective-permute-start | bytes 1105928 | tf_op jit(solution)/shard_map/ppermute | solution.py:787
  314.8 5.2 collective-permute-start.29
  372.7 25.4 %copy-start.22 = (f32[160,128]{1,0:T(8,128)S(1)}, f32[160,128]{1,0:T(8,128)}, u32[]{:S(2)}) copy-start(f32[160,128]{1,0:T(8,128)} %constant.193.clone.c_ref.refs_8_) | copy-start | bytes 245764
  372.7 25.4 %copy-start.24 = (f32[160,128]{1,0:T(8,128)S(1)}, f32[160,128]{1,0:T(8,128)}, u32[]{:S(2)}) copy-start(f32[160,128]{1,0:T(8,128)} %constant.194.clone.s_ref.refs_9_) | copy-start | bytes 245764
  372.8 46.1 %collective-permute-start.33 = (bf16[384,1536]{1,0:T(8,128)(2,1)}, bf16[384,1536]{1,0:T(8,128)(2,1)S(1)}, u32[]{:S(2)}, u32[]{:S(2)}) collective-permute-start(bf16[384,1536]{1,0:T(8,128)(2,1)} %get-tuple-element.244), channel_id=1, source_target_pairs={{0,16},{16,0},{1,17},{17,1},{2,18},{18,2},{3,19},{19,3},{4,20},{20... | collective-permute-start | bytes 3538952 | tf_op jit(solution)/shard_map/ppermute | solution.py:787
  374.5 10.5 %collective-permute-start.30 = (bf16[480,256]{1,0:T(8,128)(2,1)S(1)}, bf16[480,256]{1,0:T(8,128)(2,1)S(1)}, u32[]{:S(2)}, u32[]{:S(2)}) collective-permute-start(bf16[480,256]{1,0:T(8,128)(2,1)S(1)} %get-tuple-element.351), channel_id=1, source_target_pairs={{4,0},{8,4},{12,8},{5,1},{9,5},{13,9},{6,2},{10,6},{14,10},{7,3},{... | collective-permute-start | bytes 737288 | tf_op jit(solution)/shard_map/ppermute | solution.py:781
  375.8 22.2 %collective-permute-start.31 = (bf16[480,256]{1,0:T(8,128)(2,1)S(1)}, bf16[480,256]{1,0:T(8,128)(2,1)S(1)}, u32[]{:S(2)}, u32[]{:S(2)}) collective-permute-start(bf16[480,256]{1,0:T(8,128)(2,1)S(1)} %get-tuple-element.350), channel_id=1, source_target_pairs={{8,0},{12,4},{9,1},{13,5},{10,2},{14,6},{11,3},{15,7},{24,16},{28,... | collective-permute-start | bytes 737288 | tf_op jit(solution)/shard_map/ppermute | solution.py:781
  377.1 20.9 %collective-permute-start.32 = (bf16[480,256]{1,0:T(8,128)(2,1)S(1)}, bf16[480,256]{1,0:T(8,128)(2,1)S(1)}, u32[]{:S(2)}, u32[]{:S(2)}) collective-permute-start(bf16[480,256]{1,0:T(8,128)(2,1)S(1)} %get-tuple-element.349), channel_id=1, source_target_pairs={{12,0},{13,1},{14,2},{15,3},{28,16},{29,17},{30,18},{31,19}} | collective-permute-start | bytes 737288 | tf_op jit(solution)/shard_map/ppermute | solution.py:781
  402.2 22.3 %collective-permute-start.35 = (bf16[1,2,120,1536]{3,2,1,0:T(8,128)(2,1)}, bf16[1,2,120,1536]{3,2,1,0:T(8,128)(2,1)}, u32[]{:S(2)}, u32[]{:S(2)}) collective-permute-start(bf16[1,2,120,1536]{3,2,1,0:T(8,128)(2,1)} %bitcast.63), channel_id=1, source_target_pairs={{0,1},{1,0},{2,3},{3,2},{4,5},{5,4},{6,7},{7,6},{8,9},{9,8},{10,11... | collective-permute-start | bytes 2211848 | tf_op jit(solution)/shard_map/ppermute | solution.py:787
  420.2 31.3 %all-to-all-start = ((bf16[4,96,1536]{2,1,0:T(8,128)(2,1)}), bf16[4,96,1536]{2,1,0:T(8,128)(2,1)}, u32[]{:S(2)}, u32[]{:S(2)}) async-start(bf16[4,96,1536]{2,1,0:T(8,128)(2,1)} %bitcast.190), calls=%async_computation | async-start | bytes 2359296 | tf_op jit(solution)/shard_map/all_to_all | solution.py:931
  426.7 19.4 %collective-permute-start.36 = (bf16[1,1,120,1536]{3,2,1,0:T(8,128)(2,1)S(1)}, bf16[1,1,120,1536]{3,2,1,0:T(8,128)(2,1)}, u32[]{:S(2)}, u32[]{:S(2)}) collective-permute-start(bf16[1,1,120,1536]{3,2,1,0:T(8,128)(2,1)S(1)} %constant_dynamic-slice_fusion), channel_id=1, source_target_pairs={{0,2},{1,3},{2,0},{3,1},{4,6},{5,7},{6,4},{7,5},{8,10},{9,11},{10,... | collective-permute-start | bytes 1105928 | tf_op jit(solution)/shard_map/ppermute | solution.py:787
  428.7 55.2 %collective-permute-start.28 = (bf16[4,1,120,1536]{3,2,0,1:T(8,128)(2,1)}, bf16[4,1,120,1536]{3,2,0,1:T(8,128)(2,1)}, u32[]{:S(2)}, u32[]{:S(2)}) collective-permute-start(bf16[4,1,120,1536]{3,2,0,1:T(8,128)(2,1)} %constant_dynamic-slice_fusion.1), channel_id=1, source_target_pairs={{0,2},{1,3},{2,0},{3,1},{4,6},{5,7},{6,4},{7,5},{8,10},{9,11},{10,... | collective-permute-start | bytes 4423688 | tf_op jit(solution)/shard_map/ppermute | solution.py:787
  454.0 32.5 %all-to-all-start.1 = ((bf16[4,96,1536]{2,1,0:T(8,128)(2,1)}), bf16[4,96,1536]{2,1,0:T(8,128)(2,1)}, u32[]{:S(2)}, u32[]{:S(2)}) async-start(bf16[4,96,1536]{2,1,0:T(8,128)(2,1)} %broadcast_in_dim.116), calls=%async_computation.1 | async-start | bytes 2359296 | tf_op jit(solution)/shard_map/all_to_all | solution.py:931
  458.4 127.7 %all-gather.11.cloned.1.call-start = ((), (), s32[]{:S(2)}) async-start(), calls=%async_computation.8 | async-start | bytes 7077888 | tf_op jit(solution)/shard_map/all_gather | solution.py:906
  460.6 15.2 %collective-permute-start.41 = (bf16[1,1,128,1536]{3,2,1,0:T(8,128)(2,1)S(1)}, bf16[1,1,128,1536]{3,2,1,0:T(8,128)(2,1)}, u32[]{:S(2)}, u32[]{:S(2)}) collective-permute-start(bf16[1,1,128,1536]{3,2,1,0:T(8,128)(2,1)S(1)} %get-tuple-element.358), channel_id=1, source_target_pairs={{0,2},{1,3},{2,0},{3,1},{4,6},{5,7},{6,4},{7,5},{8,10},{9,11},{10,... | collective-permute-start | bytes 1179656 | tf_op jit(solution)/shard_map/ppermute | solution.py:787
  462.9 20.2 %collective-permute-start.34 = (bf16[128,1536]{1,0:T(8,128)(2,1)S(1)}, bf16[128,1536]{1,0:T(8,128)(2,1)S(1)}, u32[]{:S(2)}, u32[]{:S(2)}) collective-permute-start(bf16[128,1536]{1,0:T(8,128)(2,1)S(1)} %get-tuple-element.246), channel_id=1, source_target_pairs={{0,16},{16,0},{1,17},{17,1},{2,18},{18,2},{3,19},{19,3},{4,20},{20... | collective-permute-start | bytes 1179656 | tf_op jit(solution)/shard_map/ppermute | solution.py:787
  477.9 43.9 %collective-permute-start.43 = (bf16[1,2,128,1536]{3,2,1,0:T(8,128)(2,1)}, bf16[1,2,128,1536]{3,2,1,0:T(8,128)(2,1)}, u32[]{:S(2)}, u32[]{:S(2)}) collective-permute-start(bf16[1,2,128,1536]{3,2,1,0:T(8,128)(2,1)} %maximum_select_fusion.8), channel_id=1, source_target_pairs={{0,1},{1,0},{2,3},{3,2},{4,5},{5,4},{6,7},{7,6},{8,9},{9,8},{10,11... | collective-permute-start | bytes 2359304 | tf_op jit(solution)/shard_map/ppermute | solution.py:787
  486.5 15.9 %all-to-all-start.2 = ((bf16[4,32,1536]{2,1,0:T(8,128)(2,1)}), bf16[4,32,1536]{2,1,0:T(8,128)(2,1)S(1)}, u32[]{:S(2)}, u32[]{:S(2)}) async-start(bf16[4,32,1536]{2,1,0:T(8,128)(2,1)} %bitcast.75), calls=%async_computation.2 | async-start | bytes 786432 | tf_op jit(solution)/shard_map/all_to_all | solution.py:931
  493.3 32.0 %collective-permute-start.37 = (bf16[120,1536]{1,0:T(8,128)(2,1)}, bf16[120,1536]{1,0:T(8,128)(2,1)}, u32[]{:S(2)}, u32[]{:S(2)}) collective-permute-start(bf16[120,1536]{1,0:T(8,128)(2,1)} %get-tuple-element.338), channel_id=1, source_target_pairs={{0,12},{4,0},{8,4},{12,8},{1,13},{5,1},{9,5},{13,9},{2,14},{6,2},{... | collective-permute-start | bytes 1105928 | tf_op jit(solution)/shard_map/ppermute | solution.py:776
  497.1 41.3 %collective-permute-start.38 = (bf16[120,1536]{1,0:T(8,128)(2,1)}, bf16[120,1536]{1,0:T(8,128)(2,1)}, u32[]{:S(2)}, u32[]{:S(2)}) collective-permute-start(bf16[120,1536]{1,0:T(8,128)(2,1)} %get-tuple-element.340), channel_id=1, source_target_pairs={{0,8},{4,12},{8,0},{12,4},{1,9},{5,13},{9,1},{13,5},{2,10},{6,14},... | collective-permute-start | bytes 1105928 | tf_op jit(solution)/shard_map/ppermute | solution.py:776
  497.1 41.3 %collective-permute-start.39 = (bf16[120,1536]{1,0:T(8,128)(2,1)}, bf16[120,1536]{1,0:T(8,128)(2,1)}, u32[]{:S(2)}, u32[]{:S(2)}) collective-permute-start(bf16[120,1536]{1,0:T(8,128)(2,1)} %get-tuple-element.339), channel_id=1, source_target_pairs={{0,4},{4,8},{8,12},{12,0},{1,5},{5,9},{9,13},{13,1},{2,6},{6,10},{... | collective-permute-start | bytes 1105928 | tf_op jit(solution)/shard_map/ppermute | solution.py:776
  498.2 61.6 %collective-permute-start.42 = (bf16[384,1536]{1,0:T(8,128)(2,1)}, bf16[384,1536]{1,0:T(8,128)(2,1)}, u32[]{:S(2)}, u32[]{:S(2)}) collective-permute-start(bf16[384,1536]{1,0:T(8,128)(2,1)} %bitcast.74), channel_id=1, source_target_pairs={{0,16},{16,0},{1,17},{17,1},{2,18},{18,2},{3,19},{19,3},{4,20},{20... | collective-permute-start | bytes 3538952 | tf_op jit(solution)/shard_map/ppermute | solution.py:787
  503.3 41.1 %all-to-all-start.3 = ((bf16[4,32,1536]{2,1,0:T(8,128)(2,1)}), bf16[4,32,1536]{2,1,0:T(8,128)(2,1)}, u32[]{:S(2)}, u32[]{:S(2)}) async-start(bf16[4,32,1536]{2,1,0:T(8,128)(2,1)} %broadcast_in_dim.119), calls=%async_computation.3 | async-start | bytes 786432 | tf_op jit(solution)/shard_map/all_to_all | solution.py:931
  538.4 16.6 %collective-permute-start.44 = (f32[8,1536]{1,0:T(8,128)S(1)}, f32[8,1536]{1,0:T(8,128)S(1)}, u32[]{:S(2)}, u32[]{:S(2)}) collective-permute-start(f32[8,1536]{1,0:T(8,128)S(1)} %convert_reduce_fusion), channel_id=1, source_target_pairs={{0,16},{16,0},{1,17},{17,1},{2,18},{18,2},{3,19},{19,3},{4,20},{20... | collective-permute-start | bytes 147464 | tf_op jit(solution)/shard_map/ppermute | solution.py:787
  541.8 23.4 %collective-permute-start.40 = (bf16[1,1,120,1536]{3,2,1,0:T(8,128)(2,1)S(1)}, bf16[1,1,120,1536]{3,2,1,0:T(8,128)(2,1)S(1)}, u32[]{:S(2)}, u32[]{:S(2)}) collective-permute-start(bf16[1,1,120,1536]{3,2,1,0:T(8,128)(2,1)S(1)} %bitcast.196), channel_id=1, source_target_pairs={{0,2},{1,3},{2,0},{3,1},{4,6},{5,7},{6,4},{7,5},{8,10},{9,11},{10,... | collective-permute-start | bytes 1105928 | tf_op jit(solution)/shard_map/ppermute | solution.py:787
  544.4 26.5 %collective-permute-start.46 = (bf16[128,1536]{1,0:T(8,128)(2,1)}, bf16[128,1536]{1,0:T(8,128)(2,1)}, u32[]{:S(2)}, u32[]{:S(2)}) collective-permute-start(bf16[128,1536]{1,0:T(8,128)(2,1)} %bitcast.81), channel_id=1, source_target_pairs={{0,16},{16,0},{1,17},{17,1},{2,18},{18,2},{3,19},{19,3},{4,20},{20... | collective-permute-start | bytes 1179656 | tf_op jit(solution)/shard_map/ppermute | solution.py:787
  555.7 25.3 %all-to-all-start.4 = ((f32[4,8,1536]{2,1,0:T(8,128)}), f32[4,8,1536]{2,1,0:T(8,128)S(1)}, u32[]{:S(2)}, u32[]{:S(2)}) async-start(f32[4,8,1536]{2,1,0:T(8,128)} %broadcast_in_dim.120), calls=%async_computation.4 | async-start | bytes 393216 | tf_op jit(solution)/shard_map/all_to_all | solution.py:969
  566.2 17.2 %collective-permute-start.45 = (bf16[1,2,120,1536]{3,2,1,0:T(8,128)(2,1)}, bf16[1,2,120,1536]{3,2,1,0:T(8,128)(2,1)}, u32[]{:S(2)}, u32[]{:S(2)}) collective-permute-start(bf16[1,2,120,1536]{3,2,1,0:T(8,128)(2,1)} %maximum_select_fusion.14), channel_id=1, source_target_pairs={{0,1},{1,0},{2,3},{3,2},{4,5},{5,4},{6,7},{7,6},{8,9},{9,8},{10,11... | collective-permute-start | bytes 2211848 | tf_op jit(solution)/shard_map/ppermute | solution.py:787
  (51 other events, 440.5 us)
Sparse Core Ops, SparseCore 0:
  12.6 135.4 all-gather.4
Sparse Core Ops, SparseCore 1:
  180.0 75.1 all-gather.6
  372.8 112.8 all-gather.8
  487.1 95.8 all-gather.10

commit v3 on v2

--- a/solution.py
+++ b/solution.py
@@ -897,7 +897,7 @@
         self.done = 0
 
     def add(self, grads):
-        self.waiting.append(self.line.mark(grads))
+        self.waiting.append(grads)
         if self.flying is None:
             self.begin()
 
@@ -1186,6 +1186,7 @@
     pieces = [pieces[0]] + [slide(pieces[k], "expert", -k) for k in range(1, devices)]
     outer_sum = AllSum(line, *split)
     first_grads = line.mark(weight_grads(0, split_count))
+    outer_sum.step(line)
     pieces = line.take(pieces)
     line.mark(pieces[1])
     exchange.add(first_grads)
@@ -1195,7 +1196,6 @@
     )
     line.mark(pair_kept)
     summing = Summing(line, split=[h[None] for h in split])
-    outer_sum.step(line)
     pair_sum = AllSum(line, pair_kept, pair_sent)
     summing.step(line)
     last_grads = line.mark(weight_grads(split_count, half - split_count))

time: 609 us -> 608 us (level)
  starting transfers between devices: 115 us -> 97.3 us
  local copies, waits for them, and re-layouts: 32.1 us -> 46.9 us
    all_to_all x4, waiting for transfers between devices: 6.57 us -> 33.1 us  [spread(): return lax.all_to_all(blocks, 'expert', split_axis=0, concat_axis=0)]
    all_gather x2, waiting for transfers between devices: 1.82 us -> 21.7 us  [begin(): self.flying = lax.all_gather(grads, 'dp', axis=0, tiled=True)]
    ppermute x6, waiting for transfers between devices: 33.8 us -> 14.2 us  [slide(): lax.ppermute(values, axis, [(i, i + places) for i in range(size) if 0 <=...]
    ppermute x9, waiting for transfers between devices: 62.8 us -> 50.3 us  [shift(): lax.ppermute(values, axis, [(i, (i + places) % size) for i in range(size)])]
    unnamed x123 -> x149, local copies, waits for them, and re-layouts: 16.3 us -> 28.1 us
    all_to_all x4, starting transfers between devices: 30.8 us -> 20.4 us  [spread(): return lax.all_to_all(blocks, 'expert', split_axis=0, concat_axis=0)]
    ppermute x32, waiting for transfers between devices: 76.9 us -> 68.4 us  [swap(): lax.ppermute(values, axis, [(i, i ^ bit) for i in range(lax.axis_size(axi...]
    ppermute x32, starting transfers between devices: 29.4 us -> 21.2 us  [swap(): lax.ppermute(values, axis, [(i, i ^ bit) for i in range(lax.axis_size(axi...]
  transfers between devices with their start and end apart: 56 -> 56, of which waited for: 23 -> 20; matrix products, arithmetic and copies ran while one was open for 14% -> 14% of each run, Pallas kernels for 21% -> 26%
where the time goes in v3:
time: 608 us; the launch traced here: 600 us
  waiting for transfers between devices  188 us (31%)
  Pallas kernels  186 us (31%)
  starting transfers between devices  97.3 us (16%)
  other arithmetic  57.2 us (9%)
  local copies, waits for them, and re-layouts  46.9 us (8%)
  between operations  17.2 us (3%)
  matrix products  8.26 us (1%)
    ppermute x32, waiting for transfers between devices, swap(): lax.ppermute(values, axis, [(i, i ^ bit) for i in range(lax.axis_size(axi...  68.4 us
    pallas_call x4, Pallas kernels, experts_main(): pl.pallas_call(functools.partial(main_kernel, all_experts), grid_spec=plt...  63.2 us
    ppermute x9, waiting for transfers between devices, shift(): lax.ppermute(values, axis, [(i, (i + places) % size) for i in range(size)])  50.3 us
    pallas_call x2, Pallas kernels, experts_weights(): pl.pallas_call(functools.partial(weights_kernel, [g[3:] for g in groups],...  46.2 us
    ppermute x9, starting transfers between devices, shift(): lax.ppermute(values, axis, [(i, (i + places) % size) for i in range(size)])  35.7 us
    all_to_all x4, waiting for transfers between devices, spread(): return lax.all_to_all(blocks, 'expert', split_axis=0, concat_axis=0)  33.1 us
    unnamed x149, local copies, waits for them, and re-layouts  28.1 us
    pallas_call x1, Pallas kernels, attention_backward(): pl.pallas_call(functools.partial(attention_back_kernel, groups, heads), g...  22.2 us
  transfers between devices with their start and end apart: 56, of which 20 were waited for; matrix products, arithmetic and copies ran while one was open for 14% of the time, Pallas kernels for 26%

profile of v3, /device:TPU:0, one launch (start us, length us, event | category | flops | bytes accessed | tf_op | source)
XLA Modules:
  0.0 600.5 jit_solution(317890734866102084)
XLA Ops:
  13.8 2.4 project_key_value.1
  16.3 5.7 collective-permute-start
  21.9 4.5 collective-permute-start.1
  26.4 2.0 collective-permute-start.2
  31.6 9.7 %collective-permute-done.1 = bf16[480,256]{1,0:T(8,128)(2,1)} collective-permute-done((bf16[480,256]{1,0:T(8,128)(2,1)}, bf16[480,256]{1,0:T(8,128)(2,1)}, u32[]{:S(2)}, u32[]{:S(2)}) %collective-permute-start.1) | collective-permute-done | bytes 245792 | tf_op jit(solution)/shard_map/ppermute | solution.py:781
  41.3 4.5 collective-permute-done.2
  49.7 9.8 %attention_forward.1 = (bf16[480,384]{1,0:T(8,128)(2,1)S(1)}, f32[480,128]{1,0:T(8,128)S(1)}, bf16[2,120,1536]{2,1,0:T(8,128)(2,1)S(1)}, bf16[2,120,1536]{2,1,0:T(8,128)(2,1)}) custom-call(s32[3,8]{1,0:T(4,128)S(1)} %get-tuple-element.156.info_ref, s32[5]{0:T(128)S(1)} %stack.215.place_ref, bf16[480,384]{1,0:T(8,128)(2,1)S(1)} %project_query.1.q_ref, ...), custom_call_target="tpu_custom_call" | custom-call | flops 1000 | bytes 1000 | tf_op jit(solution)/shard_map/attention_forward/pallas_call | solution.py:668
  61.8 2.6 collective-permute-done.3
  67.5 9.1 %collective-permute-done.4 = bf16[1,1,120,1536]{3,2,1,0:T(8,128)(2,1)S(1)} collective-permute-done((bf16[1,1,120,1536]{3,2,1,0:T(8,128)(2,1)S(1)}, bf16[1,1,120,1536]{3,2,1,0:T(8,128)(2,1)S(1)}, u32[]{:S(2)}, u32[]{:S(2)}) %collective-permute-start.4) | collective-permute-done | bytes 368672 | tf_op jit(solution)/shard_map/ppermute | solution.py:787
  77.1 6.9 %collective-permute-start.6 = (bf16[120,1536]{1,0:T(8,128)(2,1)S(1)}, bf16[120,1536]{1,0:T(8,128)(2,1)S(1)}, u32[]{:S(2)}, u32[]{:S(2)}) collective-permute-start(bf16[120,1536]{1,0:T(8,128)(2,1)S(1)} %multiply_convert_fusion), channel_id=1, source_target_pairs={{0,4},{4,8},{8,12},{12,0},{1,5},{5,9},{9,13},{13,1},{2,6},{6,10},{... | collective-permute-start | bytes 1105928 | tf_op jit(solution)/shard_map/ppermute | solution.py:776
  85.6 17.8 %collective-permute-done.6 = bf16[120,1536]{1,0:T(8,128)(2,1)S(1)} collective-permute-done((bf16[120,1536]{1,0:T(8,128)(2,1)S(1)}, bf16[120,1536]{1,0:T(8,128)(2,1)S(1)}, u32[]{:S(2)}, u32[]{:S(2)}) %collective-permute-start.6) | collective-permute-done | bytes 368672 | tf_op jit(solution)/shard_map/ppermute | solution.py:776
  105.3 9.1 %collective-permute-start.8 = (bf16[120,1536]{1,0:T(8,128)(2,1)S(1)}, bf16[120,1536]{1,0:T(8,128)(2,1)}, u32[]{:S(2)}, u32[]{:S(2)}) collective-permute-start(bf16[120,1536]{1,0:T(8,128)(2,1)S(1)} %multiply_convert_fusion), channel_id=1, source_target_pairs={{0,8},{4,12},{8,0},{12,4},{1,9},{5,13},{9,1},{13,5},{2,10},{6,14},... | collective-permute-start | bytes 1105928 | tf_op jit(solution)/shard_map/ppermute | solution.py:776
  114.4 3.8 collective-permute-start.9
  121.8 15.4 %experts_main.4 = (bf16[480,1280]{1,0:T(8,128)(2,1)S(1)}, bf16[480,2560]{1,0:T(8,128)(2,1)}, bf16[2,120,1536]{2,1,0:T(8,128)(2,1)S(1)}, bf16[2,120,1536]{2,1,0:T(8,128)(2,1)}) custom-call(s32[5]{0:T(128)S(1)} %stack.215.place_ref, bf16[480,1536]{1,0:T(8,128)(2,1)S(1)} %bitcast.168, bf16[480,1536]{1,0:T(8,128)(2,1)S(1)} %copy-done.17, ...), custom_call_target="tpu_custom_call" | custom-call | flops 1000 | bytes 1000 | tf_op jit(solution)/shard_map/experts_main/pallas_call | solution.py:146
  138.4 6.0 %collective-permute-done.8 = bf16[120,1536]{1,0:T(8,128)(2,1)} collective-permute-done((bf16[120,1536]{1,0:T(8,128)(2,1)S(1)}, bf16[120,1536]{1,0:T(8,128)(2,1)}, u32[]{:S(2)}, u32[]{:S(2)}) %collective-permute-start.8) | collective-permute-done | bytes 368672 | tf_op jit(solution)/shard_map/ppermute | solution.py:776
  144.6 2.4 fusion.20
  150.3 15.8 %experts_main.5 = (bf16[480,1280]{1,0:T(8,128)(2,1)S(1)}, bf16[480,2560]{1,0:T(8,128)(2,1)}, bf16[2,120,1536]{2,1,0:T(8,128)(2,1)S(1)}, bf16[2,120,1536]{2,1,0:T(8,128)(2,1)S(1)}) custom-call(s32[5]{0:T(128)S(1)} %stack.233.place_ref, bf16[480,1536]{1,0:T(8,128)(2,1)S(1)} %bitcast.171, bf16[3840,1664]{1,0:T(8,128)(2,1)} %all-gather.5.cloned.1.call-done.c_ref.g_ref.refs_8_, ...), custom_call_target="tpu_custom_call" | custom-call | flops 1000 | bytes 1000 | tf_op jit(solution)/shard_map/experts_main/pallas_call | solution.py:146
  168.5 3.2 maximum_select_fusion.4
  172.2 6.2 %collective-permute-done.17 = bf16[1,1,120,1536]{3,2,1,0:T(8,128)(2,1)S(1)} collective-permute-done((bf16[1,1,120,1536]{3,2,1,0:T(8,128)(2,1)S(1)}, bf16[1,1,120,1536]{3,2,1,0:T(8,128)(2,1)S(1)}, u32[]{:S(2)}, u32[]{:S(2)}) %collective-permute-start.17) | collective-permute-done | bytes 368672 | tf_op jit(solution)/shard_map/ppermute | solution.py:787
  181.4 7.4 %collective-permute-done.18 = bf16[1,1,120,1536]{3,2,1,0:T(8,128)(2,1)} collective-permute-done((bf16[1,1,120,1536]{3,2,1,0:T(8,128)(2,1)S(1)}, bf16[1,1,120,1536]{3,2,1,0:T(8,128)(2,1)}, u32[]{:S(2)}, u32[]{:S(2)}) %collective-permute-start.18) | collective-permute-done | bytes 368672 | tf_op jit(solution)/shard_map/ppermute | solution.py:787
  189.8 9.9 %collective-permute-start.19 = (bf16[120,1536]{1,0:T(8,128)(2,1)S(1)}, bf16[120,1536]{1,0:T(8,128)(2,1)S(1)}, u32[]{:S(2)}, u32[]{:S(2)}) collective-permute-start(bf16[120,1536]{1,0:T(8,128)(2,1)S(1)} %bitcast.214), channel_id=1, source_target_pairs={{0,12},{4,0},{8,4},{12,8},{1,13},{5,1},{9,5},{13,9},{2,14},{6,2},{... | collective-permute-start | bytes 1105928 | tf_op jit(solution)/shard_map/ppermute | solution.py:776
  199.7 2.3 maximum_select_fusion
  202.0 2.0 copy.118
  204.0 15.5 %experts_main.6 = (bf16[480,1280]{1,0:T(8,128)(2,1)S(1)}, bf16[480,2560]{1,0:T(8,128)(2,1)S(1)}, bf16[2,120,1536]{2,1,0:T(8,128)(2,1)S(1)}, bf16[2,120,1536]{2,1,0:T(8,128)(2,1)S(1)}) custom-call(s32[5]{0:T(128)S(1)} %stack.226.place_ref, bf16[960,1536]{1,0:T(8,128)(2,1)} %bitcast.177, bf16[3840,1664]{1,0:T(8,128)(2,1)} %all-gather.5.cloned.1.call-done.c_ref.g_ref.refs_8_, ...), custom_call_target="tpu_custom_call" | custom-call | flops 1000 | bytes 1000 | tf_op jit(solution)/shard_map/experts_main/pallas_call | solution.py:146
  222.0 16.5 %experts_main.7 = (bf16[480,1280]{1,0:T(8,128)(2,1)S(1)}, bf16[480,2560]{1,0:T(8,128)(2,1)S(1)}, bf16[2,120,1536]{2,1,0:T(8,128)(2,1)S(1)}, bf16[2,120,1536]{2,1,0:T(8,128)(2,1)S(1)}) custom-call(s32[5]{0:T(128)S(1)} %stack.251.place_ref, bf16[960,1536]{1,0:T(8,128)(2,1)} %bitcast.178, bf16[3840,1664]{1,0:T(8,128)(2,1)} %all-gather.5.cloned.1.call-done.c_ref.g_ref.refs_8_, ...), custom_call_target="tpu_custom_call" | custom-call | flops 1000 | bytes 1000 | tf_op jit(solution)/shard_map/experts_main/pallas_call | solution.py:146
  241.4 2.1 convolution_convert_fusion.3
  243.5 8.0 %collective-permute-done.22 = bf16[1,1,120,1536]{3,2,1,0:T(8,128)(2,1)S(1)} collective-permute-done((bf16[1,1,120,1536]{3,2,1,0:T(8,128)(2,1)S(1)}, bf16[1,1,120,1536]{3,2,1,0:T(8,128)(2,1)S(1)}, u32[]{:S(2)}, u32[]{:S(2)}) %collective-permute-start.22) | collective-permute-done | bytes 368672 | tf_op jit(solution)/shard_map/ppermute | solution.py:787
  252.9 2.1 convolution_convert_fusion.2
  255.0 14.5 %collective-permute-done.24 = bf16[120,1536]{1,0:T(8,128)(2,1)S(1)} collective-permute-done((bf16[120,1536]{1,0:T(8,128)(2,1)S(1)}, bf16[120,1536]{1,0:T(8,128)(2,1)S(1)}, u32[]{:S(2)}, u32[]{:S(2)}) %collective-permute-start.24) | collective-permute-done | bytes 368672 | tf_op jit(solution)/shard_map/ppermute | solution.py:776
  269.6 2.1 convolution_convert_fusion.1
  271.7 10.2 %collective-permute-done.25 = bf16[120,1536]{1,0:T(8,128)(2,1)S(1)} collective-permute-done((bf16[120,1536]{1,0:T(8,128)(2,1)S(1)}, bf16[120,1536]{1,0:T(8,128)(2,1)S(1)}, u32[]{:S(2)}, u32[]{:S(2)}) %collective-permute-start.25) | collective-permute-done | bytes 368672 | tf_op jit(solution)/shard_map/ppermute | solution.py:776
  282.4 2.2 convert_bitcast_fusion.1
  284.7 2.1 convolution_convert_fusion
  289.2 2.2 pad_maximum_fusion
  291.8 20.9 %experts_other.1 = (bf16[1920,640]{1,0:T(8,128)(2,1)}, bf16[1920,1280]{1,0:T(8,128)(2,1)}) custom-call(s32[5]{0:T(128)} %copy-done.48, bf16[1920,1536]{1,0:T(8,128)(2,1)} %all-gather.7.cloned.1.call-done.x_ref.refs_4_.refs_5_.refs_6_.refs_7_, bf16[3840,1664]{1,0:T(8,128)(2,1)} %all-gather.5.cloned.1.call-done.c_ref.g_ref.refs_8_, ...), custom_call_target="tpu_custom_call" | custom-call | flops 1000 | bytes 1000 | tf_op jit(solution)/shard_map/experts_other/pallas_call | solution.py:185
  315.6 2.2 add_convert_fusion
  320.7 22.2 %attention_backward.1 = (bf16[480,384]{1,0:T(8,128)(2,1)}, bf16[1920,256]{1,0:T(8,128)(2,1)}, bf16[384,1536]{1,0:T(8,128)(2,1)}, bf16[384,1536]{1,0:T(8,128)(2,1)}) custom-call(s32[3,8]{1,0:T(4,128)} %copy-done.46, s32[5]{0:T(128)} %copy-done.48, bf16[480,384]{1,0:T(8,128)(2,1)} %copy-done.18, bf16[1920,256]{1,0:T(8,128)(2,1)} %copy-done.7, ...), custom_call_target="tpu_custom_call" | custom-call | flops 1000 | bytes 1000 | tf_op jit(solution)/shard_map/attention_backward/pallas_call | solution.py:713
  344.5 2.3 fusion.30
  350.9 29.2 %experts_weights.2 = bf16[3,2304,256]{2,1,0:T(8,128)(2,1)} custom-call(s32[5]{0:T(128)} %copy-done.48, bf16[480,1536]{1,0:T(8,128)(2,1)} %bitcast.169, bf16[480,1536]{1,0:T(8,128)(2,1)} %bitcast.172, bf16[960,1536]{1,0:T(8,128)(2,1)} %bitcast.179, bf16[960,1536]{1,0:T(8,128)(2,1)} %bitcast.180, ...), custom_call_target="tpu_custom_call" | custom-call | flops 1000 | bytes 1000 | tf_op jit(solution)/shard_map/experts_weights/pallas_call | solution.py:265
  380.0 2.6 add_convert_fusion.2
  391.8 4.0 project_backward.1
  398.3 7.3 %all-to-all-start = ((bf16[4,96,1536]{2,1,0:T(8,128)(2,1)}), bf16[4,96,1536]{2,1,0:T(8,128)(2,1)S(1)}, u32[]{:S(2)}, u32[]{:S(2)}) async-start(bf16[4,96,1536]{2,1,0:T(8,128)(2,1)} %bitcast.190), calls=%async_computation | async-start | bytes 2359296 | tf_op jit(solution)/shard_map/all_to_all | solution.py:931
  410.7 17.1 %experts_weights.3 = bf16[2,2304,256]{2,1,0:T(8,128)(2,1)} custom-call(s32[5]{0:T(128)} %copy-done.48, bf16[480,1536]{1,0:T(8,128)(2,1)} %bitcast.170, bf16[480,1536]{1,0:T(8,128)(2,1)} %bitcast.173, bf16[960,1536]{1,0:T(8,128)(2,1)} %bitcast.181, bf16[960,1536]{1,0:T(8,128)(2,1)} %bitcast.182, ...), custom_call_target="tpu_custom_call" | custom-call | flops 1000 | bytes 1000 | tf_op jit(solution)/shard_map/experts_weights/pallas_call | solution.py:265
  427.8 2.1 fusion.13
  429.9 4.7 all-to-all-done
  435.9 4.4 all-to-all-start.1
  442.9 16.4 %collective-permute-done.41 = bf16[1,1,128,1536]{3,2,1,0:T(8,128)(2,1)S(1)} collective-permute-done((bf16[1,1,128,1536]{3,2,1,0:T(8,128)(2,1)S(1)}, bf16[1,1,128,1536]{3,2,1,0:T(8,128)(2,1)S(1)}, u32[]{:S(2)}, u32[]{:S(2)}) %collective-permute-start.41) | collective-permute-done | bytes 393248 | tf_op jit(solution)/shard_map/ppermute | solution.py:787
  463.2 21.7 %all-gather.9.cloned.1.call-done.source = bf16[6,2304,256]{2,1,0:T(8,128)(2,1)} async-done(((bf16[3,2304,256]{2,1,0:T(8,128)(2,1)}), bf16[6,2304,256]{2,1,0:T(8,128)(2,1)}) %all-gather.9.cloned.1.call-update) | async-done | bytes 7077904 | tf_op jit(solution)/shard_map/all_gather | solution.py:906
  485.0 4.6 all-to-all-start.2
  489.6 2.2 fusion
  492.8 2.0 collective-permute-start.39
  494.8 2.4 collective-permute-start.38
  499.2 18.8 %all-to-all-done.2 = bf16[4,32,1536]{2,1,0:T(8,128)(2,1)S(1)} async-done(((bf16[4,32,1536]{2,1,0:T(8,128)(2,1)}), bf16[4,32,1536]{2,1,0:T(8,128)(2,1)S(1)}, u32[]{:S(2)}, u32[]{:S(2)}) %all-to-all-start.2) | async-done | bytes 393248 | tf_op jit(solution)/shard_map/all_to_all | solution.py:931
  518.8 4.1 all-to-all-start.3
  523.0 2.2 maximum_select_fusion.1
  531.8 9.6 %all-to-all-done.3 = bf16[4,32,1536]{2,1,0:T(8,128)(2,1)} async-done(((bf16[4,32,1536]{2,1,0:T(8,128)(2,1)}), bf16[4,32,1536]{2,1,0:T(8,128)(2,1)}, u32[]{:S(2)}, u32[]{:S(2)}) %all-to-all-start.3) | async-done | bytes 393248 | tf_op jit(solution)/shard_map/all_to_all | solution.py:931
  541.9 13.1 %collective-permute-done.44 = f32[8,1536]{1,0:T(8,128)S(1)} collective-permute-done((f32[8,1536]{1,0:T(8,128)S(1)}, f32[8,1536]{1,0:T(8,128)S(1)}, u32[]{:S(2)}, u32[]{:S(2)}) %collective-permute-start.44) | collective-permute-done | bytes 49184 | tf_op jit(solution)/shard_map/ppermute | solution.py:787
  555.7 3.6 all-to-all-start.4
  559.3 3.3 convert_bitcast_fusion
  562.6 1.9 copy.130
  566.6 4.5 collective-permute-done.46
  572.3 8.9 %finish_weights.2 = (f32[10,1536,256]{2,1,0:T(8,128)}, f32[10,128,1536]{2,1,0:T(8,128)}) custom-call(bf16[6,2304,256]{2,1,0:T(8,128)(2,1)} %all-gather.9.cloned.1.call-done.source), custom_call_target="tpu_custom_call" | custom-call | flops 1000 | bytes 1000 | tf_op jit(solution)/shard_map/finish_weights/pallas_call | solution.py:305
  583.6 2.7 maximum_select_fusion.7
  586.3 6.4 %finish_weights.3 = (f32[10,1536,256]{2,1,0:T(8,128)}, f32[10,128,1536]{2,1,0:T(8,128)}) custom-call(bf16[4,2304,256]{2,1,0:T(8,128)(2,1)} %all-gather.11.cloned.1.call-done.source, f32[10,1536,256]{2,1,0:T(8,128)} %get-tuple-element.276.refs_0_, f32[10,128,1536]{2,1,0:T(8,128)} %get-tuple-element.272.refs_1_), custom_call_target="tpu_custom_call", output_to_operand_aliasing={{0}: (1, {}), {1}: (2, {})} | custom-call | flops 1000 | bytes 1000 | tf_op jit(solution)/shard_map/finish_weights/pallas_call | solution.py:305
  (318 shorter events, 100.1 us)
Async XLA Ops:
  8.0 142.3 %all-gather.5.cloned.1.call-start = ((), (), s32[]{:S(2)}) async-start(), calls=%async_computation.5 | async-start | bytes 13178880 | tf_op jit(solution)/shard_map/all_gather | solution.py:1036
  12.5 279.3 %all-gather.7.cloned.1.call-start = ((), (), s32[]{:S(2)}) async-start(), calls=%async_computation.6 | async-start | bytes 6266880 | tf_op jit(solution)/shard_map/all_gather | solution.py:1115
  16.3 33.4 %copy-start.46 = (s32[3,8]{1,0:T(4,128)}, s32[3,8]{1,0:T(4,128)S(1)}, u32[]{:S(2)}) copy-start(s32[3,8]{1,0:T(4,128)S(1)} %get-tuple-element.156.info_ref) | copy-start | bytes 292
  16.3 15.4 %collective-permute-start = (bf16[480,256]{1,0:T(8,128)(2,1)}, bf16[480,256]{1,0:T(8,128)(2,1)}, u32[]{:S(2)}, u32[]{:S(2)}) collective-permute-start(bf16[480,256]{1,0:T(8,128)(2,1)} %get-tuple-element.159), channel_id=1, source_target_pairs={{0,4},{4,8},{8,12},{1,5},{5,9},{9,13},{2,6},{6,10},{10,14},{3,7},{... | collective-permute-start | bytes 737288 | tf_op jit(solution)/shard_map/ppermute | solution.py:781
  21.9 19.4 %collective-permute-start.1 = (bf16[480,256]{1,0:T(8,128)(2,1)}, bf16[480,256]{1,0:T(8,128)(2,1)}, u32[]{:S(2)}, u32[]{:S(2)}) collective-permute-start(bf16[480,256]{1,0:T(8,128)(2,1)} %get-tuple-element.159), channel_id=1, source_target_pairs={{0,8},{4,12},{1,9},{5,13},{2,10},{6,14},{3,11},{7,15},{16,24},{20,... | collective-permute-start | bytes 737288 | tf_op jit(solution)/shard_map/ppermute | solution.py:781
  26.4 19.4 %collective-permute-start.2 = (bf16[480,256]{1,0:T(8,128)(2,1)}, bf16[480,256]{1,0:T(8,128)(2,1)}, u32[]{:S(2)}, u32[]{:S(2)}) collective-permute-start(bf16[480,256]{1,0:T(8,128)(2,1)} %get-tuple-element.159), channel_id=1, source_target_pairs={{0,12},{1,13},{2,14},{3,15},{16,28},{17,29},{18,30},{19,31}} | collective-permute-start | bytes 737288 | tf_op jit(solution)/shard_map/ppermute | solution.py:781
  31.5 28.0 %copy-start.18 = (bf16[480,384]{1,0:T(8,128)(2,1)}, bf16[480,384]{1,0:T(8,128)(2,1)S(1)}, u32[]{:S(2)}) copy-start(bf16[480,384]{1,0:T(8,128)(2,1)S(1)} %project_query.1.q_ref) | copy-start | bytes 1105924
  31.6 88.6 %copy-start.48 = (s32[5]{0:T(128)}, s32[5]{0:T(128)S(1)}, u32[]{:S(2)}) copy-start(s32[5]{0:T(128)S(1)} %stack.215.place_ref) | copy-start | bytes 64
  61.8 2.6 collective-permute-start.3
  66.0 10.7 %collective-permute-start.4 = (bf16[1,1,120,1536]{3,2,1,0:T(8,128)(2,1)S(1)}, bf16[1,1,120,1536]{3,2,1,0:T(8,128)(2,1)S(1)}, u32[]{:S(2)}, u32[]{:S(2)}) collective-permute-start(bf16[1,1,120,1536]{3,2,1,0:T(8,128)(2,1)S(1)} %constant_dynamic-slice_fusion.8), channel_id=1, source_target_pairs={{0,2},{1,3},{2,0},{3,1},{4,6},{5,7},{6,4},{7,5},{8,10},{9,11},{10,... | collective-permute-start | bytes 1105928 | tf_op jit(solution)/shard_map/ppermute | solution.py:787
  77.0 43.0 %copy-start.56 = (bf16[120,1536]{1,0:T(8,128)(2,1)}, bf16[120,1536]{1,0:T(8,128)(2,1)S(1)}, u32[]{:S(2)}) copy-start(bf16[120,1536]{1,0:T(8,128)(2,1)S(1)} %get-tuple-element.335) | copy-start | bytes 1105924
  77.1 26.3 %collective-permute-start.6 = (bf16[120,1536]{1,0:T(8,128)(2,1)S(1)}, bf16[120,1536]{1,0:T(8,128)(2,1)S(1)}, u32[]{:S(2)}, u32[]{:S(2)}) collective-permute-start(bf16[120,1536]{1,0:T(8,128)(2,1)S(1)} %multiply_convert_fusion), channel_id=1, source_target_pairs={{0,4},{4,8},{8,12},{12,0},{1,5},{5,9},{9,13},{13,1},{2,6},{6,10},{... | collective-permute-start | bytes 1105928 | tf_op jit(solution)/shard_map/ppermute | solution.py:776
  84.0 19.4 %collective-permute-start.5 = (bf16[1,1,120,1536]{3,2,1,0:T(8,128)(2,1)S(1)}, bf16[1,1,120,1536]{3,2,1,0:T(8,128)(2,1)S(1)}, u32[]{:S(2)}, u32[]{:S(2)}) collective-permute-start(bf16[1,1,120,1536]{3,2,1,0:T(8,128)(2,1)S(1)} %bitcast.193), channel_id=1, source_target_pairs={{0,2},{1,3},{2,0},{3,1},{4,6},{5,7},{6,4},{7,5},{8,10},{9,11},{10,... | collective-permute-start | bytes 1105928 | tf_op jit(solution)/shard_map/ppermute | solution.py:787
  103.5 16.4 %collective-permute-start.7 = (bf16[1,2,120,1536]{3,2,1,0:T(8,128)(2,1)S(1)}, bf16[1,2,120,1536]{3,2,1,0:T(8,128)(2,1)S(1)}, u32[]{:S(2)}, u32[]{:S(2)}) collective-permute-start(bf16[1,2,120,1536]{3,2,1,0:T(8,128)(2,1)S(1)} %maximum_select_fusion.10), channel_id=1, source_target_pairs={{0,1},{1,0},{2,3},{3,2},{4,5},{5,4},{6,7},{7,6},{8,9},{9,8},{10,11... | collective-permute-start | bytes 2211848 | tf_op jit(solution)/shard_map/ppermute | solution.py:787
  103.6 33.6 %collective-permute-start.11 = (bf16[120,1536]{1,0:T(8,128)(2,1)S(1)}, bf16[120,1536]{1,0:T(8,128)(2,1)}, u32[]{:S(2)}, u32[]{:S(2)}) collective-permute-start(bf16[120,1536]{1,0:T(8,128)(2,1)S(1)} %multiply_convert_fusion), channel_id=1, source_target_pairs={{0,16},{16,0},{1,17},{17,1},{2,18},{18,2},{3,19},{19,3},{4,20},{20... | collective-permute-start | bytes 1105928 | tf_op jit(solution)/shard_map/ppermute | solution.py:787
  105.3 39.2 %collective-permute-start.8 = (bf16[120,1536]{1,0:T(8,128)(2,1)S(1)}, bf16[120,1536]{1,0:T(8,128)(2,1)}, u32[]{:S(2)}, u32[]{:S(2)}) collective-permute-start(bf16[120,1536]{1,0:T(8,128)(2,1)S(1)} %multiply_convert_fusion), channel_id=1, source_target_pairs={{0,8},{4,12},{8,0},{12,4},{1,9},{5,13},{9,1},{13,5},{2,10},{6,14},... | collective-permute-start | bytes 1105928 | tf_op jit(solution)/shard_map/ppermute | solution.py:776
  114.4 30.1 %collective-permute-start.9 = (bf16[120,1536]{1,0:T(8,128)(2,1)S(1)}, bf16[120,1536]{1,0:T(8,128)(2,1)}, u32[]{:S(2)}, u32[]{:S(2)}) collective-permute-start(bf16[120,1536]{1,0:T(8,128)(2,1)S(1)} %multiply_convert_fusion), channel_id=1, source_target_pairs={{0,12},{4,0},{8,4},{12,8},{1,13},{5,1},{9,5},{13,9},{2,14},{6,2},{... | collective-permute-start | bytes 1105928 | tf_op jit(solution)/shard_map/ppermute | solution.py:776
  118.2 19.0 %collective-permute-start.10 = (bf16[1,1,120,1536]{3,2,1,0:T(8,128)(2,1)S(1)}, bf16[1,1,120,1536]{3,2,1,0:T(8,128)(2,1)S(1)}, u32[]{:S(2)}, u32[]{:S(2)}) collective-permute-start(bf16[1,1,120,1536]{3,2,1,0:T(8,128)(2,1)S(1)} %bitcast.206), channel_id=1, source_target_pairs={{0,2},{1,3},{2,0},{3,1},{4,6},{5,7},{6,4},{7,5},{8,10},{9,11},{10,... | collective-permute-start | bytes 1105928 | tf_op jit(solution)/shard_map/ppermute | solution.py:787
  137.2 104.2 %copy-start.8 = (bf16[480,1280]{1,0:T(8,128)(2,1)}, bf16[480,1280]{1,0:T(8,128)(2,1)S(1)}, u32[]{:S(2)}) copy-start(bf16[480,1280]{1,0:T(8,128)(2,1)S(1)} %get-tuple-element.201.refs_17_) | copy-start | bytes 3686404
  138.4 10.2 %collective-permute-start.14 = (bf16[1,2,120,1536]{3,2,1,0:T(8,128)(2,1)}, bf16[1,2,120,1536]{3,2,1,0:T(8,128)(2,1)}, u32[]{:S(2)}, u32[]{:S(2)}) collective-permute-start(bf16[1,2,120,1536]{3,2,1,0:T(8,128)(2,1)} %maximum_select_fusion.11), channel_id=1, source_target_pairs={{0,1},{1,0},{2,3},{3,2},{4,5},{5,4},{6,7},{7,6},{8,9},{9,8},{10,11... | collective-permute-start | bytes 2211848 | tf_op jit(solution)/shard_map/ppermute | solution.py:787
  144.5 21.6 %collective-permute-start.13 = (bf16[1,2,120,1536]{3,2,1,0:T(8,128)(2,1)}, bf16[1,2,120,1536]{3,2,1,0:T(8,128)(2,1)}, u32[]{:S(2)}, u32[]{:S(2)}) collective-permute-start(bf16[1,2,120,1536]{3,2,1,0:T(8,128)(2,1)} %bitcast.20), channel_id=1, source_target_pairs={{0,1},{1,0},{2,3},{3,2},{4,5},{5,4},{6,7},{7,6},{8,9},{9,8},{10,11... | collective-permute-start | bytes 2211848 | tf_op jit(solution)/shard_map/ppermute | solution.py:787
  147.0 21.5 %collective-permute-start.12 = (bf16[2,1,120,1536]{3,2,0,1:T(8,128)(2,1)}, bf16[2,1,120,1536]{3,2,0,1:T(8,128)(2,1)}, u32[]{:S(2)}, u32[]{:S(2)}) collective-permute-start(bf16[2,1,120,1536]{3,2,0,1:T(8,128)(2,1)} %get-tuple-element.355), channel_id=1, source_target_pairs={{0,2},{1,3},{2,0},{3,1},{4,6},{5,7},{6,4},{7,5},{8,10},{9,11},{10,... | collective-permute-start | bytes 2211848 | tf_op jit(solution)/shard_map/ppermute | solution.py:787
  167.9 10.6 %collective-permute-start.17 = (bf16[1,1,120,1536]{3,2,1,0:T(8,128)(2,1)S(1)}, bf16[1,1,120,1536]{3,2,1,0:T(8,128)(2,1)S(1)}, u32[]{:S(2)}, u32[]{:S(2)}) collective-permute-start(bf16[1,1,120,1536]{3,2,1,0:T(8,128)(2,1)S(1)} %constant_dynamic-slice_fusion.5), channel_id=1, source_target_pairs={{0,2},{1,3},{2,0},{3,1},{4,6},{5,7},{6,4},{7,5},{8,10},{9,11},{10,... | collective-permute-start | bytes 1105928 | tf_op jit(solution)/shard_map/ppermute | solution.py:787
  168.5 10.1 %collective-permute-start.16 = (bf16[1,2,120,1536]{3,2,1,0:T(8,128)(2,1)S(1)}, bf16[1,2,120,1536]{3,2,1,0:T(8,128)(2,1)S(1)}, u32[]{:S(2)}, u32[]{:S(2)}) collective-permute-start(bf16[1,2,120,1536]{3,2,1,0:T(8,128)(2,1)S(1)} %bitcast.175), channel_id=1, source_target_pairs={{0,1},{1,0},{2,3},{3,2},{4,5},{5,4},{6,7},{7,6},{8,9},{9,8},{10,11... | collective-permute-start | bytes 2211848 | tf_op jit(solution)/shard_map/ppermute | solution.py:787
  171.7 28.0 %collective-permute-start.15 = (bf16[2,2,120,1536]{3,2,0,1:T(8,128)(2,1)}, bf16[2,2,120,1536]{3,2,0,1:T(8,128)(2,1)}, u32[]{:S(2)}, u32[]{:S(2)}) collective-permute-start(bf16[2,2,120,1536]{3,2,0,1:T(8,128)(2,1)} %maximum_select_fusion.4), channel_id=1, source_target_pairs={{0,1},{1,0},{2,3},{3,2},{4,5},{5,4},{6,7},{7,6},{8,9},{9,8},{10,11... | collective-permute-start | bytes 4423688 | tf_op jit(solution)/shard_map/ppermute | solution.py:787
  178.8 9.9 %collective-permute-start.18 = (bf16[1,1,120,1536]{3,2,1,0:T(8,128)(2,1)S(1)}, bf16[1,1,120,1536]{3,2,1,0:T(8,128)(2,1)}, u32[]{:S(2)}, u32[]{:S(2)}) collective-permute-start(bf16[1,1,120,1536]{3,2,1,0:T(8,128)(2,1)S(1)} %constant_dynamic-slice_fusion.4), channel_id=1, source_target_pairs={{0,2},{1,3},{2,0},{3,1},{4,6},{5,7},{6,4},{7,5},{8,10},{9,11},{10,... | collective-permute-start | bytes 1105928 | tf_op jit(solution)/shard_map/ppermute | solution.py:787
  179.6 305.4 %all-gather.9.cloned.1.call-start = ((), (), s32[]{:S(2)}) async-start(), calls=%async_computation.7 | async-start | bytes 10616832 | tf_op jit(solution)/shard_map/all_gather | solution.py:906
  189.8 32.1 %collective-permute-start.19 = (bf16[120,1536]{1,0:T(8,128)(2,1)S(1)}, bf16[120,1536]{1,0:T(8,128)(2,1)S(1)}, u32[]{:S(2)}, u32[]{:S(2)}) collective-permute-start(bf16[120,1536]{1,0:T(8,128)(2,1)S(1)} %bitcast.214), channel_id=1, source_target_pairs={{0,12},{4,0},{8,4},{12,8},{1,13},{5,1},{9,5},{13,9},{2,14},{6,2},{... | collective-permute-start | bytes 1105928 | tf_op jit(solution)/shard_map/ppermute | solution.py:776
  221.9 16.6 %collective-permute-start.20 = (bf16[1,2,120,1536]{3,2,1,0:T(8,128)(2,1)S(1)}, bf16[1,2,120,1536]{3,2,1,0:T(8,128)(2,1)}, u32[]{:S(2)}, u32[]{:S(2)}) collective-permute-start(bf16[1,2,120,1536]{3,2,1,0:T(8,128)(2,1)S(1)} %bitcast.174), channel_id=1, source_target_pairs={{0,1},{1,0},{2,3},{3,2},{4,5},{5,4},{6,7},{7,6},{8,9},{9,8},{10,11... | collective-permute-start | bytes 2211848 | tf_op jit(solution)/shard_map/ppermute | solution.py:787
  238.6 46.1 %copy-start.13 = (bf16[480,1280]{1,0:T(8,128)(2,1)}, bf16[480,1280]{1,0:T(8,128)(2,1)S(1)}, u32[]{:S(2)}) copy-start(bf16[480,1280]{1,0:T(8,128)(2,1)S(1)} %get-tuple-element.216.refs_20_) | copy-start | bytes 3686404
  240.5 10.9 %collective-permute-start.22 = (bf16[1,1,120,1536]{3,2,1,0:T(8,128)(2,1)S(1)}, bf16[1,1,120,1536]{3,2,1,0:T(8,128)(2,1)S(1)}, u32[]{:S(2)}, u32[]{:S(2)}) collective-permute-start(bf16[1,1,120,1536]{3,2,1,0:T(8,128)(2,1)S(1)} %constant_dynamic-slice_fusion.3), channel_id=1, source_target_pairs={{0,2},{1,3},{2,0},{3,1},{4,6},{5,7},{6,4},{7,5},{8,10},{9,11},{10,... | collective-permute-start | bytes 1105928 | tf_op jit(solution)/shard_map/ppermute | solution.py:787
  241.2 10.4 %collective-permute-start.21 = (bf16[1,2,120,1536]{3,2,1,0:T(8,128)(2,1)S(1)}, bf16[1,2,120,1536]{3,2,1,0:T(8,128)(2,1)S(1)}, u32[]{:S(2)}, u32[]{:S(2)}) collective-permute-start(bf16[1,2,120,1536]{3,2,1,0:T(8,128)(2,1)S(1)} %bitcast.176), channel_id=1, source_target_pairs={{0,1},{1,0},{2,3},{3,2},{4,5},{5,4},{6,7},{7,6},{8,9},{9,8},{10,11... | collective-permute-start | bytes 2211848 | tf_op jit(solution)/shard_map/ppermute | solution.py:787
  251.5 17.9 %collective-permute-start.24 = (bf16[120,1536]{1,0:T(8,128)(2,1)S(1)}, bf16[120,1536]{1,0:T(8,128)(2,1)S(1)}, u32[]{:S(2)}, u32[]{:S(2)}) collective-permute-start(bf16[120,1536]{1,0:T(8,128)(2,1)S(1)} %bitcast.215), channel_id=1, source_target_pairs={{0,8},{4,12},{8,0},{12,4},{1,9},{5,13},{9,1},{13,5},{2,10},{6,14},... | collective-permute-start | bytes 1105928 | tf_op jit(solution)/shard_map/ppermute | solution.py:776
  251.8 17.6 %collective-permute-start.23 = (bf16[1,1,120,1536]{3,2,1,0:T(8,128)(2,1)S(1)}, bf16[1,1,120,1536]{3,2,1,0:T(8,128)(2,1)S(1)}, u32[]{:S(2)}, u32[]{:S(2)}) collective-permute-start(bf16[1,1,120,1536]{3,2,1,0:T(8,128)(2,1)S(1)} %constant_dynamic-slice_fusion.2), channel_id=1, source_target_pairs={{0,2},{1,3},{2,0},{3,1},{4,6},{5,7},{6,4},{7,5},{8,10},{9,11},{10,... | collective-permute-start | bytes 1105928 | tf_op jit(solution)/shard_map/ppermute | solution.py:787
  269.6 12.4 %collective-permute-start.25 = (bf16[120,1536]{1,0:T(8,128)(2,1)S(1)}, bf16[120,1536]{1,0:T(8,128)(2,1)S(1)}, u32[]{:S(2)}, u32[]{:S(2)}) collective-permute-start(bf16[120,1536]{1,0:T(8,128)(2,1)S(1)} %bitcast.216), channel_id=1, source_target_pairs={{0,4},{4,8},{8,12},{12,0},{1,5},{5,9},{9,13},{13,1},{2,6},{6,10},{... | collective-permute-start | bytes 1105928 | tf_op jit(solution)/shard_map/ppermute | solution.py:776
  291.3 24.3 %collective-permute-start.26 = (bf16[4,2,120,1536]{3,2,0,1:T(8,128)(2,1)}, bf16[4,2,120,1536]{3,2,0,1:T(8,128)(2,1)}, u32[]{:S(2)}, u32[]{:S(2)}) collective-permute-start(bf16[4,2,120,1536]{3,2,0,1:T(8,128)(2,1)} %pad_maximum_fusion), channel_id=1, source_target_pairs={{0,1},{1,0},{2,3},{3,2},{4,5},{5,4},{6,7},{7,6},{8,9},{9,8},{10,11... | collective-permute-start | bytes 8847368 | tf_op jit(solution)/shard_map/ppermute | solution.py:787
  291.3 21.3 %collective-permute-start.27 = (bf16[1,1,120,1536]{3,2,1,0:T(8,128)(2,1)S(1)}, bf16[1,1,120,1536]{3,2,1,0:T(8,128)(2,1)}, u32[]{:S(2)}, u32[]{:S(2)}) collective-permute-start(bf16[1,1,120,1536]{3,2,1,0:T(8,128)(2,1)S(1)} %convert_bitcast_fusion.2), channel_id=1, source_target_pairs={{0,2},{1,3},{2,0},{3,1},{4,6},{5,7},{6,4},{7,5},{8,10},{9,11},{10,... | collective-permute-start | bytes 1105928 | tf_op jit(solution)/shard_map/ppermute | solution.py:787
  314.1 5.2 collective-permute-start.29
  342.9 37.1 %collective-permute-start.33 = (bf16[384,1536]{1,0:T(8,128)(2,1)}, bf16[384,1536]{1,0:T(8,128)(2,1)}, u32[]{:S(2)}, u32[]{:S(2)}) collective-permute-start(bf16[384,1536]{1,0:T(8,128)(2,1)} %get-tuple-element.232), channel_id=1, source_target_pairs={{0,16},{16,0},{1,17},{17,1},{2,18},{18,2},{3,19},{19,3},{4,20},{20... | collective-permute-start | bytes 3538952 | tf_op jit(solution)/shard_map/ppermute | solution.py:787
  346.8 35.8 %collective-permute-start.30 = (bf16[480,256]{1,0:T(8,128)(2,1)}, bf16[480,256]{1,0:T(8,128)(2,1)S(1)}, u32[]{:S(2)}, u32[]{:S(2)}) collective-permute-start(bf16[480,256]{1,0:T(8,128)(2,1)} %get-tuple-element.351), channel_id=1, source_target_pairs={{4,0},{8,4},{12,8},{5,1},{9,5},{13,9},{6,2},{10,6},{14,10},{7,3},{... | collective-permute-start | bytes 737288 | tf_op jit(solution)/shard_map/ppermute | solution.py:781
  348.1 35.2 %collective-permute-start.31 = (bf16[480,256]{1,0:T(8,128)(2,1)}, bf16[480,256]{1,0:T(8,128)(2,1)S(1)}, u32[]{:S(2)}, u32[]{:S(2)}) collective-permute-start(bf16[480,256]{1,0:T(8,128)(2,1)} %get-tuple-element.350), channel_id=1, source_target_pairs={{8,0},{12,4},{9,1},{13,5},{10,2},{14,6},{11,3},{15,7},{24,16},{28,... | collective-permute-start | bytes 737288 | tf_op jit(solution)/shard_map/ppermute | solution.py:781
  349.4 34.6 %collective-permute-start.32 = (bf16[480,256]{1,0:T(8,128)(2,1)}, bf16[480,256]{1,0:T(8,128)(2,1)S(1)}, u32[]{:S(2)}, u32[]{:S(2)}) collective-permute-start(bf16[480,256]{1,0:T(8,128)(2,1)} %get-tuple-element.349), channel_id=1, source_target_pairs={{12,0},{13,1},{14,2},{15,3},{28,16},{29,17},{30,18},{31,19}} | collective-permute-start | bytes 737288 | tf_op jit(solution)/shard_map/ppermute | solution.py:781
  350.8 29.2 %copy-start.69 = (bf16[384,1536]{1,0:T(8,128)(2,1)S(1)}, bf16[384,1536]{1,0:T(8,128)(2,1)}, u32[]{:S(2)}) copy-start(bf16[384,1536]{1,0:T(8,128)(2,1)} %get-tuple-element.230) | copy-start | bytes 3538948
  398.3 7.3 %collective-permute-start.35 = (bf16[1,2,120,1536]{3,2,1,0:T(8,128)(2,1)}, bf16[1,2,120,1536]{3,2,1,0:T(8,128)(2,1)}, u32[]{:S(2)}, u32[]{:S(2)}) collective-permute-start(bf16[1,2,120,1536]{3,2,1,0:T(8,128)(2,1)} %bitcast.63), channel_id=1, source_target_pairs={{0,1},{1,0},{2,3},{3,2},{4,5},{5,4},{6,7},{7,6},{8,9},{9,8},{10,11... | collective-permute-start | bytes 2211848 | tf_op jit(solution)/shard_map/ppermute | solution.py:787
  398.3 36.4 %all-to-all-start = ((bf16[4,96,1536]{2,1,0:T(8,128)(2,1)}), bf16[4,96,1536]{2,1,0:T(8,128)(2,1)S(1)}, u32[]{:S(2)}, u32[]{:S(2)}) async-start(bf16[4,96,1536]{2,1,0:T(8,128)(2,1)} %bitcast.190), calls=%async_computation | async-start | bytes 2359296 | tf_op jit(solution)/shard_map/all_to_all | solution.py:931
  408.6 19.2 %collective-permute-start.36 = (bf16[1,1,120,1536]{3,2,1,0:T(8,128)(2,1)}, bf16[1,1,120,1536]{3,2,1,0:T(8,128)(2,1)}, u32[]{:S(2)}, u32[]{:S(2)}) collective-permute-start(bf16[1,1,120,1536]{3,2,1,0:T(8,128)(2,1)} %constant_dynamic-slice_fusion), channel_id=1, source_target_pairs={{0,2},{1,3},{2,0},{3,1},{4,6},{5,7},{6,4},{7,5},{8,10},{9,11},{10,... | collective-permute-start | bytes 1105928 | tf_op jit(solution)/shard_map/ppermute | solution.py:787
  410.3 52.9 %collective-permute-start.28 = (bf16[4,1,120,1536]{3,2,0,1:T(8,128)(2,1)}, bf16[4,1,120,1536]{3,2,0,1:T(8,128)(2,1)}, u32[]{:S(2)}, u32[]{:S(2)}) collective-permute-start(bf16[4,1,120,1536]{3,2,0,1:T(8,128)(2,1)} %constant_dynamic-slice_fusion.1), channel_id=1, source_target_pairs={{0,2},{1,3},{2,0},{3,1},{4,6},{5,7},{6,4},{7,5},{8,10},{9,11},{10,... | collective-permute-start | bytes 4423688 | tf_op jit(solution)/shard_map/ppermute | solution.py:787
  435.9 49.1 %all-to-all-start.1 = ((bf16[4,96,1536]{2,1,0:T(8,128)(2,1)}), bf16[4,96,1536]{2,1,0:T(8,128)(2,1)}, u32[]{:S(2)}, u32[]{:S(2)}) async-start(bf16[4,96,1536]{2,1,0:T(8,128)(2,1)} %broadcast_in_dim.116), calls=%async_computation.1 | async-start | bytes 2359296 | tf_op jit(solution)/shard_map/all_to_all | solution.py:931
  440.3 145.9 %all-gather.11.cloned.1.call-start = ((), (), s32[]{:S(2)}) async-start(), calls=%async_computation.8 | async-start | bytes 7077888 | tf_op jit(solution)/shard_map/all_gather | solution.py:906
  440.8 18.5 %collective-permute-start.41 = (bf16[1,1,128,1536]{3,2,1,0:T(8,128)(2,1)S(1)}, bf16[1,1,128,1536]{3,2,1,0:T(8,128)(2,1)S(1)}, u32[]{:S(2)}, u32[]{:S(2)}) collective-permute-start(bf16[1,1,128,1536]{3,2,1,0:T(8,128)(2,1)S(1)} %get-tuple-element.358), channel_id=1, source_target_pairs={{0,2},{1,3},{2,0},{3,1},{4,6},{5,7},{6,4},{7,5},{8,10},{9,11},{10,... | collective-permute-start | bytes 1179656 | tf_op jit(solution)/shard_map/ppermute | solution.py:787
  442.7 19.7 %copy-start.32 = (bf16[128,1536]{1,0:T(8,128)(2,1)S(1)}, bf16[128,1536]{1,0:T(8,128)(2,1)}, u32[]{:S(2)}) copy-start(bf16[128,1536]{1,0:T(8,128)(2,1)} %copy-done.31) | copy-start | bytes 1179652
  442.7 19.7 %collective-permute-start.34 = (bf16[128,1536]{1,0:T(8,128)(2,1)S(1)}, bf16[128,1536]{1,0:T(8,128)(2,1)S(1)}, u32[]{:S(2)}, u32[]{:S(2)}) collective-permute-start(bf16[128,1536]{1,0:T(8,128)(2,1)S(1)} %copy-done.53), channel_id=1, source_target_pairs={{0,16},{16,0},{1,17},{17,1},{2,18},{18,2},{3,19},{19,3},{4,20},{20... | collective-permute-start | bytes 1179656 | tf_op jit(solution)/shard_map/ppermute | solution.py:787
  460.4 62.6 %collective-permute-start.43 = (bf16[1,2,128,1536]{3,2,1,0:T(8,128)(2,1)}, bf16[1,2,128,1536]{3,2,1,0:T(8,128)(2,1)}, u32[]{:S(2)}, u32[]{:S(2)}) collective-permute-start(bf16[1,2,128,1536]{3,2,1,0:T(8,128)(2,1)} %maximum_select_fusion.8), channel_id=1, source_target_pairs={{0,1},{1,0},{2,3},{3,2},{4,5},{5,4},{6,7},{7,6},{8,9},{9,8},{10,11... | collective-permute-start | bytes 2359304 | tf_op jit(solution)/shard_map/ppermute | solution.py:787
  485.0 33.1 %all-to-all-start.2 = ((bf16[4,32,1536]{2,1,0:T(8,128)(2,1)}), bf16[4,32,1536]{2,1,0:T(8,128)(2,1)S(1)}, u32[]{:S(2)}, u32[]{:S(2)}) async-start(bf16[4,32,1536]{2,1,0:T(8,128)(2,1)} %bitcast.75), calls=%async_computation.2 | async-start | bytes 786432 | tf_op jit(solution)/shard_map/all_to_all | solution.py:931
  492.8 33.7 %collective-permute-start.39 = (bf16[120,1536]{1,0:T(8,128)(2,1)}, bf16[120,1536]{1,0:T(8,128)(2,1)}, u32[]{:S(2)}, u32[]{:S(2)}) collective-permute-start(bf16[120,1536]{1,0:T(8,128)(2,1)} %get-tuple-element.339), channel_id=1, source_target_pairs={{0,4},{4,8},{8,12},{12,0},{1,5},{5,9},{9,13},{13,1},{2,6},{6,10},{... | collective-permute-start | bytes 1105928 | tf_op jit(solution)/shard_map/ppermute | solution.py:776
  494.8 33.4 %collective-permute-start.38 = (bf16[120,1536]{1,0:T(8,128)(2,1)}, bf16[120,1536]{1,0:T(8,128)(2,1)}, u32[]{:S(2)}, u32[]{:S(2)}) collective-permute-start(bf16[120,1536]{1,0:T(8,128)(2,1)} %get-tuple-element.340), channel_id=1, source_target_pairs={{0,8},{4,12},{8,0},{12,4},{1,9},{5,13},{9,1},{13,5},{2,10},{6,14},... | collective-permute-start | bytes 1105928 | tf_op jit(solution)/shard_map/ppermute | solution.py:776
  497.2 31.0 %collective-permute-start.37 = (bf16[120,1536]{1,0:T(8,128)(2,1)}, bf16[120,1536]{1,0:T(8,128)(2,1)}, u32[]{:S(2)}, u32[]{:S(2)}) collective-permute-start(bf16[120,1536]{1,0:T(8,128)(2,1)} %get-tuple-element.338), channel_id=1, source_target_pairs={{0,12},{4,0},{8,4},{12,8},{1,13},{5,1},{9,5},{13,9},{2,14},{6,2},{... | collective-permute-start | bytes 1105928 | tf_op jit(solution)/shard_map/ppermute | solution.py:776
  498.6 60.7 %collective-permute-start.42 = (bf16[384,1536]{1,0:T(8,128)(2,1)}, bf16[384,1536]{1,0:T(8,128)(2,1)}, u32[]{:S(2)}, u32[]{:S(2)}) collective-permute-start(bf16[384,1536]{1,0:T(8,128)(2,1)} %bitcast.74), channel_id=1, source_target_pairs={{0,16},{16,0},{1,17},{17,1},{2,18},{18,2},{3,19},{19,3},{4,20},{20... | collective-permute-start | bytes 3538952 | tf_op jit(solution)/shard_map/ppermute | solution.py:787
  518.8 22.5 %all-to-all-start.3 = ((bf16[4,32,1536]{2,1,0:T(8,128)(2,1)}), bf16[4,32,1536]{2,1,0:T(8,128)(2,1)}, u32[]{:S(2)}, u32[]{:S(2)}) async-start(bf16[4,32,1536]{2,1,0:T(8,128)(2,1)} %broadcast_in_dim.119), calls=%async_computation.3 | async-start | bytes 786432 | tf_op jit(solution)/shard_map/all_to_all | solution.py:931
  528.2 26.8 %collective-permute-start.44 = (f32[8,1536]{1,0:T(8,128)S(1)}, f32[8,1536]{1,0:T(8,128)S(1)}, u32[]{:S(2)}, u32[]{:S(2)}) collective-permute-start(f32[8,1536]{1,0:T(8,128)S(1)} %convert_reduce_fusion), channel_id=1, source_target_pairs={{0,16},{16,0},{1,17},{17,1},{2,18},{18,2},{3,19},{19,3},{4,20},{20... | collective-permute-start | bytes 147464 | tf_op jit(solution)/shard_map/ppermute | solution.py:787
  530.2 34.4 %collective-permute-start.40 = (bf16[1,1,120,1536]{3,2,1,0:T(8,128)(2,1)S(1)}, bf16[1,1,120,1536]{3,2,1,0:T(8,128)(2,1)S(1)}, u32[]{:S(2)}, u32[]{:S(2)}) collective-permute-start(bf16[1,1,120,1536]{3,2,1,0:T(8,128)(2,1)S(1)} %bitcast.196), channel_id=1, source_target_pairs={{0,2},{1,3},{2,0},{3,1},{4,6},{5,7},{6,4},{7,5},{8,10},{9,11},{10,... | collective-permute-start | bytes 1105928 | tf_op jit(solution)/shard_map/ppermute | solution.py:787
  541.3 29.7 %collective-permute-start.46 = (bf16[128,1536]{1,0:T(8,128)(2,1)}, bf16[128,1536]{1,0:T(8,128)(2,1)}, u32[]{:S(2)}, u32[]{:S(2)}) collective-permute-start(bf16[128,1536]{1,0:T(8,128)(2,1)} %bitcast.81), channel_id=1, source_target_pairs={{0,16},{16,0},{1,17},{17,1},{2,18},{18,2},{3,19},{19,3},{4,20},{20... | collective-permute-start | bytes 1179656 | tf_op jit(solution)/shard_map/ppermute | solution.py:787
  555.7 25.5 %all-to-all-start.4 = ((f32[4,8,1536]{2,1,0:T(8,128)}), f32[4,8,1536]{2,1,0:T(8,128)S(1)}, u32[]{:S(2)}, u32[]{:S(2)}) async-start(f32[4,8,1536]{2,1,0:T(8,128)} %broadcast_in_dim.120), calls=%async_computation.4 | async-start | bytes 393216 | tf_op jit(solution)/shard_map/all_to_all | solution.py:969
  565.6 18.0 %collective-permute-start.45 = (bf16[1,2,120,1536]{3,2,1,0:T(8,128)(2,1)}, bf16[1,2,120,1536]{3,2,1,0:T(8,128)(2,1)}, u32[]{:S(2)}, u32[]{:S(2)}) collective-permute-start(bf16[1,2,120,1536]{3,2,1,0:T(8,128)(2,1)} %maximum_select_fusion.14), channel_id=1, source_target_pairs={{0,1},{1,0},{2,3},{3,2},{4,5},{5,4},{6,7},{7,6},{8,9},{9,8},{10,11... | collective-permute-start | bytes 2211848 | tf_op jit(solution)/shard_map/ppermute | solution.py:787
  (64 other events, 261.4 us)
Sparse Core Ops, SparseCore 0:
  12.6 134.3 all-gather.4
Sparse Core Ops, SparseCore 1:
  179.6 73.4 all-gather.6
  384.8 100.0 all-gather.8
  486.3 97.2 all-gather.10
